TPU v7x, 512 devices: a whole 4x4x16 slice. The times are simulated.
512 devices in a mesh: span: 8 (over y, x_lo), ctx: 64 (over x_hi, z, core).
Axes of the slice: x: 4 (x_hi: 2, x_lo: 2; x = x_hi * 2 + x_lo), y: 4, z: 16, core: 2. Of those that a mesh axis runs over, the one named last changes fastest.
Arguments:
- queries: bfloat16 [8, 1024, 8192], P('span', 'ctx'), may hold values from -120 to 120
- keys: bfloat16 [8, 1024, 8192], P('span', 'ctx'), may hold values from -6 to 6
- values: bfloat16 [8, 1024, 8192], P('span', 'ctx'), may hold values from -6 to 6
- span_mask: int32 [8, 8], replicated, may hold values from 0 to 1, as said below
- span_counts: int32 [8], replicated, may hold values from 768 to 1024, as said below
Outputs:
- attended: bfloat16 [8, 1024, 8192], P('span', 'ctx')
Inputs may be any that keep to these rules, and one draw needn't show every extreme that they name: span_mask[i, i] is 1; span_mask[i, j] is 1 only for spans j that come before i in the denoising order, which is a permutation of the 8 spans. `span_counts`: some span is full.
All inputs are finite; a program needn't handle non-finite values.
Results may differ from a plain program's by a relative error of at most 0.02.
Values may be sent and summed in bfloat16 or wider, within the bound.
No kernel may reach another device: no remote copies, remote signals or barrier semaphores. Data moves between devices by JAX's collectives and lax.ppermute only.
A program may use at most 128 MiB of HBM per device.

v0:
```python
import jax
import jax.numpy as jnp
from jax import lax
from jax.sharding import PartitionSpec as P

HD = 128


def partial_attend(query, key_part, value_part, keep):
    scale = 1.0 / query.shape[-1] ** 0.5
    score = jnp.einsum("thd,shd->hts", query, key_part, preferred_element_type=jnp.float32) * scale
    score = jnp.where(keep[None, None, :], score, -1e30)
    top = jnp.max(score, axis=2)
    weight = jnp.where(keep[None, None, :], jnp.exp(score - top[:, :, None]), 0.0)
    total = jnp.sum(weight, axis=2)
    mixed = jnp.einsum(
        "hts,shd->htd", weight.astype(jnp.bfloat16), value_part, preferred_element_type=jnp.float32
    )
    return (top, total, mixed)


def per_device(queries, keys, values, span_mask, span_counts):
    tok_rows = queries.shape[1]
    width = queries.shape[2]
    n_ctx = lax.axis_size("ctx")
    heads_all = width // HD
    local_heads = heads_all // n_ctx
    n_span = span_mask.shape[0]
    shaped = (tok_rows, heads_all, HD)
    q_heads, k_heads, v_heads = (
        lax.all_to_all(queries.reshape(shaped), "ctx", split_axis=1, concat_axis=0, tiled=True),
        lax.all_to_all(keys.reshape(shaped), "ctx", split_axis=1, concat_axis=0, tiled=True),
        lax.all_to_all(values.reshape(shaped), "ctx", split_axis=1, concat_axis=0, tiled=True),
    )
    span_rows = q_heads.shape[0]
    group = lax.axis_index("span")
    span_ids = jnp.arange(n_span, dtype=jnp.int32)
    mask_row = lax.dynamic_index_in_dim(span_mask, group, 0, keepdims=False)
    run_top = jnp.full((local_heads, span_rows), -1e30, jnp.float32)
    key_part = lax.all_gather(k_heads, "span", axis=0, tiled=True)
    value_part = lax.all_gather(v_heads, "span", axis=0, tiled=True)
    rows = jnp.arange(key_part.shape[0], dtype=jnp.int32)
    onehot = (rows // span_rows)[:, None] == span_ids[None, :]
    allowed = jnp.sum(jnp.where(onehot, mask_row[None, :], 0), axis=1) > 0
    live = jnp.sum(jnp.where(onehot, span_counts[None, :], 0), axis=1)
    keep = allowed & (rows % span_rows < live)
    top, total, mixed = partial_attend(q_heads, key_part, value_part, keep)
    new_top = jnp.maximum(run_top, top)
    new_factor = jnp.exp(top - new_top)
    final_total = total * new_factor
    final_mixed = mixed * new_factor[:, :, None]
    result = final_mixed / final_total[:, :, None]
    result = result.astype(jnp.bfloat16).transpose(1, 0, 2)
    back = lax.all_to_all(result, "ctx", split_axis=0, concat_axis=1, tiled=True)
    return back.reshape(1, tok_rows, width)


def solution(mesh):
    in_specs = (P("span", "ctx", None), P("span", "ctx", None), P("span", "ctx", None), P(), P())
    out_specs = P("span", "ctx", None)
    return jax.shard_map(
        per_device, mesh=mesh, in_specs=in_specs, out_specs=out_specs, check_vma=False
    )
```

profile of v0, /device:TPU:1, one launch (start us, length us, event | category | flops | bytes accessed | tf_op | source)
XLA Modules:
  0.0 230.7 jit_solution(14853883479953814071)
XLA Ops:
  6.5 0.0 copy-start
  6.5 0.0 all-gather.3.cloned.1.call-start
  6.5 1.0 copy.33
  7.5 0.2 copy.27
  7.7 43.3 %all_to_all.66 = bf16[16,64,128]{2,0,1:T(8,128)(2,1)} all-to-all(bf16[16,64,128]{2,0,1:T(8,128)(2,1)S(1)} %copy.27), channel_id=1, replica_groups=mesh['span'=8,'ctx'=64] {'ctx'}, dimensions={1} | all-to-all | bytes 524288 | tf_op jit(solution)/shard_map/all_to_all | solution.py:32
  51.0 0.0 all-gather.3.cloned.1.call-update
  51.0 1.0 copy.34
  52.0 0.9 copy.28
  52.9 4.2 %all-to-all-start.2 = ((bf16[16,64,128]{2,0,1:T(8,128)(2,1)}), bf16[16,64,128]{2,0,1:T(8,128)(2,1)S(1)}, u32[]{:S(2)}, u32[]{:S(2)}) async-start(bf16[16,64,128]{2,0,1:T(8,128)(2,1)} %copy.28), calls=%async_computation.2 | async-start | bytes 524288 | tf_op jit(solution)/shard_map/all_to_all | solution.py:33
  57.1 1.0 copy.32
  58.1 0.9 copy.26
  59.0 21.7 %all-to-all-done.2 = bf16[16,64,128]{2,0,1:T(8,128)(2,1)S(1)} async-done(((bf16[16,64,128]{2,0,1:T(8,128)(2,1)}), bf16[16,64,128]{2,0,1:T(8,128)(2,1)S(1)}, u32[]{:S(2)}, u32[]{:S(2)}) %all-to-all-start.2) | async-done | bytes 262176 | tf_op jit(solution)/shard_map/all_to_all | solution.py:33
  80.7 0.0 copy-start.1
  80.7 4.2 %all-to-all-start = ((bf16[16,64,128]{2,0,1:T(8,128)(2,1)}), bf16[16,64,128]{2,0,1:T(8,128)(2,1)S(1)}, u32[]{:S(2)}, u32[]{:S(2)}) async-start(bf16[16,64,128]{2,0,1:T(8,128)(2,1)} %copy.26), calls=%async_computation | async-start | bytes 524288 | tf_op jit(solution)/shard_map/all_to_all | solution.py:31
  84.9 0.2 all-gather.5.cloned.1.call-start
  85.1 0.0 copy-done
  85.1 0.9 select_reduce_fusion.1
  86.1 0.0 copy-done.1
  86.1 0.0 all-gather.5.cloned.1.call-update
  86.1 22.4 %all-to-all-done = bf16[16,64,128]{2,0,1:T(8,128)(2,1)S(1)} async-done(((bf16[16,64,128]{2,0,1:T(8,128)(2,1)}), bf16[16,64,128]{2,0,1:T(8,128)(2,1)S(1)}, u32[]{:S(2)}, u32[]{:S(2)}) %all-to-all-start) | async-done | bytes 262176 | tf_op jit(solution)/shard_map/all_to_all | solution.py:31
  108.5 0.0 all-gather.3.cloned.1.call-done
  108.5 15.0 %fusion = (f32[1024]{0:T(1024)S(1)}, f32[1024,8192]{1,0:T(8,128)}) fusion(pred[8192]{0:T(1024)(128)(4,1)S(1)} %fusion.36, bf16[1024,128]{1,0:T(8,128)(2,1)S(1)} %bitcast.52, bf16[8192,1,128]{2,0,1:T(8,128)(2,1)} %all-gather.3.cloned.1.call-done), kind=kOutput, calls=%fused_computation.2 | convolution fusion | flops 2172648448 | bytes 35926016 | tf_op jit(solution)/shard_map/thd,shd->hts/dot_general | solution.py:11
  123.5 15.9 %fusion.1 = f32[1024]{0:T(1024)S(1)} fusion(f32[1024,8192]{1,0:T(8,128)} %get-tuple-element.10, f32[1024]{0:T(1024)S(1)} %get-tuple-element.9, pred[8192]{0:T(1024)(128)(4,1)S(1)} %fusion.36), kind=kLoop, calls=%fused_computation.3 | loop fusion | flops 41942016 | bytes 33570816 | tf_op jit(solution)/shard_map/reduce_sum | solution.py:15
  139.5 27.9 %all-gather.5.cloned.1.call-done = bf16[8192,1,128]{2,0,1:T(8,128)(2,1)} async-done(((bf16[1024,1,128]{2,0,1:T(8,128)(2,1)}), bf16[8192,1,128]{2,0,1:T(8,128)(2,1)}) %all-gather.5.cloned.1.call-update) | async-done | bytes 2097168 | tf_op jit(solution)/shard_map/all_gather | solution.py:41
  167.4 14.6 %fusion.23 = bf16[1024,1,128]{2,0,1:T(8,128)(2,1)S(1)} fusion(bf16[8192,1,128]{2,0,1:T(8,128)(2,1)} %all-gather.5.cloned.1.call-done, f32[1024,8192]{1,0:T(8,128)} %get-tuple-element.10, f32[1024]{0:T(1024)S(1)} %get-tuple-element.9, pred[8192]{0:T(1024)(128)(4,1)S(1)} %fusion.36, f32[1024]{0:T(1024)S(1)} %get-tuple-element.8, f32[1024]{0:T(1024)S(1)} %get-tuple-element.7), kind=kOutput, calls=%fused_computation.12 | convolution fusion | flops 2189819904 | bytes 35934208 | tf_op jit(solution)/shard_map/hts,shd->htd/dot_general | solution.py:16
  182.0 0.5 broadcast.78
  182.5 0.8 reduce.4
  183.3 0.1 reshape.106
  183.4 39.3 %all_to_all.67 = bf16[64,2,1024]{2,1,0:T(2,128)(2,1)S(1)} all-to-all(bf16[64,2,1024]{2,1,0:T(2,128)(2,1)S(1)} %reshape.106), channel_id=1, replica_groups=mesh['span'=8,'ctx'=64] {'ctx'}, dimensions={0} | all-to-all | bytes 524288 | tf_op jit(solution)/shard_map/all_to_all | solution.py:54
  222.7 0.2 reshape.107
  222.9 0.1 copy.30
  223.0 0.8 reshape.105
  (5 shorter events, 0.1 us)
Async XLA Ops:
  6.5 78.6 %copy-start = (s32[8,8]{1,0:T(8,128)S(1)}, s32[8,8]{1,0:T(8,128)}, u32[]{:S(2)}) copy-start(s32[8,8]{1,0:T(8,128)} %param.8) | copy-start | bytes 772
  6.5 102.0 %all-gather.3.cloned.1.call-start = ((), (), s32[]{:S(2)}) async-start(), calls=%async_computation.4 | async-start | bytes 2359296 | tf_op jit(solution)/shard_map/all_gather | solution.py:40
  52.9 27.8 %all-to-all-start.2 = ((bf16[16,64,128]{2,0,1:T(8,128)(2,1)}), bf16[16,64,128]{2,0,1:T(8,128)(2,1)S(1)}, u32[]{:S(2)}, u32[]{:S(2)}) async-start(bf16[16,64,128]{2,0,1:T(8,128)(2,1)} %copy.28), calls=%async_computation.2 | async-start | bytes 524288 | tf_op jit(solution)/shard_map/all_to_all | solution.py:33
  80.7 5.4 %copy-start.1 = (bf16[16,64,128]{2,0,1:T(8,128)(2,1)}, bf16[16,64,128]{2,0,1:T(8,128)(2,1)S(1)}, u32[]{:S(2)}) copy-start(bf16[16,64,128]{2,0,1:T(8,128)(2,1)S(1)} %all-to-all-done.2) | copy-start | bytes 786436
  80.7 27.8 %all-to-all-start = ((bf16[16,64,128]{2,0,1:T(8,128)(2,1)}), bf16[16,64,128]{2,0,1:T(8,128)(2,1)S(1)}, u32[]{:S(2)}, u32[]{:S(2)}) async-start(bf16[16,64,128]{2,0,1:T(8,128)(2,1)} %copy.26), calls=%async_computation | async-start | bytes 524288 | tf_op jit(solution)/shard_map/all_to_all | solution.py:31
  84.9 82.5 %all-gather.5.cloned.1.call-start = ((), (), s32[]{:S(2)}) async-start(), calls=%async_computation.5 | async-start | bytes 2359296 | tf_op jit(solution)/shard_map/all_gather | solution.py:41
Sparse Core Ops, SparseCore 0:
  51.1 54.6 all-gather.2
  107.9 59.3 all-gather.4
where the time goes:
time: 231 us
  blocking collectives  82.6 us (36%)
  waiting for transfers between devices  72 us (31%)
  matrix products  29.6 us (13%)
  other arithmetic  17.6 us (8%)
  between operations  13.5 us (6%)
  starting transfers between devices  8.6 us (4%)
  local copies, waits for them, and re-layouts  6.65 us (3%)
    all_to_all x1, blocking collectives, per_device(): lax.all_to_all(keys.reshape(shaped), 'ctx', split_axis=1, concat_axis=0,...  43.3 us
    all_to_all x1, blocking collectives, per_device(): lax.all_to_all(result, 'ctx', split_axis=0, concat_axis=1, tiled=True)  39.3 us
    all_gather x1, waiting for transfers between devices, per_device(): value_part = lax.all_gather(v_heads, 'span', axis=0, tiled=True)  27.9 us
    all_to_all x1, waiting for transfers between devices, per_device(): lax.all_to_all(queries.reshape(shaped), 'ctx', split_axis=1, concat_axis=...  22.4 us
    all_to_all x1, waiting for transfers between devices, per_device(): lax.all_to_all(values.reshape(shaped), 'ctx', split_axis=1, concat_axis=0...  21.7 us
    reduce_sum x1, other arithmetic, partial_attend(): total = jnp.sum(weight, axis=2)  15.9 us
    dot_general x1, matrix products, partial_attend(): jnp.einsum('thd,shd->hts', query, key_part, preferred_element_type=jnp.fl...  15 us
    dot_general x1, matrix products, partial_attend(): jnp.einsum('hts,shd->htd', weight.astype(jnp.bfloat16), value_part, prefe...  14.6 us
  transfers between devices with their start and end apart: 4, of which 3 were waited for; matrix products, arithmetic and copies ran while one was open for 15% of the time, Pallas kernels for 0%

commit v1 on v0

v1 whole, which is shorter than its diff:
```python
import jax
import jax.numpy as jnp
from jax import lax
from jax.experimental import pallas as pl
from jax.experimental.pallas import tpu as pltpu
from jax.sharding import Mesh, PartitionSpec as P

HD = 128
LOW = -1e30


def attend_kernel(place, mask, counts, q_ref, *rest):
    pieces = rest[:8]
    out_ref, k_buf, v_buf, acc_ref, top_ref, total_ref, sems = rest[8:]
    x_lo, x_hi, core = place[0], place[1], place[2]
    x = x_hi * 2 + x_lo
    copies = []
    for d in range(4):
        from_hi = ((x + d) % 4) // 2
        for e in range(2):
            piece = pieces[2 * d + e]
            from_core = (core + e) % 2
            copies.append(
                pltpu.make_async_copy(
                    piece.at[:, 0], k_buf.at[d % 2, from_hi, from_core], sems.at[2 * d + e, 0]
                )
            )
            copies.append(
                pltpu.make_async_copy(
                    piece.at[:, 1], v_buf.at[d % 2, from_hi, from_core], sems.at[2 * d + e, 1]
                )
            )
    for copy in copies:
        copy.start()
    for copy in copies:
        copy.wait()

    scale = 1.0 / HD**0.5
    lane = lax.broadcasted_iota(jnp.int32, (1, 512), 1)
    slot = 512 + (lane % 256) // 16 * 32 + lane // 256 * 16 + lane % 16

    def query_block(iy, _):
        top_ref[...] = jnp.full_like(top_ref, LOW)
        total_ref[...] = jnp.zeros_like(total_ref)
        acc_ref[...] = jnp.zeros_like(acc_ref)
        span = iy * 2 + x_lo

        def key_block(block, _):
            rel, jy = block // 4, block % 4
            key_span = jy * 2 + (x_lo + rel) % 2

            @pl.when(mask[span, key_span] == 1)
            def _():
                q = q_ref[pl.ds(iy * 16, 16)].reshape(256, HD)
                k = k_buf[rel, :, :, pl.ds(jy * 16, 16)].reshape(1024, HD)
                v = v_buf[rel, :, :, pl.ds(jy * 16, 16)].reshape(1024, HD)
                s = lax.dot_general(
                    q, k, (((1,), (1,)), ((), ())), preferred_element_type=jnp.float32
                )
                upper = jnp.where(slot < counts[key_span], s[:, 512:], LOW)
                s = jnp.concatenate([s[:, :512], upper], axis=1)
                old = top_ref[...]
                top = jnp.maximum(old, jnp.max(s, axis=1, keepdims=True))
                factor = jnp.exp((old - top) * scale)
                weight = jnp.exp((s - top[:, :1]) * scale)
                total_ref[...] = total_ref[...] * factor + jnp.sum(weight, axis=1, keepdims=True)
                top_ref[...] = top
                acc_ref[...] = acc_ref[...] * factor + jnp.dot(
                    weight.astype(jnp.bfloat16), v, preferred_element_type=jnp.float32
                )

            return 0

        lax.fori_loop(0, 8, key_block, 0)
        result = acc_ref[...] / total_ref[...]
        out_ref[pl.ds(iy * 16, 16)] = result.astype(jnp.bfloat16).reshape(16, 16, HD)
        return 0

    lax.fori_loop(0, 4, query_block, 0)


def attend(place, mask, counts, q, pieces):
    smem = pl.BlockSpec(memory_space=pltpu.SMEM)
    vmem = pl.BlockSpec(memory_space=pltpu.VMEM)
    return pl.pallas_call(
        attend_kernel,
        out_shape=jax.ShapeDtypeStruct(q.shape, jnp.bfloat16),
        in_specs=[smem, smem, smem, vmem] + [pl.BlockSpec(memory_space=pl.ANY)] * 8,
        out_specs=vmem,
        scratch_shapes=[
            pltpu.VMEM((2, 2, 2, 64, 16, HD), jnp.bfloat16),
            pltpu.VMEM((2, 2, 2, 64, 16, HD), jnp.bfloat16),
            pltpu.VMEM((256, HD), jnp.float32),
            pltpu.VMEM((256, HD), jnp.float32),
            pltpu.VMEM((256, HD), jnp.float32),
            pltpu.SemaphoreType.DMA((8, 2)),
        ],
        compiler_params=pltpu.CompilerParams(vmem_limit_bytes=40 * 1024 * 1024),
        cost_estimate=pl.CostEstimate(
            flops=4 * 1024 * 8192 * HD, bytes_accessed=5 << 20, transcendentals=1024 * 8192
        ),
    )(place, mask, counts, q, *pieces)


def ring(step):
    def index(x):
        return (x % 2) * 2 + x // 2

    return [(index(x), index((x + step) % 4)) for x in range(4)]


def per_device(queries, keys, values, span_mask, span_counts):
    tok_rows, width = queries.shape[1], queries.shape[2]
    heads = width // HD

    def by_head(array):
        return array.reshape(tok_rows, heads, HD).transpose(1, 0, 2)

    def exchange(array):
        return lax.all_to_all(array, ("y", "z"), split_axis=0, concat_axis=0, tiled=True)

    kv = exchange(jnp.stack([by_head(keys), by_head(values)], axis=1))
    q_in, kv = lax.optimization_barrier((by_head(queries), kv))
    q = exchange(q_in)

    x_axes = ("x_lo", "x_hi")
    swap = [(0, 1), (1, 0)]
    own = [
        kv,
        lax.ppermute(kv, x_axes, ring(-1)),
        lax.ppermute(kv, x_axes, ring(2)),
        lax.ppermute(kv, x_axes, ring(1)),
    ]
    pieces = []
    for piece in own:
        pieces += [piece, lax.ppermute(piece, "core", swap)]
    place = jnp.stack([lax.axis_index("x_lo"), lax.axis_index("x_hi"), lax.axis_index("core")])
    out = attend(place.astype(jnp.int32), span_mask, span_counts, q, pieces)
    back = exchange(out)
    return back.transpose(1, 0, 2).reshape(1, tok_rows, width)


def solution(mesh):
    fine = Mesh(mesh.devices.reshape(4, 2, 2, 16, 2), ("y", "x_lo", "x_hi", "z", "core"))
    split = P(("y", "x_lo"), ("x_hi", "z", "core"), None)
    return jax.shard_map(
        per_device,
        mesh=fine,
        in_specs=(split, split, split, P(), P()),
        out_specs=split,
        check_vma=False,
    )
```

time: 231 us -> 136 us (0.59)
  the two profiles are of different devices: /device:TPU:1 before, /device:TPU:2 now
where the time goes in v1:
time: 136 us
  starting transfers between devices  44.4 us (33%)
  waiting for transfers between devices  42 us (31%)
  blocking collectives  27.2 us (20%)
  Pallas kernels  17.8 us (13%)
  local copies, waits for them, and re-layouts  3.25 us (2%)
    all_to_all x2, waiting for transfers between devices, exchange(): lax.all_to_all(array, ('y', 'z'), split_axis=0, concat_axis=0, tiled=True)  36.9 us
    all_to_all x1, blocking collectives, exchange(): lax.all_to_all(array, ('y', 'z'), split_axis=0, concat_axis=0, tiled=True)  27.2 us
    all_to_all x2, starting transfers between devices, exchange(): lax.all_to_all(array, ('y', 'z'), split_axis=0, concat_axis=0, tiled=True)  25.7 us
    pallas_call x1, Pallas kernels, attend(): pl.pallas_call(attend_kernel, out_shape=jax.ShapeDtypeStruct(q.shape, jnp...  17.8 us
    ppermute x4, starting transfers between devices, per_device(): pieces += [piece, lax.ppermute(piece, 'core', swap)]  8.16 us
    ppermute x1, waiting for transfers between devices, per_device(): lax.ppermute(kv, x_axes, ring(-1))  5.16 us
    ppermute x1, starting transfers between devices, per_device(): lax.ppermute(kv, x_axes, ring(-1))  4.06 us
    ppermute x1, starting transfers between devices, per_device(): lax.ppermute(kv, x_axes, ring(1))  3.39 us
  transfers between devices with their start and end apart: 9, of which 3 were waited for; matrix products, arithmetic and copies ran while one was open for 1% of the time, Pallas kernels for 0%

profile of v1, /device:TPU:2, one launch (start us, length us, event | category | flops | bytes accessed | tf_op | source)
XLA Modules:
  0.0 135.8 jit_solution(14132844814635692663)
XLA Ops:
  0.0 1.0 copy.11
  1.0 0.0 copy-done.2
  1.1 0.3 copy_bitcast_fusion
  1.5 0.8 pad_maximum_fusion
  2.3 18.9 %all-to-all-start = ((bf16[64,2,16,128]{3,2,1,0:T(8,128)(2,1)}), bf16[64,2,16,128]{3,2,1,0:T(8,128)(2,1)S(1)}, u32[]{:S(2)}, u32[]{:S(2)}) async-start(bf16[64,2,16,128]{3,2,1,0:T(8,128)(2,1)} %pad_maximum_fusion), calls=%async_computation | async-start | bytes 1048576 | tf_op jit(solution)/shard_map/all_to_all | solution.py:120
  21.2 0.0 copy-done.3
  21.2 0.9 copy.16
  22.1 30.8 %all-to-all-done.rest_0_ = bf16[64,2,16,128]{3,2,1,0:T(8,128)(2,1)S(1)} async-done(((bf16[64,2,16,128]{3,2,1,0:T(8,128)(2,1)}), bf16[64,2,16,128]{3,2,1,0:T(8,128)(2,1)S(1)}, u32[]{:S(2)}, u32[]{:S(2)}) %all-to-all-start) | async-done | bytes 524320 | tf_op jit(solution)/shard_map/all_to_all | solution.py:120
  52.9 3.4 %collective-permute-start.5 = (bf16[64,2,16,128]{3,2,1,0:T(8,128)(2,1)S(1)}, bf16[64,2,16,128]{3,2,1,0:T(8,128)(2,1)S(1)}, u32[]{:S(2)}, u32[]{:S(2)}) collective-permute-start(bf16[64,2,16,128]{3,2,1,0:T(8,128)(2,1)S(1)} %all-to-all-done.rest_0_), channel_id=1, source_target_pairs={{0,64},{64,32},{32,96},{96,0},{1,65},{65,33},{33,97},{97,1},{2,66}... | collective-permute-start | bytes 1572872 | tf_op jit(solution)/shard_map/ppermute | solution.py:132
  56.3 3.0 %collective-permute-start.3 = (bf16[64,2,16,128]{3,2,1,0:T(8,128)(2,1)S(1)}, bf16[64,2,16,128]{3,2,1,0:T(8,128)(2,1)S(1)}, u32[]{:S(2)}, u32[]{:S(2)}) collective-permute-start(bf16[64,2,16,128]{3,2,1,0:T(8,128)(2,1)S(1)} %all-to-all-done.rest_0_), channel_id=1, source_target_pairs={{0,32},{64,96},{32,0},{96,64},{1,33},{65,97},{33,1},{97,65},{2,34}... | collective-permute-start | bytes 1572872 | tf_op jit(solution)/shard_map/ppermute | solution.py:131
  59.3 4.1 %collective-permute-start.1 = (bf16[64,2,16,128]{3,2,1,0:T(8,128)(2,1)S(1)}, bf16[64,2,16,128]{3,2,1,0:T(8,128)(2,1)S(1)}, u32[]{:S(2)}, u32[]{:S(2)}) collective-permute-start(bf16[64,2,16,128]{3,2,1,0:T(8,128)(2,1)S(1)} %all-to-all-done.rest_0_), channel_id=1, source_target_pairs={{0,96},{64,0},{32,64},{96,32},{1,97},{65,1},{33,65},{97,33},{2,98}... | collective-permute-start | bytes 1572872 | tf_op jit(solution)/shard_map/ppermute | solution.py:130
  63.4 6.9 %all-to-all-start.1 = ((bf16[64,16,128]{2,1,0:T(8,128)(2,1)}), bf16[64,16,128]{2,1,0:T(8,128)(2,1)S(1)}, u32[]{:S(2)}, u32[]{:S(2)}) async-start(bf16[64,16,128]{2,1,0:T(8,128)(2,1)} %bitcast.23), calls=%async_computation.1 | async-start | bytes 524288 | tf_op jit(solution)/shard_map/all_to_all | solution.py:120
  70.2 1.9 %collective-permute-start = (bf16[64,2,16,128]{3,2,1,0:T(8,128)(2,1)S(1)}, bf16[64,2,16,128]{3,2,1,0:T(8,128)(2,1)S(1)}, u32[]{:S(2)}, u32[]{:S(2)}) collective-permute-start(bf16[64,2,16,128]{3,2,1,0:T(8,128)(2,1)S(1)} %all-to-all-done.rest_0_), channel_id=1, source_target_pairs={{0,1},{1,0},{2,3},{3,2},{4,5},{5,4},{6,7},{7,6},{8,9},{9,8},{10,11... | collective-permute-start | bytes 1572872 | tf_op jit(solution)/shard_map/ppermute | solution.py:136
  72.2 0.0 collective-permute-done.5.rest_6_
  72.2 2.4 %collective-permute-start.6 = (bf16[64,2,16,128]{3,2,1,0:T(8,128)(2,1)S(1)}, bf16[64,2,16,128]{3,2,1,0:T(8,128)(2,1)S(1)}, u32[]{:S(2)}, u32[]{:S(2)}) collective-permute-start(bf16[64,2,16,128]{3,2,1,0:T(8,128)(2,1)S(1)} %collective-permute-done.5.rest_6_), channel_id=1, source_target_pairs={{0,1},{1,0},{2,3},{3,2},{4,5},{5,4},{6,7},{7,6},{8,9},{9,8},{10,11... | collective-permute-start | bytes 1572872 | tf_op jit(solution)/shard_map/ppermute | solution.py:136
  74.6 0.0 collective-permute-done.3.rest_4_
  74.6 1.9 %collective-permute-start.4 = (bf16[64,2,16,128]{3,2,1,0:T(8,128)(2,1)S(1)}, bf16[64,2,16,128]{3,2,1,0:T(8,128)(2,1)}, u32[]{:S(2)}, u32[]{:S(2)}) collective-permute-start(bf16[64,2,16,128]{3,2,1,0:T(8,128)(2,1)S(1)} %collective-permute-done.3.rest_4_), channel_id=1, source_target_pairs={{0,1},{1,0},{2,3},{3,2},{4,5},{5,4},{6,7},{7,6},{8,9},{9,8},{10,11... | collective-permute-start | bytes 1572872 | tf_op jit(solution)/shard_map/ppermute | solution.py:136
  76.5 5.2 %collective-permute-done.1.rest_2_ = bf16[64,2,16,128]{3,2,1,0:T(8,128)(2,1)S(1)} collective-permute-done((bf16[64,2,16,128]{3,2,1,0:T(8,128)(2,1)S(1)}, bf16[64,2,16,128]{3,2,1,0:T(8,128)(2,1)S(1)}, u32[]{:S(2)}, u32[]{:S(2)}) %collective-permute-start.1) | collective-permute-done | bytes 524320 | tf_op jit(solution)/shard_map/ppermute | solution.py:130
  81.7 1.9 %collective-permute-start.2 = (bf16[64,2,16,128]{3,2,1,0:T(8,128)(2,1)S(1)}, bf16[64,2,16,128]{3,2,1,0:T(8,128)(2,1)}, u32[]{:S(2)}, u32[]{:S(2)}) collective-permute-start(bf16[64,2,16,128]{3,2,1,0:T(8,128)(2,1)S(1)} %collective-permute-done.1.rest_2_), channel_id=1, source_target_pairs={{0,1},{1,0},{2,3},{3,2},{4,5},{5,4},{6,7},{7,6},{8,9},{9,8},{10,11... | collective-permute-start | bytes 1572872 | tf_op jit(solution)/shard_map/ppermute | solution.py:136
  83.6 0.0 copy-start
  83.6 0.0 copy-start.1
  83.7 0.1 pad_add_fusion.place
  83.7 0.0 collective-permute-done.rest_1_
  83.7 6.1 %all-to-all-done.1.q_ref = bf16[64,16,128]{2,1,0:T(8,128)(2,1)S(1)} async-done(((bf16[64,16,128]{2,1,0:T(8,128)(2,1)}), bf16[64,16,128]{2,1,0:T(8,128)(2,1)S(1)}, u32[]{:S(2)}, u32[]{:S(2)}) %all-to-all-start.1) | async-done | bytes 262176 | tf_op jit(solution)/shard_map/all_to_all | solution.py:120
  89.8 0.0 collective-permute-done.6.rest_7_
  89.8 0.0 collective-permute-done.4.rest_5_
  89.8 0.0 collective-permute-done.2.rest_3_
  89.8 0.0 copy-done
  89.9 17.8 %shard_map.55 = bf16[64,16,128]{2,1,0:T(8,128)(2,1)S(1)} custom-call(s32[3]{0:T(128)S(1)} %pad_add_fusion.place, s32[8,8]{1,0:T(8,128)S(1)} %copy-done, s32[8]{0:T(128)S(1)} %copy-done.1, bf16[64,16,128]{2,1,0:T(8,128)(2,1)S(1)} %all-to-all-done.1.q_ref, bf16[64,2,16,128]{3,2,1,0:T(8,128)(2,1)S(1)} %all-to-all-done.rest_0_, ...), custom_call_target="tpu_custom_call" | custom-call | flops 4294967296 | bytes 5242880 | tf_op jit(solution)/shard_map/pallas_call | solution.py:85
  107.7 27.2 %all_to_all.15 = bf16[64,16,128]{2,1,0:T(8,128)(2,1)S(1)} all-to-all(bf16[64,16,128]{2,1,0:T(8,128)(2,1)S(1)} %shard_map.55), channel_id=1, replica_groups=mesh['y'=4,'x_lo'=2,'x_hi'=2,'z'=16,'core'=2] {'y','z'}, dimensions={0} | all-to-all | bytes 524288 | tf_op jit(solution)/shard_map/all_to_all | solution.py:120
  134.9 0.1 copy.9
  134.9 0.8 reshape.15
  (5 shorter events, 0.1 us)
Async XLA Ops:
  0.0 1.0 copy-start.2
  2.3 18.9 %copy-start.3 = (bf16[1,16,8192]{2,1,0:T(8,128)(2,1)S(1)}, bf16[1,16,8192]{2,1,0:T(8,128)(2,1)}, u32[]{:S(2)}) copy-start(bf16[1,16,8192]{2,1,0:T(8,128)(2,1)} %param.5) | copy-start | bytes 786436
  2.3 50.6 %all-to-all-start = ((bf16[64,2,16,128]{3,2,1,0:T(8,128)(2,1)}), bf16[64,2,16,128]{3,2,1,0:T(8,128)(2,1)S(1)}, u32[]{:S(2)}, u32[]{:S(2)}) async-start(bf16[64,2,16,128]{3,2,1,0:T(8,128)(2,1)} %pad_maximum_fusion), calls=%async_computation | async-start | bytes 1048576 | tf_op jit(solution)/shard_map/all_to_all | solution.py:120
  52.9 19.3 %collective-permute-start.5 = (bf16[64,2,16,128]{3,2,1,0:T(8,128)(2,1)S(1)}, bf16[64,2,16,128]{3,2,1,0:T(8,128)(2,1)S(1)}, u32[]{:S(2)}, u32[]{:S(2)}) collective-permute-start(bf16[64,2,16,128]{3,2,1,0:T(8,128)(2,1)S(1)} %all-to-all-done.rest_0_), channel_id=1, source_target_pairs={{0,64},{64,32},{32,96},{96,0},{1,65},{65,33},{33,97},{97,1},{2,66}... | collective-permute-start | bytes 1572872 | tf_op jit(solution)/shard_map/ppermute | solution.py:132
  56.3 18.3 %collective-permute-start.3 = (bf16[64,2,16,128]{3,2,1,0:T(8,128)(2,1)S(1)}, bf16[64,2,16,128]{3,2,1,0:T(8,128)(2,1)S(1)}, u32[]{:S(2)}, u32[]{:S(2)}) collective-permute-start(bf16[64,2,16,128]{3,2,1,0:T(8,128)(2,1)S(1)} %all-to-all-done.rest_0_), channel_id=1, source_target_pairs={{0,32},{64,96},{32,0},{96,64},{1,33},{65,97},{33,1},{97,65},{2,34}... | collective-permute-start | bytes 1572872 | tf_op jit(solution)/shard_map/ppermute | solution.py:131
  59.3 22.4 %collective-permute-start.1 = (bf16[64,2,16,128]{3,2,1,0:T(8,128)(2,1)S(1)}, bf16[64,2,16,128]{3,2,1,0:T(8,128)(2,1)S(1)}, u32[]{:S(2)}, u32[]{:S(2)}) collective-permute-start(bf16[64,2,16,128]{3,2,1,0:T(8,128)(2,1)S(1)} %all-to-all-done.rest_0_), channel_id=1, source_target_pairs={{0,96},{64,0},{32,64},{96,32},{1,97},{65,1},{33,65},{97,33},{2,98}... | collective-permute-start | bytes 1572872 | tf_op jit(solution)/shard_map/ppermute | solution.py:130
  63.4 26.5 %all-to-all-start.1 = ((bf16[64,16,128]{2,1,0:T(8,128)(2,1)}), bf16[64,16,128]{2,1,0:T(8,128)(2,1)S(1)}, u32[]{:S(2)}, u32[]{:S(2)}) async-start(bf16[64,16,128]{2,1,0:T(8,128)(2,1)} %bitcast.23), calls=%async_computation.1 | async-start | bytes 524288 | tf_op jit(solution)/shard_map/all_to_all | solution.py:120
  70.2 13.5 %collective-permute-start = (bf16[64,2,16,128]{3,2,1,0:T(8,128)(2,1)S(1)}, bf16[64,2,16,128]{3,2,1,0:T(8,128)(2,1)S(1)}, u32[]{:S(2)}, u32[]{:S(2)}) collective-permute-start(bf16[64,2,16,128]{3,2,1,0:T(8,128)(2,1)S(1)} %all-to-all-done.rest_0_), channel_id=1, source_target_pairs={{0,1},{1,0},{2,3},{3,2},{4,5},{5,4},{6,7},{7,6},{8,9},{9,8},{10,11... | collective-permute-start | bytes 1572872 | tf_op jit(solution)/shard_map/ppermute | solution.py:136
  72.2 17.7 %collective-permute-start.6 = (bf16[64,2,16,128]{3,2,1,0:T(8,128)(2,1)S(1)}, bf16[64,2,16,128]{3,2,1,0:T(8,128)(2,1)S(1)}, u32[]{:S(2)}, u32[]{:S(2)}) collective-permute-start(bf16[64,2,16,128]{3,2,1,0:T(8,128)(2,1)S(1)} %collective-permute-done.5.rest_6_), channel_id=1, source_target_pairs={{0,1},{1,0},{2,3},{3,2},{4,5},{5,4},{6,7},{7,6},{8,9},{9,8},{10,11... | collective-permute-start | bytes 1572872 | tf_op jit(solution)/shard_map/ppermute | solution.py:136
  74.6 15.2 %collective-permute-start.4 = (bf16[64,2,16,128]{3,2,1,0:T(8,128)(2,1)S(1)}, bf16[64,2,16,128]{3,2,1,0:T(8,128)(2,1)}, u32[]{:S(2)}, u32[]{:S(2)}) collective-permute-start(bf16[64,2,16,128]{3,2,1,0:T(8,128)(2,1)S(1)} %collective-permute-done.3.rest_4_), channel_id=1, source_target_pairs={{0,1},{1,0},{2,3},{3,2},{4,5},{5,4},{6,7},{7,6},{8,9},{9,8},{10,11... | collective-permute-start | bytes 1572872 | tf_op jit(solution)/shard_map/ppermute | solution.py:136
  81.7 8.1 %collective-permute-start.2 = (bf16[64,2,16,128]{3,2,1,0:T(8,128)(2,1)S(1)}, bf16[64,2,16,128]{3,2,1,0:T(8,128)(2,1)}, u32[]{:S(2)}, u32[]{:S(2)}) collective-permute-start(bf16[64,2,16,128]{3,2,1,0:T(8,128)(2,1)S(1)} %collective-permute-done.1.rest_2_), channel_id=1, source_target_pairs={{0,1},{1,0},{2,3},{3,2},{4,5},{5,4},{6,7},{7,6},{8,9},{9,8},{10,11... | collective-permute-start | bytes 1572872 | tf_op jit(solution)/shard_map/ppermute | solution.py:136
  83.6 6.2 %copy-start = (s32[8,8]{1,0:T(8,128)S(1)}, s32[8,8]{1,0:T(8,128)}, u32[]{:S(2)}) copy-start(s32[8,8]{1,0:T(8,128)} %mask.1) | copy-start | bytes 772
  83.6 6.2 %copy-start.1 = (s32[8]{0:T(128)S(1)}, s32[8]{0:T(128)}, u32[]{:S(2)}) copy-start(s32[8]{0:T(128)} %counts.1) | copy-start | bytes 100

commit v2 on v1

v2 whole, which is shorter than its diff:
```python
import jax
import jax.numpy as jnp
from jax import lax
from jax.experimental import pallas as pl
from jax.experimental.pallas import tpu as pltpu
from jax.sharding import Mesh, PartitionSpec as P

HD = 128
LOW = -1e30
LOG2E = 1.4426950408889634


def attend_kernel(place, mask, counts, q_ref, *rest):
    pieces = rest[:8]
    out_ref, k_buf, v_buf, s_a, s_b, m_a, m_b, acc_ref, top_ref, total_ref, todo, sems = rest[8:]
    scores, row_tops = (s_a, s_b), (m_a, m_b)
    x_lo, x_hi, core = place[0], place[1], place[2]
    x = x_hi * 2 + x_lo
    copies = {}
    for d in (0, 2, 1, 3):
        for part, buf in enumerate((k_buf, v_buf)):
            for e in range(2):
                copies[d, e, part] = pltpu.make_async_copy(
                    pieces[2 * d + e].at[:, part],
                    buf.at[d % 2, ((x + d) % 4) // 2, (core + e) % 2],
                    sems.at[2 * d + e, part],
                )
    for side in range(2):
        for part in range(2):
            for d in (side, side + 2):
                for e in range(2):
                    copies[d, e, part].start()

    def wait(side, part):
        for d in (side, side + 2):
            for e in range(2):
                copies[d, e, part].wait()

    def list_block(i, n):
        side, iy, jy = i // 16, i // 4 % 4, i % 4
        todo[n] = i
        return n + mask[iy * 2 + x_lo, jy * 2 + (x_lo + side) % 2]

    near = lax.fori_loop(0, 16, list_block, 0)
    count = lax.fori_loop(16, 32, list_block, near)

    acc_ref[...] = jnp.zeros_like(acc_ref)
    top_ref[...] = jnp.full_like(top_ref, LOW)
    total_ref[...] = jnp.zeros_like(total_ref)
    scale = LOG2E / HD**0.5
    lane = lax.broadcasted_iota(jnp.int32, (1, 128), 1)
    late = 768 + lane // 16 * 32 + lane % 16

    def score(n, slot):
        i = todo[n]
        side, iy, jy = i // 16, i // 4 % 4, i % 4
        live = counts[jy * 2 + (x_lo + side) % 2]
        q = q_ref[pl.ds(iy * 16, 16)].reshape(256, HD)
        top = None
        for hi in range(2):
            for c in range(2):
                k = k_buf[side, hi, c, pl.ds(jy * 16, 16)].reshape(256, HD)
                s = lax.dot_general(q, k, (((1,), (1,)), ((), ())), preferred_element_type=jnp.float32)
                a, b = s[:, :128], s[:, 128:]
                if hi == 1:
                    b = jnp.where(late + c * 16 < live, b, LOW)
                at = (hi * 2 + c) * 256
                scores[slot][:, at : at + 128] = a
                scores[slot][:, at + 128 : at + 256] = b
                both = jnp.maximum(a, b)
                top = both if top is None else jnp.maximum(top, both)
        row_tops[slot][...] = jnp.broadcast_to(jnp.max(top, axis=1, keepdims=True), (256, 128))

    def half(n, slot):
        i = todo[n]
        side, iy, jy = i // 16, i // 4 % 4, i % 4

        @pl.when(n + 1 == near)
        def _():
            wait(1, 0)
            wait(1, 1)
        old = top_ref[iy]
        top = jnp.maximum(old, row_tops[slot][...])
        shift = top * scale
        factor = jnp.exp2(old * scale - shift)
        total = total_ref[iy] * factor
        acc = acc_ref[iy] * factor
        score(jnp.minimum(n + 1, count - 1), 1 - slot)
        for g in range(4):
            at = g * 256
            wa = jnp.exp2(scores[slot][:, at : at + 128] * scale - shift)
            wb = jnp.exp2(scores[slot][:, at + 128 : at + 256] * scale - shift)
            total = total + wa + wb
            w = jnp.concatenate([wa.astype(jnp.bfloat16), wb.astype(jnp.bfloat16)], axis=1)
            v = v_buf[side, g // 2, g % 2, pl.ds(jy * 16, 16)].reshape(256, HD)
            acc = acc + jnp.dot(w, v, preferred_element_type=jnp.float32)
        total_ref[iy] = total
        top_ref[iy] = top
        acc_ref[iy] = acc

    wait(0, 0)
    score(0, 0)
    wait(0, 1)

    def pair(n, _):
        half(2 * n, 0)

        @pl.when(2 * n + 1 < count)
        def _():
            half(2 * n + 1, 1)

        return 0

    lax.fori_loop(0, (count + 1) // 2, pair, 0)
    for iy in range(4):
        total = jnp.sum(total_ref[iy], axis=1, keepdims=True)
        out_ref[iy * 16 : (iy + 1) * 16] = (acc_ref[iy] / total).astype(jnp.bfloat16).reshape(16, 16, HD)

def attend(place, mask, counts, q, pieces):
    smem = pl.BlockSpec(memory_space=pltpu.SMEM)
    vmem = pl.BlockSpec(memory_space=pltpu.VMEM)
    return pl.pallas_call(
        attend_kernel,
        out_shape=jax.ShapeDtypeStruct(q.shape, jnp.bfloat16),
        in_specs=[smem, smem, smem, vmem] + [pl.BlockSpec(memory_space=pl.ANY)] * 8,
        out_specs=vmem,
        scratch_shapes=[
            pltpu.VMEM((2, 2, 2, 64, 16, HD), jnp.bfloat16),
            pltpu.VMEM((2, 2, 2, 64, 16, HD), jnp.bfloat16),
            pltpu.VMEM((256, 1024), jnp.float32),
            pltpu.VMEM((256, 1024), jnp.float32),
            pltpu.VMEM((256, HD), jnp.float32),
            pltpu.VMEM((256, HD), jnp.float32),
            pltpu.VMEM((4, 256, HD), jnp.float32),
            pltpu.VMEM((4, 256, HD), jnp.float32),
            pltpu.VMEM((4, 256, HD), jnp.float32),
            pltpu.SMEM((33,), jnp.int32),
            pltpu.SemaphoreType.DMA((8, 2)),
        ],
        compiler_params=pltpu.CompilerParams(vmem_limit_bytes=40 * 1024 * 1024),
        cost_estimate=pl.CostEstimate(
            flops=4 * 1024 * 8192 * HD, bytes_accessed=5 << 20, transcendentals=1024 * 8192
        ),
    )(place, mask, counts, q, *pieces)


def ring(step):
    def index(x):
        return (x % 2) * 2 + x // 2

    return [(index(x), index((x + step) % 4)) for x in range(4)]


def per_device(queries, keys, values, span_mask, span_counts):
    tok_rows, width = queries.shape[1], queries.shape[2]
    heads = width // HD

    def by_head(array):
        return array.reshape(tok_rows, heads, HD).transpose(1, 0, 2)

    def exchange(array):
        return lax.all_to_all(array, ("y", "z"), split_axis=0, concat_axis=0, tiled=True)

    kv = exchange(jnp.stack([by_head(keys), by_head(values)], axis=1))
    q_in, kv = lax.optimization_barrier((by_head(queries), kv))
    q = exchange(q_in)

    def gather(kv):
        x_axes = ("x_lo", "x_hi")
        swap = [(0, 1), (1, 0)]
        ahead, back, far = [lax.ppermute(kv, x_axes, ring(step)) for step in (-1, 1, 2)]
        other = [lax.ppermute(piece, "core", swap) for piece in (kv, ahead, back, far)]
        return [other[0], ahead, other[1], far, other[3], back, other[2]]

    def gather_own(kv):
        x_axes = ("x_lo", "x_hi")
        swap = [(0, 1), (1, 0)]
        far = lax.ppermute(kv, x_axes, ring(2))
        other = lax.ppermute(kv, "core", swap)
        return [other, kv, other, far, lax.ppermute(far, "core", swap), kv, other]

    crossing = jnp.sum(span_mask) > span_mask.shape[0]
    pieces = [kv] + lax.cond(crossing, gather, gather_own, kv)
    place = jnp.stack([lax.axis_index("x_lo"), lax.axis_index("x_hi"), lax.axis_index("core")])
    out = attend(place.astype(jnp.int32), span_mask, span_counts, q, pieces)
    back = exchange(out)
    return back.transpose(1, 0, 2).reshape(1, tok_rows, width)


def solution(mesh):
    fine = Mesh(mesh.devices.reshape(4, 2, 2, 16, 2), ("y", "x_lo", "x_hi", "z", "core"))
    split = P(("y", "x_lo"), ("x_hi", "z", "core"), None)
    return jax.shard_map(
        per_device,
        mesh=fine,
        in_specs=(split, split, split, P(), P()),
        out_specs=split,
        check_vma=False,
    )
```

time: 136 us -> 146 us (1.074)
  the two profiles are of different devices: /device:TPU:2 before, /device:TPU:6 now
where the time goes in v2:
time: 146 us; the launch traced here: 145 us
  waiting for transfers between devices  48.6 us (33%)
  starting transfers between devices  43.8 us (30%)
  blocking collectives  35.9 us (25%)
  Pallas kernels  11 us (8%)
  local copies, waits for them, and re-layouts  3.9 us (3%)
  other arithmetic  1.52 us (1%)
    all_to_all x1, blocking collectives, exchange(): lax.all_to_all(array, ('y', 'z'), split_axis=0, concat_axis=0, tiled=True)  35.9 us
    all_to_all x2, waiting for transfers between devices, exchange(): lax.all_to_all(array, ('y', 'z'), split_axis=0, concat_axis=0, tiled=True)  30.8 us
    all_to_all x2, starting transfers between devices, exchange(): lax.all_to_all(array, ('y', 'z'), split_axis=0, concat_axis=0, tiled=True)  25.9 us
    ppermute x3, waiting for transfers between devices, gather(): lax.ppermute(kv, x_axes, ring(step))  15.6 us
    pallas_call x1, Pallas kernels, attend(): pl.pallas_call(attend_kernel, out_shape=jax.ShapeDtypeStruct(q.shape, jnp...  11 us
    ppermute x3, starting transfers between devices, gather(): lax.ppermute(kv, x_axes, ring(step))  9.75 us
    ppermute x4, starting transfers between devices, gather(): lax.ppermute(piece, 'core', swap)  8.16 us
  transfers between devices with their start and end apart: 9, of which 3 were waited for; matrix products, arithmetic and copies ran while one was open for 1% of the time, Pallas kernels for 0%

profile of v2, /device:TPU:6, one launch (start us, length us, event | category | flops | bytes accessed | tf_op | source)
XLA Modules:
  0.0 145.4 jit_solution(12772048201195452844)
XLA Ops:
  0.0 1.0 copy.11
  1.0 0.0 copy-done.2
  1.1 0.3 copy_bitcast_fusion
  1.5 0.8 pad_maximum_fusion
  2.3 18.9 %all-to-all-start = ((bf16[64,2,16,128]{3,2,1,0:T(8,128)(2,1)}), bf16[64,2,16,128]{3,2,1,0:T(8,128)(2,1)S(1)}, u32[]{:S(2)}, u32[]{:S(2)}) async-start(bf16[64,2,16,128]{3,2,1,0:T(8,128)(2,1)} %pad_maximum_fusion), calls=%async_computation | async-start | bytes 1048576 | tf_op jit(solution)/shard_map/all_to_all | solution.py:162
  21.2 0.9 copy.16
  22.1 30.8 %all-to-all-done.rest_0_ = bf16[64,2,16,128]{3,2,1,0:T(8,128)(2,1)S(1)} async-done(((bf16[64,2,16,128]{3,2,1,0:T(8,128)(2,1)}), bf16[64,2,16,128]{3,2,1,0:T(8,128)(2,1)S(1)}, u32[]{:S(2)}, u32[]{:S(2)}) %all-to-all-start) | async-done | bytes 524320 | tf_op jit(solution)/shard_map/all_to_all | solution.py:162
  52.9 7.0 %all-to-all-start.1 = ((bf16[64,16,128]{2,1,0:T(8,128)(2,1)}), bf16[64,16,128]{2,1,0:T(8,128)(2,1)S(1)}, u32[]{:S(2)}, u32[]{:S(2)}) async-start(bf16[64,16,128]{2,1,0:T(8,128)(2,1)} %bitcast.23), calls=%async_computation.1 | async-start | bytes 524288 | tf_op jit(solution)/shard_map/all_to_all | solution.py:162
  59.9 0.0 copy-done
  59.9 0.6 reduce_sum.9
  61.0 0.1 pad_add_fusion.place
  61.1 35.8 %conditional.1 = (bf16[64,2,16,128]{3,2,1,0:T(8,128)(2,1)}, bf16[64,2,16,128]{3,2,1,0:T(8,128)(2,1)}, bf16[64,2,16,128]{3,2,1,0:T(8,128)(2,1)}, bf16[64,2,16,128...) conditional(s32[]{:T(128)} %convert_element_type.3, ...), branch_computations={%region_1.0_spmd, %region_2.0_spmd} | conditional | bytes 14680400 | solution.py:183
  61.1 2.7 %collective-permute-start.4 = (bf16[64,2,16,128]{3,2,1,0:T(8,128)(2,1)S(1)}, bf16[64,2,16,128]{3,2,1,0:T(8,128)(2,1)}, u32[]{:S(2)}, u32[]{:S(2)}) collective-permute-start(bf16[64,2,16,128]{3,2,1,0:T(8,128)(2,1)S(1)} %param.1), channel_id=1, source_target_pairs={{0,96},{64,0},{32,64},{96,32},{1,97},{65,1},{33,65},{97,33},{2,98}... | collective-permute-start | bytes 1572872 | tf_op jit(solution)/shard_map/cond/branch_1_fun/ppermute | solution.py:171
  63.9 3.0 %collective-permute-start.6 = (bf16[64,2,16,128]{3,2,1,0:T(8,128)(2,1)S(1)}, bf16[64,2,16,128]{3,2,1,0:T(8,128)(2,1)}, u32[]{:S(2)}, u32[]{:S(2)}) collective-permute-start(bf16[64,2,16,128]{3,2,1,0:T(8,128)(2,1)S(1)} %param.1), channel_id=1, source_target_pairs={{0,32},{64,96},{32,0},{96,64},{1,33},{65,97},{33,1},{97,65},{2,34}... | collective-permute-start | bytes 1572872 | tf_op jit(solution)/shard_map/cond/branch_1_fun/ppermute | solution.py:171
  66.9 4.0 %collective-permute-start.8 = (bf16[64,2,16,128]{3,2,1,0:T(8,128)(2,1)S(1)}, bf16[64,2,16,128]{3,2,1,0:T(8,128)(2,1)}, u32[]{:S(2)}, u32[]{:S(2)}) collective-permute-start(bf16[64,2,16,128]{3,2,1,0:T(8,128)(2,1)S(1)} %param.1), channel_id=1, source_target_pairs={{0,64},{64,32},{32,96},{96,0},{1,65},{65,33},{33,97},{97,1},{2,66}... | collective-permute-start | bytes 1572872 | tf_op jit(solution)/shard_map/cond/branch_1_fun/ppermute | solution.py:171
  70.9 1.9 %collective-permute-start.3 = (bf16[64,2,16,128]{3,2,1,0:T(8,128)(2,1)S(1)}, bf16[64,2,16,128]{3,2,1,0:T(8,128)(2,1)}, u32[]{:S(2)}, u32[]{:S(2)}) collective-permute-start(bf16[64,2,16,128]{3,2,1,0:T(8,128)(2,1)S(1)} %param.1), channel_id=1, source_target_pairs={{0,1},{1,0},{2,3},{3,2},{4,5},{5,4},{6,7},{7,6},{8,9},{9,8},{10,11... | collective-permute-start | bytes 1572872 | tf_op jit(solution)/shard_map/cond/branch_1_fun/ppermute | solution.py:172
  72.8 15.6 %collective-permute-done.4 = bf16[64,2,16,128]{3,2,1,0:T(8,128)(2,1)} collective-permute-done((bf16[64,2,16,128]{3,2,1,0:T(8,128)(2,1)S(1)}, bf16[64,2,16,128]{3,2,1,0:T(8,128)(2,1)}, u32[]{:S(2)}, u32[]{:S(2)}) %collective-permute-start.4) | collective-permute-done | bytes 524320 | tf_op jit(solution)/shard_map/cond/branch_1_fun/ppermute | solution.py:171
  88.4 1.9 %collective-permute-start.5 = (bf16[64,2,16,128]{3,2,1,0:T(8,128)(2,1)}, bf16[64,2,16,128]{3,2,1,0:T(8,128)(2,1)}, u32[]{:S(2)}, u32[]{:S(2)}) collective-permute-start(bf16[64,2,16,128]{3,2,1,0:T(8,128)(2,1)} %collective-permute-done.4), channel_id=1, source_target_pairs={{0,1},{1,0},{2,3},{3,2},{4,5},{5,4},{6,7},{7,6},{8,9},{9,8},{10,11... | collective-permute-start | bytes 1572872 | tf_op jit(solution)/shard_map/cond/branch_1_fun/ppermute | solution.py:172
  90.3 0.0 collective-permute-done.6
  90.4 2.4 %collective-permute-start.7 = (bf16[64,2,16,128]{3,2,1,0:T(8,128)(2,1)}, bf16[64,2,16,128]{3,2,1,0:T(8,128)(2,1)}, u32[]{:S(2)}, u32[]{:S(2)}) collective-permute-start(bf16[64,2,16,128]{3,2,1,0:T(8,128)(2,1)} %collective-permute-done.6), channel_id=1, source_target_pairs={{0,1},{1,0},{2,3},{3,2},{4,5},{5,4},{6,7},{7,6},{8,9},{9,8},{10,11... | collective-permute-start | bytes 1572872 | tf_op jit(solution)/shard_map/cond/branch_1_fun/ppermute | solution.py:172
  92.8 0.0 collective-permute-done.8
  92.8 1.9 %collective-permute-start.9 = (bf16[64,2,16,128]{3,2,1,0:T(8,128)(2,1)}, bf16[64,2,16,128]{3,2,1,0:T(8,128)(2,1)}, u32[]{:S(2)}, u32[]{:S(2)}) collective-permute-start(bf16[64,2,16,128]{3,2,1,0:T(8,128)(2,1)} %collective-permute-done.8), channel_id=1, source_target_pairs={{0,1},{1,0},{2,3},{3,2},{4,5},{5,4},{6,7},{7,6},{8,9},{9,8},{10,11... | collective-permute-start | bytes 1572872 | tf_op jit(solution)/shard_map/cond/branch_1_fun/ppermute | solution.py:172
  94.7 0.0 collective-permute-done.3
  94.7 0.0 collective-permute-done.5
  94.7 0.0 collective-permute-done.7
  94.7 2.2 %collective-permute-done.9 = bf16[64,2,16,128]{3,2,1,0:T(8,128)(2,1)} collective-permute-done((bf16[64,2,16,128]{3,2,1,0:T(8,128)(2,1)}, bf16[64,2,16,128]{3,2,1,0:T(8,128)(2,1)}, u32[]{:S(2)}, u32[]{:S(2)}) %collective-permute-start.9) | collective-permute-done | bytes 524320 | tf_op jit(solution)/shard_map/cond/branch_1_fun/ppermute | solution.py:172
  96.9 0.0 all-to-all-done.1.q_ref
  96.9 0.7 copy-done.1
  97.6 11.0 %shard_map.55 = bf16[64,16,128]{2,1,0:T(8,128)(2,1)S(1)} custom-call(s32[3]{0:T(128)S(1)} %pad_add_fusion.place, s32[8,8]{1,0:T(8,128)S(1)} %copy-done, s32[8]{0:T(128)S(1)} %copy-done.1, bf16[64,16,128]{2,1,0:T(8,128)(2,1)S(1)} %all-to-all-done.1.q_ref, bf16[64,2,16,128]{3,2,1,0:T(8,128)(2,1)S(1)} %all-to-all-done.rest_0_, ...), custom_call_target="tpu_custom_call" | custom-call | flops 4294967296 | bytes 5242880 | tf_op jit(solution)/shard_map/pallas_call | solution.py:122
  108.6 35.9 %all_to_all.15 = bf16[64,16,128]{2,1,0:T(8,128)(2,1)S(1)} all-to-all(bf16[64,16,128]{2,1,0:T(8,128)(2,1)S(1)} %shard_map.55), channel_id=1, replica_groups=mesh['y'=4,'x_lo'=2,'x_hi'=2,'z'=16,'core'=2] {'y','z'}, dimensions={0} | all-to-all | bytes 524288 | tf_op jit(solution)/shard_map/all_to_all | solution.py:162
  144.5 0.1 copy.9
  144.6 0.8 reshape.15
  (7 shorter events, 0.1 us)
Async XLA Ops:
  0.0 1.0 copy-start.2
  2.3 18.9 %copy-start.3 = (bf16[1,16,8192]{2,1,0:T(8,128)(2,1)S(1)}, bf16[1,16,8192]{2,1,0:T(8,128)(2,1)}, u32[]{:S(2)}) copy-start(bf16[1,16,8192]{2,1,0:T(8,128)(2,1)} %param.7) | copy-start | bytes 786436
  2.3 50.6 %all-to-all-start = ((bf16[64,2,16,128]{3,2,1,0:T(8,128)(2,1)}), bf16[64,2,16,128]{3,2,1,0:T(8,128)(2,1)S(1)}, u32[]{:S(2)}, u32[]{:S(2)}) async-start(bf16[64,2,16,128]{3,2,1,0:T(8,128)(2,1)} %pad_maximum_fusion), calls=%async_computation | async-start | bytes 1048576 | tf_op jit(solution)/shard_map/all_to_all | solution.py:162
  52.9 7.0 %copy-start = (s32[8,8]{1,0:T(8,128)S(1)}, s32[8,8]{1,0:T(8,128)}, u32[]{:S(2)}) copy-start(s32[8,8]{1,0:T(8,128)} %mask.1) | copy-start | bytes 772
  52.9 44.1 %all-to-all-start.1 = ((bf16[64,16,128]{2,1,0:T(8,128)(2,1)}), bf16[64,16,128]{2,1,0:T(8,128)(2,1)S(1)}, u32[]{:S(2)}, u32[]{:S(2)}) async-start(bf16[64,16,128]{2,1,0:T(8,128)(2,1)} %bitcast.23), calls=%async_computation.1 | async-start | bytes 524288 | tf_op jit(solution)/shard_map/all_to_all | solution.py:162
  61.1 27.3 %collective-permute-start.4 = (bf16[64,2,16,128]{3,2,1,0:T(8,128)(2,1)S(1)}, bf16[64,2,16,128]{3,2,1,0:T(8,128)(2,1)}, u32[]{:S(2)}, u32[]{:S(2)}) collective-permute-start(bf16[64,2,16,128]{3,2,1,0:T(8,128)(2,1)S(1)} %param.1), channel_id=1, source_target_pairs={{0,96},{64,0},{32,64},{96,32},{1,97},{65,1},{33,65},{97,33},{2,98}... | collective-permute-start | bytes 1572872 | tf_op jit(solution)/shard_map/cond/branch_1_fun/ppermute | solution.py:171
  63.9 26.5 %collective-permute-start.6 = (bf16[64,2,16,128]{3,2,1,0:T(8,128)(2,1)S(1)}, bf16[64,2,16,128]{3,2,1,0:T(8,128)(2,1)}, u32[]{:S(2)}, u32[]{:S(2)}) collective-permute-start(bf16[64,2,16,128]{3,2,1,0:T(8,128)(2,1)S(1)} %param.1), channel_id=1, source_target_pairs={{0,32},{64,96},{32,0},{96,64},{1,33},{65,97},{33,1},{97,65},{2,34}... | collective-permute-start | bytes 1572872 | tf_op jit(solution)/shard_map/cond/branch_1_fun/ppermute | solution.py:171
  66.9 25.9 %collective-permute-start.8 = (bf16[64,2,16,128]{3,2,1,0:T(8,128)(2,1)S(1)}, bf16[64,2,16,128]{3,2,1,0:T(8,128)(2,1)}, u32[]{:S(2)}, u32[]{:S(2)}) collective-permute-start(bf16[64,2,16,128]{3,2,1,0:T(8,128)(2,1)S(1)} %param.1), channel_id=1, source_target_pairs={{0,64},{64,32},{32,96},{96,0},{1,65},{65,33},{33,97},{97,1},{2,66}... | collective-permute-start | bytes 1572872 | tf_op jit(solution)/shard_map/cond/branch_1_fun/ppermute | solution.py:171
  70.9 23.8 %collective-permute-start.3 = (bf16[64,2,16,128]{3,2,1,0:T(8,128)(2,1)S(1)}, bf16[64,2,16,128]{3,2,1,0:T(8,128)(2,1)}, u32[]{:S(2)}, u32[]{:S(2)}) collective-permute-start(bf16[64,2,16,128]{3,2,1,0:T(8,128)(2,1)S(1)} %param.1), channel_id=1, source_target_pairs={{0,1},{1,0},{2,3},{3,2},{4,5},{5,4},{6,7},{7,6},{8,9},{9,8},{10,11... | collective-permute-start | bytes 1572872 | tf_op jit(solution)/shard_map/cond/branch_1_fun/ppermute | solution.py:172
  88.4 6.3 %collective-permute-start.5 = (bf16[64,2,16,128]{3,2,1,0:T(8,128)(2,1)}, bf16[64,2,16,128]{3,2,1,0:T(8,128)(2,1)}, u32[]{:S(2)}, u32[]{:S(2)}) collective-permute-start(bf16[64,2,16,128]{3,2,1,0:T(8,128)(2,1)} %collective-permute-done.4), channel_id=1, source_target_pairs={{0,1},{1,0},{2,3},{3,2},{4,5},{5,4},{6,7},{7,6},{8,9},{9,8},{10,11... | collective-permute-start | bytes 1572872 | tf_op jit(solution)/shard_map/cond/branch_1_fun/ppermute | solution.py:172
  90.4 4.4 %collective-permute-start.7 = (bf16[64,2,16,128]{3,2,1,0:T(8,128)(2,1)}, bf16[64,2,16,128]{3,2,1,0:T(8,128)(2,1)}, u32[]{:S(2)}, u32[]{:S(2)}) collective-permute-start(bf16[64,2,16,128]{3,2,1,0:T(8,128)(2,1)} %collective-permute-done.6), channel_id=1, source_target_pairs={{0,1},{1,0},{2,3},{3,2},{4,5},{5,4},{6,7},{7,6},{8,9},{9,8},{10,11... | collective-permute-start | bytes 1572872 | tf_op jit(solution)/shard_map/cond/branch_1_fun/ppermute | solution.py:172
  92.8 4.1 %collective-permute-start.9 = (bf16[64,2,16,128]{3,2,1,0:T(8,128)(2,1)}, bf16[64,2,16,128]{3,2,1,0:T(8,128)(2,1)}, u32[]{:S(2)}, u32[]{:S(2)}) collective-permute-start(bf16[64,2,16,128]{3,2,1,0:T(8,128)(2,1)} %collective-permute-done.8), channel_id=1, source_target_pairs={{0,1},{1,0},{2,3},{3,2},{4,5},{5,4},{6,7},{7,6},{8,9},{9,8},{10,11... | collective-permute-start | bytes 1572872 | tf_op jit(solution)/shard_map/cond/branch_1_fun/ppermute | solution.py:172
  96.9 0.7 copy-start.1

commit v3 on v2

--- a/solution.py
+++ b/solution.py
@@ -11,17 +11,17 @@
 
 
 def attend_kernel(place, mask, counts, q_ref, *rest):
-    pieces = rest[:8]
-    out_ref, k_buf, v_buf, s_a, s_b, m_a, m_b, acc_ref, top_ref, total_ref, todo, sems = rest[8:]
+    near, far = rest[:6], rest[6:10]
+    out_ref, k_buf, v_buf, s_a, s_b, m_a, m_b, acc_ref, top_ref, total_ref, todo, sems = rest[10:]
     scores, row_tops = (s_a, s_b), (m_a, m_b)
     x_lo, x_hi, core = place[0], place[1], place[2]
     x = x_hi * 2 + x_lo
     copies = {}
-    for d in (0, 2, 1, 3):
+    for d in range(4):
         for part, buf in enumerate((k_buf, v_buf)):
             for e in range(2):
                 copies[d, e, part] = pltpu.make_async_copy(
-                    pieces[2 * d + e].at[:, part],
+                    far[2 * part + e] if d == 2 else near[2 * (d - d // 3) + e].at[:, part],
                     buf.at[d % 2, ((x + d) % 4) // 2, (core + e) % 2],
                     sems.at[2 * d + e, part],
                 )
@@ -41,8 +41,8 @@
         todo[n] = i
         return n + mask[iy * 2 + x_lo, jy * 2 + (x_lo + side) % 2]
 
-    near = lax.fori_loop(0, 16, list_block, 0)
-    count = lax.fori_loop(16, 32, list_block, near)
+    first = lax.fori_loop(0, 16, list_block, 0)
+    count = lax.fori_loop(16, 32, list_block, first)
 
     acc_ref[...] = jnp.zeros_like(acc_ref)
     top_ref[...] = jnp.full_like(top_ref, LOW)
@@ -75,7 +75,7 @@
         i = todo[n]
         side, iy, jy = i // 16, i // 4 % 4, i % 4
 
-        @pl.when(n + 1 == near)
+        @pl.when(n + 1 == first)
         def _():
             wait(1, 0)
             wait(1, 1)
@@ -116,13 +116,13 @@
         total = jnp.sum(total_ref[iy], axis=1, keepdims=True)
         out_ref[iy * 16 : (iy + 1) * 16] = (acc_ref[iy] / total).astype(jnp.bfloat16).reshape(16, 16, HD)
 
-def attend(place, mask, counts, q, pieces):
+def attend(place, mask, counts, q, near, far):
     smem = pl.BlockSpec(memory_space=pltpu.SMEM)
     vmem = pl.BlockSpec(memory_space=pltpu.VMEM)
     return pl.pallas_call(
         attend_kernel,
         out_shape=jax.ShapeDtypeStruct(q.shape, jnp.bfloat16),
-        in_specs=[smem, smem, smem, vmem] + [pl.BlockSpec(memory_space=pl.ANY)] * 8,
+        in_specs=[smem, smem, smem, vmem] + [pl.BlockSpec(memory_space=pl.ANY)] * 10,
         out_specs=vmem,
         scratch_shapes=[
             pltpu.VMEM((2, 2, 2, 64, 16, HD), jnp.bfloat16),
@@ -141,7 +141,24 @@
         cost_estimate=pl.CostEstimate(
             flops=4 * 1024 * 8192 * HD, bytes_accessed=5 << 20, transcendentals=1024 * 8192
         ),
-    )(place, mask, counts, q, *pieces)
+    )(place, mask, counts, q, *near, *far)
+
+
+def pack_kernel(k_ref, v_ref, out_ref):
+    for head in range(out_ref.shape[0]):
+        at = head * HD
+        out_ref[head, 0] = k_ref[:, at : at + HD]
+        out_ref[head, 1] = v_ref[:, at : at + HD]
+
+
+def pack(keys, values):
+    rows, width = keys.shape
+    return pl.pallas_call(
+        pack_kernel,
+        out_shape=jax.ShapeDtypeStruct((width // HD, 2, rows, HD), keys.dtype),
+        in_specs=[pl.BlockSpec(memory_space=pltpu.VMEM)] * 2,
+        out_specs=pl.BlockSpec(memory_space=pltpu.VMEM),
+    )(keys, values)
 
 
 def ring(step):
@@ -161,28 +178,23 @@
     def exchange(array):
         return lax.all_to_all(array, ("y", "z"), split_axis=0, concat_axis=0, tiled=True)
 
-    kv = exchange(jnp.stack([by_head(keys), by_head(values)], axis=1))
+    kv = exchange(pack(keys[0], values[0]))
     q_in, kv = lax.optimization_barrier((by_head(queries), kv))
     q = exchange(q_in)
 
-    def gather(kv):
-        x_axes = ("x_lo", "x_hi")
-        swap = [(0, 1), (1, 0)]
-        ahead, back, far = [lax.ppermute(kv, x_axes, ring(step)) for step in (-1, 1, 2)]
-        other = [lax.ppermute(piece, "core", swap) for piece in (kv, ahead, back, far)]
-        return [other[0], ahead, other[1], far, other[3], back, other[2]]
-
-    def gather_own(kv):
-        x_axes = ("x_lo", "x_hi")
-        swap = [(0, 1), (1, 0)]
-        far = lax.ppermute(kv, x_axes, ring(2))
-        other = lax.ppermute(kv, "core", swap)
-        return [other, kv, other, far, lax.ppermute(far, "core", swap), kv, other]
-
-    crossing = jnp.sum(span_mask) > span_mask.shape[0]
-    pieces = [kv] + lax.cond(crossing, gather, gather_own, kv)
+    x_axes = ("x_lo", "x_hi")
+
+    def with_other_core(piece):
+        return [piece, lax.ppermute(piece, "core", [(0, 1), (1, 0)])]
+
+    near = with_other_core(kv)
+    for step in (-1, 1):
+        near += with_other_core(lax.ppermute(kv, x_axes, ring(step)))
+    far = []
+    for part in range(2):
+        far += with_other_core(lax.ppermute(kv[:, part], x_axes, ring(2)))
     place = jnp.stack([lax.axis_index("x_lo"), lax.axis_index("x_hi"), lax.axis_index("core")])
-    out = attend(place.astype(jnp.int32), span_mask, span_counts, q, pieces)
+    out = attend(place.astype(jnp.int32), span_mask, span_counts, q, near, far)
     back = exchange(out)
     return back.transpose(1, 0, 2).reshape(1, tok_rows, width)
 

time: 146 us -> 135 us (0.925)
  the two profiles are of different devices: /device:TPU:6 before, /device:TPU:1 now
where the time goes in v3:
time: 135 us; the launch traced here: 134 us
  starting transfers between devices  54.5 us (40%)
  blocking collectives  34.5 us (26%)
  waiting for transfers between devices  29.9 us (22%)
  Pallas kernels  12.8 us (9%)
  local copies, waits for them, and re-layouts  1.86 us (1%)
    all_to_all x1, blocking collectives, exchange(): lax.all_to_all(array, ('y', 'z'), split_axis=0, concat_axis=0, tiled=True)  34.5 us
    all_to_all x2, waiting for transfers between devices, exchange(): lax.all_to_all(array, ('y', 'z'), split_axis=0, concat_axis=0, tiled=True)  28.5 us
    all_to_all x2, starting transfers between devices, exchange(): lax.all_to_all(array, ('y', 'z'), split_axis=0, concat_axis=0, tiled=True)  28.1 us
    ppermute x5, starting transfers between devices, with_other_core(): return [piece, lax.ppermute(piece, 'core', [(0, 1), (1, 0)])]  13.2 us
    pallas_call x1, Pallas kernels, attend(): pl.pallas_call(attend_kernel, out_shape=jax.ShapeDtypeStruct(q.shape, jnp...  10.9 us
    ppermute x2, starting transfers between devices, per_device(): far += with_other_core(lax.ppermute(kv[:, part], x_axes, ring(2)))  6.79 us
    ppermute x2, starting transfers between devices, per_device(): near += with_other_core(lax.ppermute(kv, x_axes, ring(step)))  6.48 us
  transfers between devices with their start and end apart: 11, of which 2 were waited for; matrix products, arithmetic and copies ran while one was open for 1% of the time, Pallas kernels for 0%

profile of v3, /device:TPU:1, one launch (start us, length us, event | category | flops | bytes accessed | tf_op | source)
XLA Modules:
  0.0 133.8 jit_solution(1437729916666557933)
XLA Ops:
  0.0 1.9 %shard_map.55 = bf16[64,2,16,128]{3,2,1,0:T(8,128)(2,1)} custom-call(bf16[16,8192]{1,0:T(8,128)(2,1)} %bitcast.19, bf16[16,8192]{1,0:T(8,128)(2,1)} %bitcast.20), custom_call_target="tpu_custom_call" | custom-call | tf_op jit(solution)/shard_map/pallas_call | solution.py:156
  1.9 19.4 %all-to-all-start = ((bf16[64,2,16,128]{3,2,1,0:T(8,128)(2,1)}), bf16[64,2,16,128]{3,2,1,0:T(8,128)(2,1)S(1)}, u32[]{:S(2)}, u32[]{:S(2)}) async-start(bf16[64,2,16,128]{3,2,1,0:T(8,128)(2,1)} %shard_map.55), calls=%async_computation | async-start | bytes 1048576 | tf_op jit(solution)/shard_map/all_to_all | solution.py:179
  21.3 0.0 copy-done.2
  21.4 0.9 copy.30
  22.3 28.5 %all-to-all-done.rest_0_ = bf16[64,2,16,128]{3,2,1,0:T(8,128)(2,1)S(1)} async-done(((bf16[64,2,16,128]{3,2,1,0:T(8,128)(2,1)}), bf16[64,2,16,128]{3,2,1,0:T(8,128)(2,1)S(1)}, u32[]{:S(2)}, u32[]{:S(2)}) %all-to-all-start) | async-done | bytes 524320 | tf_op jit(solution)/shard_map/all_to_all | solution.py:179
  50.7 3.1 %collective-permute-start.3 = (bf16[64,2,16,128]{3,2,1,0:T(8,128)(2,1)S(1)}, bf16[64,2,16,128]{3,2,1,0:T(8,128)(2,1)S(1)}, u32[]{:S(2)}, u32[]{:S(2)}) collective-permute-start(bf16[64,2,16,128]{3,2,1,0:T(8,128)(2,1)S(1)} %all-to-all-done.rest_0_), channel_id=1, source_target_pairs={{0,64},{64,32},{32,96},{96,0},{1,65},{65,33},{33,97},{97,1},{2,66}... | collective-permute-start | bytes 1572872 | tf_op jit(solution)/shard_map/ppermute | solution.py:192
  53.9 3.4 %collective-permute-start.1 = (bf16[64,2,16,128]{3,2,1,0:T(8,128)(2,1)S(1)}, bf16[64,2,16,128]{3,2,1,0:T(8,128)(2,1)S(1)}, u32[]{:S(2)}, u32[]{:S(2)}) collective-permute-start(bf16[64,2,16,128]{3,2,1,0:T(8,128)(2,1)S(1)} %all-to-all-done.rest_0_), channel_id=1, source_target_pairs={{0,96},{64,0},{32,64},{96,32},{1,97},{65,1},{33,65},{97,33},{2,98}... | collective-permute-start | bytes 1572872 | tf_op jit(solution)/shard_map/ppermute | solution.py:192
  57.2 8.7 %all-to-all-start.1 = ((bf16[64,16,128]{2,1,0:T(8,128)(2,1)}), bf16[64,16,128]{2,1,0:T(8,128)(2,1)S(1)}, u32[]{:S(2)}, u32[]{:S(2)}) async-start(bf16[64,16,128]{2,1,0:T(8,128)(2,1)} %bitcast.15), calls=%async_computation.1 | async-start | bytes 524288 | tf_op jit(solution)/shard_map/all_to_all | solution.py:179
  65.9 3.4 %collective-permute-start.7 = (bf16[64,16,128]{2,1,0:T(8,128)(2,1)S(1)}, bf16[64,16,128]{2,1,0:T(8,128)(2,1)}, u32[]{:S(2)}, u32[]{:S(2)}) collective-permute-start(bf16[64,16,128]{2,1,0:T(8,128)(2,1)S(1)} %get-tuple-element.9), channel_id=1, source_target_pairs={{0,32},{64,96},{32,0},{96,64},{1,33},{65,97},{33,1},{97,65},{2,34}... | collective-permute-start | bytes 786440 | tf_op jit(solution)/shard_map/ppermute | solution.py:195
  69.4 3.3 %collective-permute-start.5 = (bf16[64,16,128]{2,1,0:T(8,128)(2,1)S(1)}, bf16[64,16,128]{2,1,0:T(8,128)(2,1)}, u32[]{:S(2)}, u32[]{:S(2)}) collective-permute-start(bf16[64,16,128]{2,1,0:T(8,128)(2,1)S(1)} %get-tuple-element.10), channel_id=1, source_target_pairs={{0,32},{64,96},{32,0},{96,64},{1,33},{65,97},{33,1},{97,65},{2,34}... | collective-permute-start | bytes 786440 | tf_op jit(solution)/shard_map/ppermute | solution.py:195
  72.8 4.5 %collective-permute-start = (bf16[64,2,16,128]{3,2,1,0:T(8,128)(2,1)S(1)}, bf16[64,2,16,128]{3,2,1,0:T(8,128)(2,1)S(1)}, u32[]{:S(2)}, u32[]{:S(2)}) collective-permute-start(bf16[64,2,16,128]{3,2,1,0:T(8,128)(2,1)S(1)} %all-to-all-done.rest_0_), channel_id=1, source_target_pairs={{0,1},{1,0},{2,3},{3,2},{4,5},{5,4},{6,7},{7,6},{8,9},{9,8},{10,11... | collective-permute-start | bytes 1572872 | tf_op jit(solution)/shard_map/ppermute | solution.py:188
  77.3 0.0 collective-permute-done.3.rest_4_
  77.3 1.9 %collective-permute-start.4 = (bf16[64,2,16,128]{3,2,1,0:T(8,128)(2,1)S(1)}, bf16[64,2,16,128]{3,2,1,0:T(8,128)(2,1)S(1)}, u32[]{:S(2)}, u32[]{:S(2)}) collective-permute-start(bf16[64,2,16,128]{3,2,1,0:T(8,128)(2,1)S(1)} %collective-permute-done.3.rest_4_), channel_id=1, source_target_pairs={{0,1},{1,0},{2,3},{3,2},{4,5},{5,4},{6,7},{7,6},{8,9},{9,8},{10,11... | collective-permute-start | bytes 1572872 | tf_op jit(solution)/shard_map/ppermute | solution.py:188
  79.2 0.0 collective-permute-done.1.rest_2_
  79.2 2.4 %collective-permute-start.2 = (bf16[64,2,16,128]{3,2,1,0:T(8,128)(2,1)S(1)}, bf16[64,2,16,128]{3,2,1,0:T(8,128)(2,1)S(1)}, u32[]{:S(2)}, u32[]{:S(2)}) collective-permute-start(bf16[64,2,16,128]{3,2,1,0:T(8,128)(2,1)S(1)} %collective-permute-done.1.rest_2_), channel_id=1, source_target_pairs={{0,1},{1,0},{2,3},{3,2},{4,5},{5,4},{6,7},{7,6},{8,9},{9,8},{10,11... | collective-permute-start | bytes 1572872 | tf_op jit(solution)/shard_map/ppermute | solution.py:188
  81.6 0.0 collective-permute-done.7.rest_8_
  81.6 1.9 %collective-permute-start.8 = (bf16[64,16,128]{2,1,0:T(8,128)(2,1)}, bf16[64,16,128]{2,1,0:T(8,128)(2,1)}, u32[]{:S(2)}, u32[]{:S(2)}) collective-permute-start(bf16[64,16,128]{2,1,0:T(8,128)(2,1)} %collective-permute-done.7.rest_8_), channel_id=1, source_target_pairs={{0,1},{1,0},{2,3},{3,2},{4,5},{5,4},{6,7},{7,6},{8,9},{9,8},{10,11... | collective-permute-start | bytes 786440 | tf_op jit(solution)/shard_map/ppermute | solution.py:188
  83.6 0.0 collective-permute-done.5.rest_6_
  83.6 2.4 %collective-permute-start.6 = (bf16[64,16,128]{2,1,0:T(8,128)(2,1)}, bf16[64,16,128]{2,1,0:T(8,128)(2,1)}, u32[]{:S(2)}, u32[]{:S(2)}) collective-permute-start(bf16[64,16,128]{2,1,0:T(8,128)(2,1)} %collective-permute-done.5.rest_6_), channel_id=1, source_target_pairs={{0,1},{1,0},{2,3},{3,2},{4,5},{5,4},{6,7},{7,6},{8,9},{9,8},{10,11... | collective-permute-start | bytes 786440 | tf_op jit(solution)/shard_map/ppermute | solution.py:188
  86.0 0.0 copy-start
  86.0 0.0 copy-start.1
  86.0 0.1 pad_add_fusion.place
  86.1 0.0 collective-permute-done.8.rest_9_
  86.1 1.4 %collective-permute-done.6.rest_7_ = bf16[64,16,128]{2,1,0:T(8,128)(2,1)} collective-permute-done((bf16[64,16,128]{2,1,0:T(8,128)(2,1)}, bf16[64,16,128]{2,1,0:T(8,128)(2,1)}, u32[]{:S(2)}, u32[]{:S(2)}) %collective-permute-start.6) | collective-permute-done | bytes 262176 | tf_op jit(solution)/shard_map/ppermute | solution.py:188
  87.5 0.0 collective-permute-done.rest_1_
  87.5 0.0 all-to-all-done.1.q_ref
  87.5 0.0 collective-permute-done.4.rest_5_
  87.5 0.0 collective-permute-done.2.rest_3_
  87.5 10.9 %shard_map.56 = bf16[64,16,128]{2,1,0:T(8,128)(2,1)S(1)} custom-call(s32[3]{0:T(128)S(1)} %pad_add_fusion.place, s32[8,8]{1,0:T(8,128)S(1)} %copy-done, s32[8]{0:T(128)S(1)} %copy-done.1, bf16[64,16,128]{2,1,0:T(8,128)(2,1)S(1)} %all-to-all-done.1.q_ref, bf16[64,2,16,128]{3,2,1,0:T(8,128)(2,1)S(1)} %all-to-all-done.rest_0_, ...), custom_call_target="tpu_custom_call" | custom-call | flops 4294967296 | bytes 5242880 | tf_op jit(solution)/shard_map/pallas_call | solution.py:122
  98.4 34.5 %all_to_all.15 = bf16[64,16,128]{2,1,0:T(8,128)(2,1)S(1)} all-to-all(bf16[64,16,128]{2,1,0:T(8,128)(2,1)S(1)} %shard_map.56), channel_id=1, replica_groups=mesh['y'=4,'x_lo'=2,'x_hi'=2,'z'=16,'core'=2] {'y','z'}, dimensions={0} | all-to-all | bytes 524288 | tf_op jit(solution)/shard_map/all_to_all | solution.py:179
  132.9 0.1 copy.25
  133.0 0.8 reshape.7
  (5 shorter events, 0.1 us)
Async XLA Ops:
  1.9 19.4 %copy-start.2 = (bf16[1,16,8192]{2,1,0:T(8,128)(2,1)S(1)}, bf16[1,16,8192]{2,1,0:T(8,128)(2,1)}, u32[]{:S(2)}) copy-start(bf16[1,16,8192]{2,1,0:T(8,128)(2,1)} %param.5) | copy-start | bytes 786436
  1.9 48.8 %all-to-all-start = ((bf16[64,2,16,128]{3,2,1,0:T(8,128)(2,1)}), bf16[64,2,16,128]{3,2,1,0:T(8,128)(2,1)S(1)}, u32[]{:S(2)}, u32[]{:S(2)}) async-start(bf16[64,2,16,128]{3,2,1,0:T(8,128)(2,1)} %shard_map.55), calls=%async_computation | async-start | bytes 1048576 | tf_op jit(solution)/shard_map/all_to_all | solution.py:179
  50.7 26.5 %collective-permute-start.3 = (bf16[64,2,16,128]{3,2,1,0:T(8,128)(2,1)S(1)}, bf16[64,2,16,128]{3,2,1,0:T(8,128)(2,1)S(1)}, u32[]{:S(2)}, u32[]{:S(2)}) collective-permute-start(bf16[64,2,16,128]{3,2,1,0:T(8,128)(2,1)S(1)} %all-to-all-done.rest_0_), channel_id=1, source_target_pairs={{0,64},{64,32},{32,96},{96,0},{1,65},{65,33},{33,97},{97,1},{2,66}... | collective-permute-start | bytes 1572872 | tf_op jit(solution)/shard_map/ppermute | solution.py:192
  53.9 25.3 %collective-permute-start.1 = (bf16[64,2,16,128]{3,2,1,0:T(8,128)(2,1)S(1)}, bf16[64,2,16,128]{3,2,1,0:T(8,128)(2,1)S(1)}, u32[]{:S(2)}, u32[]{:S(2)}) collective-permute-start(bf16[64,2,16,128]{3,2,1,0:T(8,128)(2,1)S(1)} %all-to-all-done.rest_0_), channel_id=1, source_target_pairs={{0,96},{64,0},{32,64},{96,32},{1,97},{65,1},{33,65},{97,33},{2,98}... | collective-permute-start | bytes 1572872 | tf_op jit(solution)/shard_map/ppermute | solution.py:192
  57.2 30.2 %all-to-all-start.1 = ((bf16[64,16,128]{2,1,0:T(8,128)(2,1)}), bf16[64,16,128]{2,1,0:T(8,128)(2,1)S(1)}, u32[]{:S(2)}, u32[]{:S(2)}) async-start(bf16[64,16,128]{2,1,0:T(8,128)(2,1)} %bitcast.15), calls=%async_computation.1 | async-start | bytes 524288 | tf_op jit(solution)/shard_map/all_to_all | solution.py:179
  65.9 15.7 %collective-permute-start.7 = (bf16[64,16,128]{2,1,0:T(8,128)(2,1)S(1)}, bf16[64,16,128]{2,1,0:T(8,128)(2,1)}, u32[]{:S(2)}, u32[]{:S(2)}) collective-permute-start(bf16[64,16,128]{2,1,0:T(8,128)(2,1)S(1)} %get-tuple-element.9), channel_id=1, source_target_pairs={{0,32},{64,96},{32,0},{96,64},{1,33},{65,97},{33,1},{97,65},{2,34}... | collective-permute-start | bytes 786440 | tf_op jit(solution)/shard_map/ppermute | solution.py:195
  69.4 14.2 %collective-permute-start.5 = (bf16[64,16,128]{2,1,0:T(8,128)(2,1)S(1)}, bf16[64,16,128]{2,1,0:T(8,128)(2,1)}, u32[]{:S(2)}, u32[]{:S(2)}) collective-permute-start(bf16[64,16,128]{2,1,0:T(8,128)(2,1)S(1)} %get-tuple-element.10), channel_id=1, source_target_pairs={{0,32},{64,96},{32,0},{96,64},{1,33},{65,97},{33,1},{97,65},{2,34}... | collective-permute-start | bytes 786440 | tf_op jit(solution)/shard_map/ppermute | solution.py:195
  72.8 14.7 %collective-permute-start = (bf16[64,2,16,128]{3,2,1,0:T(8,128)(2,1)S(1)}, bf16[64,2,16,128]{3,2,1,0:T(8,128)(2,1)S(1)}, u32[]{:S(2)}, u32[]{:S(2)}) collective-permute-start(bf16[64,2,16,128]{3,2,1,0:T(8,128)(2,1)S(1)} %all-to-all-done.rest_0_), channel_id=1, source_target_pairs={{0,1},{1,0},{2,3},{3,2},{4,5},{5,4},{6,7},{7,6},{8,9},{9,8},{10,11... | collective-permute-start | bytes 1572872 | tf_op jit(solution)/shard_map/ppermute | solution.py:188
  77.3 10.2 %collective-permute-start.4 = (bf16[64,2,16,128]{3,2,1,0:T(8,128)(2,1)S(1)}, bf16[64,2,16,128]{3,2,1,0:T(8,128)(2,1)S(1)}, u32[]{:S(2)}, u32[]{:S(2)}) collective-permute-start(bf16[64,2,16,128]{3,2,1,0:T(8,128)(2,1)S(1)} %collective-permute-done.3.rest_4_), channel_id=1, source_target_pairs={{0,1},{1,0},{2,3},{3,2},{4,5},{5,4},{6,7},{7,6},{8,9},{9,8},{10,11... | collective-permute-start | bytes 1572872 | tf_op jit(solution)/shard_map/ppermute | solution.py:188
  79.2 8.3 %collective-permute-start.2 = (bf16[64,2,16,128]{3,2,1,0:T(8,128)(2,1)S(1)}, bf16[64,2,16,128]{3,2,1,0:T(8,128)(2,1)S(1)}, u32[]{:S(2)}, u32[]{:S(2)}) collective-permute-start(bf16[64,2,16,128]{3,2,1,0:T(8,128)(2,1)S(1)} %collective-permute-done.1.rest_2_), channel_id=1, source_target_pairs={{0,1},{1,0},{2,3},{3,2},{4,5},{5,4},{6,7},{7,6},{8,9},{9,8},{10,11... | collective-permute-start | bytes 1572872 | tf_op jit(solution)/shard_map/ppermute | solution.py:188
  81.6 4.5 %collective-permute-start.8 = (bf16[64,16,128]{2,1,0:T(8,128)(2,1)}, bf16[64,16,128]{2,1,0:T(8,128)(2,1)}, u32[]{:S(2)}, u32[]{:S(2)}) collective-permute-start(bf16[64,16,128]{2,1,0:T(8,128)(2,1)} %collective-permute-done.7.rest_8_), channel_id=1, source_target_pairs={{0,1},{1,0},{2,3},{3,2},{4,5},{5,4},{6,7},{7,6},{8,9},{9,8},{10,11... | collective-permute-start | bytes 786440 | tf_op jit(solution)/shard_map/ppermute | solution.py:188
  83.6 3.9 %collective-permute-start.6 = (bf16[64,16,128]{2,1,0:T(8,128)(2,1)}, bf16[64,16,128]{2,1,0:T(8,128)(2,1)}, u32[]{:S(2)}, u32[]{:S(2)}) collective-permute-start(bf16[64,16,128]{2,1,0:T(8,128)(2,1)} %collective-permute-done.5.rest_6_), channel_id=1, source_target_pairs={{0,1},{1,0},{2,3},{3,2},{4,5},{5,4},{6,7},{7,6},{8,9},{9,8},{10,11... | collective-permute-start | bytes 786440 | tf_op jit(solution)/shard_map/ppermute | solution.py:188
  86.0 1.5 %copy-start = (s32[8,8]{1,0:T(8,128)S(1)}, s32[8,8]{1,0:T(8,128)}, u32[]{:S(2)}) copy-start(s32[8,8]{1,0:T(8,128)} %mask.1) | copy-start | bytes 772
  86.0 1.5 %copy-start.1 = (s32[8]{0:T(128)S(1)}, s32[8]{0:T(128)}, u32[]{:S(2)}) copy-start(s32[8]{0:T(128)} %counts.1) | copy-start | bytes 100

commit v4 on v3

--- a/solution.py
+++ b/solution.py
@@ -11,8 +11,8 @@
 
 
 def attend_kernel(place, mask, counts, q_ref, *rest):
-    near, far = rest[:6], rest[6:10]
-    out_ref, k_buf, v_buf, s_a, s_b, m_a, m_b, acc_ref, top_ref, total_ref, todo, sems = rest[10:]
+    pieces = rest[:8]
+    out_ref, k_buf, v_buf, s_a, s_b, m_a, m_b, acc_ref, top_ref, total_ref, todo, sems = rest[8:]
     scores, row_tops = (s_a, s_b), (m_a, m_b)
     x_lo, x_hi, core = place[0], place[1], place[2]
     x = x_hi * 2 + x_lo
@@ -21,7 +21,7 @@
         for part, buf in enumerate((k_buf, v_buf)):
             for e in range(2):
                 copies[d, e, part] = pltpu.make_async_copy(
-                    far[2 * part + e] if d == 2 else near[2 * (d - d // 3) + e].at[:, part],
+                    pieces[2 * d + e].at[:, part],
                     buf.at[d % 2, ((x + d) % 4) // 2, (core + e) % 2],
                     sems.at[2 * d + e, part],
                 )
@@ -116,13 +116,13 @@
         total = jnp.sum(total_ref[iy], axis=1, keepdims=True)
         out_ref[iy * 16 : (iy + 1) * 16] = (acc_ref[iy] / total).astype(jnp.bfloat16).reshape(16, 16, HD)
 
-def attend(place, mask, counts, q, near, far):
+def attend(place, mask, counts, q, pieces):
     smem = pl.BlockSpec(memory_space=pltpu.SMEM)
     vmem = pl.BlockSpec(memory_space=pltpu.VMEM)
     return pl.pallas_call(
         attend_kernel,
         out_shape=jax.ShapeDtypeStruct(q.shape, jnp.bfloat16),
-        in_specs=[smem, smem, smem, vmem] + [pl.BlockSpec(memory_space=pl.ANY)] * 10,
+        in_specs=[smem, smem, smem, vmem] + [pl.BlockSpec(memory_space=pl.ANY)] * 8,
         out_specs=vmem,
         scratch_shapes=[
             pltpu.VMEM((2, 2, 2, 64, 16, HD), jnp.bfloat16),
@@ -141,7 +141,7 @@
         cost_estimate=pl.CostEstimate(
             flops=4 * 1024 * 8192 * HD, bytes_accessed=5 << 20, transcendentals=1024 * 8192
         ),
-    )(place, mask, counts, q, *near, *far)
+    )(place, mask, counts, q, *pieces)
 
 
 def pack_kernel(k_ref, v_ref, out_ref):
@@ -183,18 +183,11 @@
     q = exchange(q_in)
 
     x_axes = ("x_lo", "x_hi")
-
-    def with_other_core(piece):
-        return [piece, lax.ppermute(piece, "core", [(0, 1), (1, 0)])]
-
-    near = with_other_core(kv)
-    for step in (-1, 1):
-        near += with_other_core(lax.ppermute(kv, x_axes, ring(step)))
-    far = []
-    for part in range(2):
-        far += with_other_core(lax.ppermute(kv[:, part], x_axes, ring(2)))
+    pieces = []
+    for piece in [kv] + [lax.ppermute(kv, x_axes, ring(step)) for step in (-1, 2, 1)]:
+        pieces += [piece, lax.ppermute(piece, "core", [(0, 1), (1, 0)])]
     place = jnp.stack([lax.axis_index("x_lo"), lax.axis_index("x_hi"), lax.axis_index("core")])
-    out = attend(place.astype(jnp.int32), span_mask, span_counts, q, near, far)
+    out = attend(place.astype(jnp.int32), span_mask, span_counts, q, pieces)
     back = exchange(out)
     return back.transpose(1, 0, 2).reshape(1, tok_rows, width)
 

time: 135 us -> 128 us (0.948)
  blocking collectives: 34.5 us -> 28.2 us
  waiting for transfers between devices: 29.9 us -> 32.1 us
  starting transfers between devices: 54.5 us -> 52.7 us
  Pallas kernels: 12.8 us -> 11.2 us
    all_to_all x1, blocking collectives: 34.5 us -> 28.2 us  [exchange(): lax.all_to_all(array, ('y', 'z'), split_axis=0, concat_axis=0, tiled=True)]
    all_to_all x2, waiting for transfers between devices: 28.5 us -> 32 us  [exchange(): lax.all_to_all(array, ('y', 'z'), split_axis=0, concat_axis=0, tiled=True)]
    ppermute x9 -> x7, starting transfers between devices: 26.4 us -> 24.7 us  [the longest x4 14.1 us: per_device(): pieces += [piece, lax.ppermute(piece, 'core', [(0, 1), (1, 0)])]]
    pallas_call x1, Pallas kernels: 10.9 us -> 9.3 us  [attend(): pl.pallas_call(attend_kernel, out_shape=jax.ShapeDtypeStruct(q.shape, jnp...]
  transfers between devices with their start and end apart: 11 -> 9, of which waited for: 2 -> 3; matrix products, arithmetic and copies ran while one was open for 1% -> 1% of each run, Pallas kernels for 0% -> 0%
where the time goes in v4:
time: 128 us; the launch traced here: 126 us
  starting transfers between devices  52.7 us (41%)
  waiting for transfers between devices  32.1 us (25%)
  blocking collectives  28.2 us (22%)
  Pallas kernels  11.2 us (9%)
  local copies, waits for them, and re-layouts  1.82 us (1%)
    all_to_all x2, waiting for transfers between devices, exchange(): lax.all_to_all(array, ('y', 'z'), split_axis=0, concat_axis=0, tiled=True)  32 us
    all_to_all x1, blocking collectives, exchange(): lax.all_to_all(array, ('y', 'z'), split_axis=0, concat_axis=0, tiled=True)  28.2 us
    all_to_all x2, starting transfers between devices, exchange(): lax.all_to_all(array, ('y', 'z'), split_axis=0, concat_axis=0, tiled=True)  28.1 us
    ppermute x4, starting transfers between devices, per_device(): pieces += [piece, lax.ppermute(piece, 'core', [(0, 1), (1, 0)])]  14.1 us
    ppermute x3, starting transfers between devices, per_device(): lax.ppermute(kv, x_axes, ring(step))  10.5 us
    pallas_call x1, Pallas kernels, attend(): pl.pallas_call(attend_kernel, out_shape=jax.ShapeDtypeStruct(q.shape, jnp...  9.3 us
  transfers between devices with their start and end apart: 9, of which 3 were waited for; matrix products, arithmetic and copies ran while one was open for 1% of the time, Pallas kernels for 0%

profile of v4, /device:TPU:1, one launch (start us, length us, event | category | flops | bytes accessed | tf_op | source)
XLA Modules:
  0.0 126.3 jit_solution(254711421813290829)
XLA Ops:
  0.0 1.9 %shard_map.55 = bf16[64,2,16,128]{3,2,1,0:T(8,128)(2,1)} custom-call(bf16[16,8192]{1,0:T(8,128)(2,1)} %bitcast.15, bf16[16,8192]{1,0:T(8,128)(2,1)} %bitcast.16), custom_call_target="tpu_custom_call" | custom-call | tf_op jit(solution)/shard_map/pallas_call | solution.py:156
  1.9 0.0 copy-start.2
  1.9 19.4 %all-to-all-start = ((bf16[64,2,16,128]{3,2,1,0:T(8,128)(2,1)}), bf16[64,2,16,128]{3,2,1,0:T(8,128)(2,1)S(1)}, u32[]{:S(2)}, u32[]{:S(2)}) async-start(bf16[64,2,16,128]{3,2,1,0:T(8,128)(2,1)} %shard_map.55), calls=%async_computation | async-start | bytes 1048576 | tf_op jit(solution)/shard_map/all_to_all | solution.py:179
  21.3 0.0 copy-done.2
  21.4 0.9 copy.10
  22.3 28.5 %all-to-all-done.rest_0_ = bf16[64,2,16,128]{3,2,1,0:T(8,128)(2,1)S(1)} async-done(((bf16[64,2,16,128]{3,2,1,0:T(8,128)(2,1)}), bf16[64,2,16,128]{3,2,1,0:T(8,128)(2,1)S(1)}, u32[]{:S(2)}, u32[]{:S(2)}) %all-to-all-start) | async-done | bytes 524320 | tf_op jit(solution)/shard_map/all_to_all | solution.py:179
  50.7 3.1 %collective-permute-start.5 = (bf16[64,2,16,128]{3,2,1,0:T(8,128)(2,1)S(1)}, bf16[64,2,16,128]{3,2,1,0:T(8,128)(2,1)S(1)}, u32[]{:S(2)}, u32[]{:S(2)}) collective-permute-start(bf16[64,2,16,128]{3,2,1,0:T(8,128)(2,1)S(1)} %all-to-all-done.rest_0_), channel_id=1, source_target_pairs={{0,64},{64,32},{32,96},{96,0},{1,65},{65,33},{33,97},{97,1},{2,66}... | collective-permute-start | bytes 1572872 | tf_op jit(solution)/shard_map/ppermute | solution.py:187
  53.9 4.4 %collective-permute-start.3 = (bf16[64,2,16,128]{3,2,1,0:T(8,128)(2,1)S(1)}, bf16[64,2,16,128]{3,2,1,0:T(8,128)(2,1)S(1)}, u32[]{:S(2)}, u32[]{:S(2)}) collective-permute-start(bf16[64,2,16,128]{3,2,1,0:T(8,128)(2,1)S(1)} %all-to-all-done.rest_0_), channel_id=1, source_target_pairs={{0,32},{64,96},{32,0},{96,64},{1,33},{65,97},{33,1},{97,65},{2,34}... | collective-permute-start | bytes 1572872 | tf_op jit(solution)/shard_map/ppermute | solution.py:187
  58.2 3.1 %collective-permute-start.1 = (bf16[64,2,16,128]{3,2,1,0:T(8,128)(2,1)S(1)}, bf16[64,2,16,128]{3,2,1,0:T(8,128)(2,1)S(1)}, u32[]{:S(2)}, u32[]{:S(2)}) collective-permute-start(bf16[64,2,16,128]{3,2,1,0:T(8,128)(2,1)S(1)} %all-to-all-done.rest_0_), channel_id=1, source_target_pairs={{0,96},{64,0},{32,64},{96,32},{1,97},{65,1},{33,65},{97,33},{2,98}... | collective-permute-start | bytes 1572872 | tf_op jit(solution)/shard_map/ppermute | solution.py:187
  61.3 8.7 %all-to-all-start.1 = ((bf16[64,16,128]{2,1,0:T(8,128)(2,1)}), bf16[64,16,128]{2,1,0:T(8,128)(2,1)S(1)}, u32[]{:S(2)}, u32[]{:S(2)}) async-start(bf16[64,16,128]{2,1,0:T(8,128)(2,1)} %bitcast.11), calls=%async_computation.1 | async-start | bytes 524288 | tf_op jit(solution)/shard_map/all_to_all | solution.py:179
  70.0 4.2 %collective-permute-start = (bf16[64,2,16,128]{3,2,1,0:T(8,128)(2,1)S(1)}, bf16[64,2,16,128]{3,2,1,0:T(8,128)(2,1)S(1)}, u32[]{:S(2)}, u32[]{:S(2)}) collective-permute-start(bf16[64,2,16,128]{3,2,1,0:T(8,128)(2,1)S(1)} %all-to-all-done.rest_0_), channel_id=1, source_target_pairs={{0,1},{1,0},{2,3},{3,2},{4,5},{5,4},{6,7},{7,6},{8,9},{9,8},{10,11... | collective-permute-start | bytes 1572872 | tf_op jit(solution)/shard_map/ppermute | solution.py:188
  74.2 0.0 collective-permute-done.5.rest_6_
  74.2 1.9 %collective-permute-start.6 = (bf16[64,2,16,128]{3,2,1,0:T(8,128)(2,1)S(1)}, bf16[64,2,16,128]{3,2,1,0:T(8,128)(2,1)S(1)}, u32[]{:S(2)}, u32[]{:S(2)}) collective-permute-start(bf16[64,2,16,128]{3,2,1,0:T(8,128)(2,1)S(1)} %collective-permute-done.5.rest_6_), channel_id=1, source_target_pairs={{0,1},{1,0},{2,3},{3,2},{4,5},{5,4},{6,7},{7,6},{8,9},{9,8},{10,11... | collective-permute-start | bytes 1572872 | tf_op jit(solution)/shard_map/ppermute | solution.py:188
  76.1 0.1 collective-permute-done.3.rest_4_
  76.2 6.1 %collective-permute-start.4 = (bf16[64,2,16,128]{3,2,1,0:T(8,128)(2,1)S(1)}, bf16[64,2,16,128]{3,2,1,0:T(8,128)(2,1)}, u32[]{:S(2)}, u32[]{:S(2)}) collective-permute-start(bf16[64,2,16,128]{3,2,1,0:T(8,128)(2,1)S(1)} %collective-permute-done.3.rest_4_), channel_id=1, source_target_pairs={{0,1},{1,0},{2,3},{3,2},{4,5},{5,4},{6,7},{7,6},{8,9},{9,8},{10,11... | collective-permute-start | bytes 1572872 | tf_op jit(solution)/shard_map/ppermute | solution.py:188
  82.3 0.0 collective-permute-done.1.rest_2_
  82.3 1.9 %collective-permute-start.2 = (bf16[64,2,16,128]{3,2,1,0:T(8,128)(2,1)S(1)}, bf16[64,2,16,128]{3,2,1,0:T(8,128)(2,1)}, u32[]{:S(2)}, u32[]{:S(2)}) collective-permute-start(bf16[64,2,16,128]{3,2,1,0:T(8,128)(2,1)S(1)} %collective-permute-done.1.rest_2_), channel_id=1, source_target_pairs={{0,1},{1,0},{2,3},{3,2},{4,5},{5,4},{6,7},{7,6},{8,9},{9,8},{10,11... | collective-permute-start | bytes 1572872 | tf_op jit(solution)/shard_map/ppermute | solution.py:188
  84.2 0.0 copy-start
  84.3 0.0 copy-start.1
  84.3 0.1 pad_add_fusion.place
  84.3 0.0 collective-permute-done.rest_1_
  84.3 3.5 %all-to-all-done.1.q_ref = bf16[64,16,128]{2,1,0:T(8,128)(2,1)S(1)} async-done(((bf16[64,16,128]{2,1,0:T(8,128)(2,1)}), bf16[64,16,128]{2,1,0:T(8,128)(2,1)S(1)}, u32[]{:S(2)}, u32[]{:S(2)}) %all-to-all-start.1) | async-done | bytes 262176 | tf_op jit(solution)/shard_map/all_to_all | solution.py:179
  87.9 0.0 collective-permute-done.6.rest_7_
  87.9 0.0 collective-permute-done.4.rest_5_
  87.9 0.0 collective-permute-done.2.rest_3_
  87.9 0.0 copy-done
  87.9 0.0 copy-done.1
  87.9 9.3 %shard_map.56 = bf16[64,16,128]{2,1,0:T(8,128)(2,1)S(1)} custom-call(s32[3]{0:T(128)S(1)} %pad_add_fusion.place, s32[8,8]{1,0:T(8,128)S(1)} %copy-done, s32[8]{0:T(128)S(1)} %copy-done.1, bf16[64,16,128]{2,1,0:T(8,128)(2,1)S(1)} %all-to-all-done.1.q_ref, bf16[64,2,16,128]{3,2,1,0:T(8,128)(2,1)S(1)} %all-to-all-done.rest_0_, ...), custom_call_target="tpu_custom_call" | custom-call | flops 4294967296 | bytes 5242880 | tf_op jit(solution)/shard_map/pallas_call | solution.py:122
  97.2 28.2 %all_to_all.15 = bf16[64,16,128]{2,1,0:T(8,128)(2,1)S(1)} all-to-all(bf16[64,16,128]{2,1,0:T(8,128)(2,1)S(1)} %shard_map.56), channel_id=1, replica_groups=mesh['y'=4,'x_lo'=2,'x_hi'=2,'z'=16,'core'=2] {'y','z'}, dimensions={0} | all-to-all | bytes 524288 | tf_op jit(solution)/shard_map/all_to_all | solution.py:179
  125.4 0.1 copy.7
  125.5 0.8 reshape.7
  (1 shorter events, 0.0 us)
Async XLA Ops:
  1.9 19.4 %copy-start.2 = (bf16[1,16,8192]{2,1,0:T(8,128)(2,1)S(1)}, bf16[1,16,8192]{2,1,0:T(8,128)(2,1)}, u32[]{:S(2)}) copy-start(bf16[1,16,8192]{2,1,0:T(8,128)(2,1)} %param.5) | copy-start | bytes 786436
  1.9 48.8 %all-to-all-start = ((bf16[64,2,16,128]{3,2,1,0:T(8,128)(2,1)}), bf16[64,2,16,128]{3,2,1,0:T(8,128)(2,1)S(1)}, u32[]{:S(2)}, u32[]{:S(2)}) async-start(bf16[64,2,16,128]{3,2,1,0:T(8,128)(2,1)} %shard_map.55), calls=%async_computation | async-start | bytes 1048576 | tf_op jit(solution)/shard_map/all_to_all | solution.py:179
  50.7 23.4 %collective-permute-start.5 = (bf16[64,2,16,128]{3,2,1,0:T(8,128)(2,1)S(1)}, bf16[64,2,16,128]{3,2,1,0:T(8,128)(2,1)S(1)}, u32[]{:S(2)}, u32[]{:S(2)}) collective-permute-start(bf16[64,2,16,128]{3,2,1,0:T(8,128)(2,1)S(1)} %all-to-all-done.rest_0_), channel_id=1, source_target_pairs={{0,64},{64,32},{32,96},{96,0},{1,65},{65,33},{33,97},{97,1},{2,66}... | collective-permute-start | bytes 1572872 | tf_op jit(solution)/shard_map/ppermute | solution.py:187
  53.9 22.4 %collective-permute-start.3 = (bf16[64,2,16,128]{3,2,1,0:T(8,128)(2,1)S(1)}, bf16[64,2,16,128]{3,2,1,0:T(8,128)(2,1)S(1)}, u32[]{:S(2)}, u32[]{:S(2)}) collective-permute-start(bf16[64,2,16,128]{3,2,1,0:T(8,128)(2,1)S(1)} %all-to-all-done.rest_0_), channel_id=1, source_target_pairs={{0,32},{64,96},{32,0},{96,64},{1,33},{65,97},{33,1},{97,65},{2,34}... | collective-permute-start | bytes 1572872 | tf_op jit(solution)/shard_map/ppermute | solution.py:187
  58.2 24.1 %collective-permute-start.1 = (bf16[64,2,16,128]{3,2,1,0:T(8,128)(2,1)S(1)}, bf16[64,2,16,128]{3,2,1,0:T(8,128)(2,1)S(1)}, u32[]{:S(2)}, u32[]{:S(2)}) collective-permute-start(bf16[64,2,16,128]{3,2,1,0:T(8,128)(2,1)S(1)} %all-to-all-done.rest_0_), channel_id=1, source_target_pairs={{0,96},{64,0},{32,64},{96,32},{1,97},{65,1},{33,65},{97,33},{2,98}... | collective-permute-start | bytes 1572872 | tf_op jit(solution)/shard_map/ppermute | solution.py:187
  61.3 26.6 %all-to-all-start.1 = ((bf16[64,16,128]{2,1,0:T(8,128)(2,1)}), bf16[64,16,128]{2,1,0:T(8,128)(2,1)S(1)}, u32[]{:S(2)}, u32[]{:S(2)}) async-start(bf16[64,16,128]{2,1,0:T(8,128)(2,1)} %bitcast.11), calls=%async_computation.1 | async-start | bytes 524288 | tf_op jit(solution)/shard_map/all_to_all | solution.py:179
  70.0 14.4 %collective-permute-start = (bf16[64,2,16,128]{3,2,1,0:T(8,128)(2,1)S(1)}, bf16[64,2,16,128]{3,2,1,0:T(8,128)(2,1)S(1)}, u32[]{:S(2)}, u32[]{:S(2)}) collective-permute-start(bf16[64,2,16,128]{3,2,1,0:T(8,128)(2,1)S(1)} %all-to-all-done.rest_0_), channel_id=1, source_target_pairs={{0,1},{1,0},{2,3},{3,2},{4,5},{5,4},{6,7},{7,6},{8,9},{9,8},{10,11... | collective-permute-start | bytes 1572872 | tf_op jit(solution)/shard_map/ppermute | solution.py:188
  74.2 13.7 %collective-permute-start.6 = (bf16[64,2,16,128]{3,2,1,0:T(8,128)(2,1)S(1)}, bf16[64,2,16,128]{3,2,1,0:T(8,128)(2,1)S(1)}, u32[]{:S(2)}, u32[]{:S(2)}) collective-permute-start(bf16[64,2,16,128]{3,2,1,0:T(8,128)(2,1)S(1)} %collective-permute-done.5.rest_6_), channel_id=1, source_target_pairs={{0,1},{1,0},{2,3},{3,2},{4,5},{5,4},{6,7},{7,6},{8,9},{9,8},{10,11... | collective-permute-start | bytes 1572872 | tf_op jit(solution)/shard_map/ppermute | solution.py:188
  76.2 11.7 %collective-permute-start.4 = (bf16[64,2,16,128]{3,2,1,0:T(8,128)(2,1)S(1)}, bf16[64,2,16,128]{3,2,1,0:T(8,128)(2,1)}, u32[]{:S(2)}, u32[]{:S(2)}) collective-permute-start(bf16[64,2,16,128]{3,2,1,0:T(8,128)(2,1)S(1)} %collective-permute-done.3.rest_4_), channel_id=1, source_target_pairs={{0,1},{1,0},{2,3},{3,2},{4,5},{5,4},{6,7},{7,6},{8,9},{9,8},{10,11... | collective-permute-start | bytes 1572872 | tf_op jit(solution)/shard_map/ppermute | solution.py:188
  82.3 5.6 %collective-permute-start.2 = (bf16[64,2,16,128]{3,2,1,0:T(8,128)(2,1)S(1)}, bf16[64,2,16,128]{3,2,1,0:T(8,128)(2,1)}, u32[]{:S(2)}, u32[]{:S(2)}) collective-permute-start(bf16[64,2,16,128]{3,2,1,0:T(8,128)(2,1)S(1)} %collective-permute-done.1.rest_2_), channel_id=1, source_target_pairs={{0,1},{1,0},{2,3},{3,2},{4,5},{5,4},{6,7},{7,6},{8,9},{9,8},{10,11... | collective-permute-start | bytes 1572872 | tf_op jit(solution)/shard_map/ppermute | solution.py:188
  84.2 3.6 %copy-start = (s32[8,8]{1,0:T(8,128)S(1)}, s32[8,8]{1,0:T(8,128)}, u32[]{:S(2)}) copy-start(s32[8,8]{1,0:T(8,128)} %mask.1) | copy-start | bytes 772
  84.3 3.6 %copy-start.1 = (s32[8]{0:T(128)S(1)}, s32[8]{0:T(128)}, u32[]{:S(2)}) copy-start(s32[8]{0:T(128)} %counts.1) | copy-start | bytes 100

commit v5 on v4

--- a/solution.py
+++ b/solution.py
@@ -14,7 +14,7 @@
     pieces = rest[:8]
     out_ref, k_buf, v_buf, s_a, s_b, m_a, m_b, acc_ref, top_ref, total_ref, todo, sems = rest[8:]
     scores, row_tops = (s_a, s_b), (m_a, m_b)
-    x_lo, x_hi, core = place[0], place[1], place[2]
+    x_lo, x_hi, core, y = place[0], place[1], place[2], place[3]
     x = x_hi * 2 + x_lo
     copies = {}
     for d in range(4):
@@ -55,7 +55,7 @@
         i = todo[n]
         side, iy, jy = i // 16, i // 4 % 4, i % 4
         live = counts[jy * 2 + (x_lo + side) % 2]
-        q = q_ref[pl.ds(iy * 16, 16)].reshape(256, HD)
+        q = q_ref[:, (y + 4 - iy) % 4].reshape(256, HD)
         top = None
         for hi in range(2):
             for c in range(2):
@@ -121,7 +121,7 @@
     vmem = pl.BlockSpec(memory_space=pltpu.VMEM)
     return pl.pallas_call(
         attend_kernel,
-        out_shape=jax.ShapeDtypeStruct(q.shape, jnp.bfloat16),
+        out_shape=jax.ShapeDtypeStruct((64, 16, HD), jnp.bfloat16),
         in_specs=[smem, smem, smem, vmem] + [pl.BlockSpec(memory_space=pl.ANY)] * 8,
         out_specs=vmem,
         scratch_shapes=[
@@ -179,14 +179,23 @@
         return lax.all_to_all(array, ("y", "z"), split_axis=0, concat_axis=0, tiled=True)
 
     kv = exchange(pack(keys[0], values[0]))
-    q_in, kv = lax.optimization_barrier((by_head(queries), kv))
-    q = exchange(q_in)
+    n_y = lax.axis_size("y")
+    y = lax.axis_index("y")
+    by_group = by_head(queries).reshape(n_y, heads // n_y, tok_rows, HD)
+    parts = []
+    for d in range(n_y):
+        part = lax.dynamic_index_in_dim(by_group, (y + d) % n_y, 0, keepdims=False)
+        if d > 0:
+            part = lax.ppermute(part, "y", [(a, (a + d) % n_y) for a in range(n_y)])
+        parts.append(part)
+    q_in, kv = lax.optimization_barrier((jnp.stack(parts, axis=1), kv))
+    q = lax.all_to_all(q_in, "z", split_axis=0, concat_axis=0, tiled=True)
 
     x_axes = ("x_lo", "x_hi")
     pieces = []
     for piece in [kv] + [lax.ppermute(kv, x_axes, ring(step)) for step in (-1, 2, 1)]:
         pieces += [piece, lax.ppermute(piece, "core", [(0, 1), (1, 0)])]
-    place = jnp.stack([lax.axis_index("x_lo"), lax.axis_index("x_hi"), lax.axis_index("core")])
+    place = jnp.stack([lax.axis_index(name) for name in ("x_lo", "x_hi", "core", "y")])
     out = attend(place.astype(jnp.int32), span_mask, span_counts, q, pieces)
     back = exchange(out)
     return back.transpose(1, 0, 2).reshape(1, tok_rows, width)

time: 128 us -> 127 us (level); the launches traced: 126 us -> 127 us
  waiting for transfers between devices: 32.1 us -> 22.6 us
  starting transfers between devices: 52.7 us -> 60.4 us
  Pallas kernels: 11.2 us -> 12.8 us
    all_to_all x2 -> x1, waiting for transfers between devices: 32 us -> 14 us  [exchange(): lax.all_to_all(array, ('y', 'z'), split_axis=0, concat_axis=0, tiled=True)]
    ppermute x0 -> x3, starting transfers between devices: none -> 9.2 us  [per_device(): part = lax.ppermute(part, 'y', [(a, (a + d) % n_y) for a in range(n_y)])]
    all_to_all x2 -> x1, starting transfers between devices: 28.1 us -> 19.4 us  [exchange(): lax.all_to_all(array, ('y', 'z'), split_axis=0, concat_axis=0, tiled=True)]
    all_to_all x0 -> x1, starting transfers between devices: none -> 6.75 us  [per_device(): q = lax.all_to_all(q_in, 'z', split_axis=0, concat_axis=0, tiled=True)]
    ppermute x0 -> x3, waiting for transfers between devices: none -> 5.03 us  [per_device(): part = lax.ppermute(part, 'y', [(a, (a + d) % n_y) for a in range(n_y)])]
    ppermute x4, waiting for transfers between devices: 0.01 us -> 1.88 us  [per_device(): pieces += [piece, lax.ppermute(piece, 'core', [(0, 1), (1, 0)])]]
    pallas_call x1, Pallas kernels: 9.3 us -> 10.9 us  [attend(): pl.pallas_call(attend_kernel, out_shape=jax.ShapeDtypeStruct((64, 16, HD)...]
    ppermute x3, waiting for transfers between devices: 0.09 us -> 1.63 us  [per_device(): lax.ppermute(kv, x_axes, ring(step))]
  transfers between devices with their start and end apart: 9 -> 12, of which waited for: 3 -> 5; matrix products, arithmetic and copies ran while one was open for 1% -> 1% of each run, Pallas kernels for 0% -> 0%
where the time goes in v5:
time: 127 us
  starting transfers between devices  60.4 us (48%)
  blocking collectives  28.6 us (23%)
  waiting for transfers between devices  22.6 us (18%)
  Pallas kernels  12.8 us (10%)
    all_to_all x1, blocking collectives, exchange(): lax.all_to_all(array, ('y', 'z'), split_axis=0, concat_axis=0, tiled=True)  28.6 us
    all_to_all x1, starting transfers between devices, exchange(): lax.all_to_all(array, ('y', 'z'), split_axis=0, concat_axis=0, tiled=True)  19.4 us
    ppermute x4, starting transfers between devices, per_device(): pieces += [piece, lax.ppermute(piece, 'core', [(0, 1), (1, 0)])]  14.5 us
    all_to_all x1, waiting for transfers between devices, exchange(): lax.all_to_all(array, ('y', 'z'), split_axis=0, concat_axis=0, tiled=True)  14 us
    pallas_call x1, Pallas kernels, attend(): pl.pallas_call(attend_kernel, out_shape=jax.ShapeDtypeStruct((64, 16, HD)...  10.9 us
    ppermute x3, starting transfers between devices, per_device(): lax.ppermute(kv, x_axes, ring(step))  10.5 us
    ppermute x3, starting transfers between devices, per_device(): part = lax.ppermute(part, 'y', [(a, (a + d) % n_y) for a in range(n_y)])  9.2 us
    all_to_all x1, starting transfers between devices, per_device(): q = lax.all_to_all(q_in, 'z', split_axis=0, concat_axis=0, tiled=True)  6.75 us
  transfers between devices with their start and end apart: 12, of which 5 were waited for; matrix products, arithmetic and copies ran while one was open for 1% of the time, Pallas kernels for 0%

profile of v5, /device:TPU:1, one launch (start us, length us, event | category | flops | bytes accessed | tf_op | source)
XLA Modules:
  0.0 126.7 jit_solution(2856617546509593803)
XLA Ops:
  0.0 1.9 %shard_map.55 = bf16[64,2,16,128]{3,2,1,0:T(8,128)(2,1)} custom-call(bf16[16,8192]{1,0:T(8,128)(2,1)} %bitcast.28, bf16[16,8192]{1,0:T(8,128)(2,1)} %bitcast.29), custom_call_target="tpu_custom_call" | custom-call | tf_op jit(solution)/shard_map/pallas_call | solution.py:156
  1.9 19.4 %all-to-all-start = ((bf16[64,2,16,128]{3,2,1,0:T(8,128)(2,1)}), bf16[64,2,16,128]{3,2,1,0:T(8,128)(2,1)S(1)}, u32[]{:S(2)}, u32[]{:S(2)}) async-start(bf16[64,2,16,128]{3,2,1,0:T(8,128)(2,1)} %shard_map.55), calls=%async_computation | async-start | bytes 1048576 | tf_op jit(solution)/shard_map/all_to_all | solution.py:179
  21.4 0.2 copy.7
  21.7 4.3 %collective-permute-start.2 = (bf16[16,16,128]{2,1,0:T(8,128)(2,1)S(1)}, bf16[16,16,128]{2,1,0:T(8,128)(2,1)S(1)}, u32[]{:S(2)}, u32[]{:S(2)}) collective-permute-start(bf16[16,16,128]{2,1,0:T(8,128)(2,1)S(1)} %get-tuple-element.10), channel_id=1, source_target_pairs={{0,384},{128,0},{256,128},{384,256},{1,385},{129,1},{257,129},{385... | collective-permute-start | bytes 196616 | tf_op jit(solution)/shard_map/ppermute | solution.py:189
  26.0 2.3 %collective-permute-start.1 = (bf16[16,16,128]{2,1,0:T(8,128)(2,1)S(1)}, bf16[16,16,128]{2,1,0:T(8,128)(2,1)S(1)}, u32[]{:S(2)}, u32[]{:S(2)}) collective-permute-start(bf16[16,16,128]{2,1,0:T(8,128)(2,1)S(1)} %get-tuple-element.11), channel_id=1, source_target_pairs={{0,256},{128,384},{256,0},{384,128},{1,257},{129,385},{257,1},{385... | collective-permute-start | bytes 196616 | tf_op jit(solution)/shard_map/ppermute | solution.py:189
  28.3 2.6 %collective-permute-start = (bf16[16,16,128]{2,1,0:T(8,128)(2,1)S(1)}, bf16[16,16,128]{2,1,0:T(8,128)(2,1)S(1)}, u32[]{:S(2)}, u32[]{:S(2)}) collective-permute-start(bf16[16,16,128]{2,1,0:T(8,128)(2,1)S(1)} %get-tuple-element.12), channel_id=1, source_target_pairs={{0,128},{128,256},{256,384},{384,0},{1,129},{129,257},{257,385},{3... | collective-permute-start | bytes 196616 | tf_op jit(solution)/shard_map/ppermute | solution.py:189
  30.9 0.0 collective-permute-done.2
  30.9 2.2 %collective-permute-done.1 = bf16[16,16,128]{2,1,0:T(8,128)(2,1)S(1)} collective-permute-done((bf16[16,16,128]{2,1,0:T(8,128)(2,1)S(1)}, bf16[16,16,128]{2,1,0:T(8,128)(2,1)S(1)}, u32[]{:S(2)}, u32[]{:S(2)}) %collective-permute-start.1) | collective-permute-done | bytes 65568 | tf_op jit(solution)/shard_map/ppermute | solution.py:189
  33.1 2.9 %collective-permute-done = bf16[16,16,128]{2,1,0:T(8,128)(2,1)S(1)} collective-permute-done((bf16[16,16,128]{2,1,0:T(8,128)(2,1)S(1)}, bf16[16,16,128]{2,1,0:T(8,128)(2,1)S(1)}, u32[]{:S(2)}, u32[]{:S(2)}) %collective-permute-start) | collective-permute-done | bytes 65568 | tf_op jit(solution)/shard_map/ppermute | solution.py:189
  36.0 0.7 pad_maximum_fusion
  36.7 14.0 %all-to-all-done.rest_0_ = bf16[64,2,16,128]{3,2,1,0:T(8,128)(2,1)S(1)} async-done(((bf16[64,2,16,128]{3,2,1,0:T(8,128)(2,1)}), bf16[64,2,16,128]{3,2,1,0:T(8,128)(2,1)S(1)}, u32[]{:S(2)}, u32[]{:S(2)}) %all-to-all-start) | async-done | bytes 524320 | tf_op jit(solution)/shard_map/all_to_all | solution.py:179
  50.7 3.1 %collective-permute-start.8 = (bf16[64,2,16,128]{3,2,1,0:T(8,128)(2,1)S(1)}, bf16[64,2,16,128]{3,2,1,0:T(8,128)(2,1)S(1)}, u32[]{:S(2)}, u32[]{:S(2)}) collective-permute-start(bf16[64,2,16,128]{3,2,1,0:T(8,128)(2,1)S(1)} %all-to-all-done.rest_0_), channel_id=1, source_target_pairs={{0,64},{64,32},{32,96},{96,0},{1,65},{65,33},{33,97},{97,1},{2,66}... | collective-permute-start | bytes 1572872 | tf_op jit(solution)/shard_map/ppermute | solution.py:196
  53.8 4.4 %collective-permute-start.6 = (bf16[64,2,16,128]{3,2,1,0:T(8,128)(2,1)S(1)}, bf16[64,2,16,128]{3,2,1,0:T(8,128)(2,1)S(1)}, u32[]{:S(2)}, u32[]{:S(2)}) collective-permute-start(bf16[64,2,16,128]{3,2,1,0:T(8,128)(2,1)S(1)} %all-to-all-done.rest_0_), channel_id=1, source_target_pairs={{0,32},{64,96},{32,0},{96,64},{1,33},{65,97},{33,1},{97,65},{2,34}... | collective-permute-start | bytes 1572872 | tf_op jit(solution)/shard_map/ppermute | solution.py:196
  58.2 3.1 %collective-permute-start.4 = (bf16[64,2,16,128]{3,2,1,0:T(8,128)(2,1)S(1)}, bf16[64,2,16,128]{3,2,1,0:T(8,128)(2,1)S(1)}, u32[]{:S(2)}, u32[]{:S(2)}) collective-permute-start(bf16[64,2,16,128]{3,2,1,0:T(8,128)(2,1)S(1)} %all-to-all-done.rest_0_), channel_id=1, source_target_pairs={{0,96},{64,0},{32,64},{96,32},{1,97},{65,1},{33,65},{97,33},{2,98}... | collective-permute-start | bytes 1572872 | tf_op jit(solution)/shard_map/ppermute | solution.py:196
  61.3 6.7 %all-to-all-start.1 = ((bf16[16,4,16,128]{3,2,1,0:T(8,128)(2,1)}), bf16[16,4,16,128]{3,2,1,0:T(8,128)(2,1)S(1)}, u32[]{:S(2)}, u32[]{:S(2)}) async-start(bf16[16,4,16,128]{3,2,1,0:T(8,128)(2,1)} %pad_maximum_fusion), calls=%async_computation.1 | async-start | bytes 524288 | tf_op jit(solution)/shard_map/all_to_all | solution.py:192
  68.0 4.6 %collective-permute-start.3 = (bf16[64,2,16,128]{3,2,1,0:T(8,128)(2,1)S(1)}, bf16[64,2,16,128]{3,2,1,0:T(8,128)(2,1)S(1)}, u32[]{:S(2)}, u32[]{:S(2)}) collective-permute-start(bf16[64,2,16,128]{3,2,1,0:T(8,128)(2,1)S(1)} %all-to-all-done.rest_0_), channel_id=1, source_target_pairs={{0,1},{1,0},{2,3},{3,2},{4,5},{5,4},{6,7},{7,6},{8,9},{9,8},{10,11... | collective-permute-start | bytes 1572872 | tf_op jit(solution)/shard_map/ppermute | solution.py:197
  72.6 0.0 collective-permute-done.8.rest_6_
  72.7 1.9 %collective-permute-start.9 = (bf16[64,2,16,128]{3,2,1,0:T(8,128)(2,1)S(1)}, bf16[64,2,16,128]{3,2,1,0:T(8,128)(2,1)S(1)}, u32[]{:S(2)}, u32[]{:S(2)}) collective-permute-start(bf16[64,2,16,128]{3,2,1,0:T(8,128)(2,1)S(1)} %collective-permute-done.8.rest_6_), channel_id=1, source_target_pairs={{0,1},{1,0},{2,3},{3,2},{4,5},{5,4},{6,7},{7,6},{8,9},{9,8},{10,11... | collective-permute-start | bytes 1572872 | tf_op jit(solution)/shard_map/ppermute | solution.py:197
  74.6 1.6 %collective-permute-done.6.rest_4_ = bf16[64,2,16,128]{3,2,1,0:T(8,128)(2,1)S(1)} collective-permute-done((bf16[64,2,16,128]{3,2,1,0:T(8,128)(2,1)S(1)}, bf16[64,2,16,128]{3,2,1,0:T(8,128)(2,1)S(1)}, u32[]{:S(2)}, u32[]{:S(2)}) %collective-permute-start.6) | collective-permute-done | bytes 524320 | tf_op jit(solution)/shard_map/ppermute | solution.py:196
  76.2 6.1 %collective-permute-start.7 = (bf16[64,2,16,128]{3,2,1,0:T(8,128)(2,1)S(1)}, bf16[64,2,16,128]{3,2,1,0:T(8,128)(2,1)}, u32[]{:S(2)}, u32[]{:S(2)}) collective-permute-start(bf16[64,2,16,128]{3,2,1,0:T(8,128)(2,1)S(1)} %collective-permute-done.6.rest_4_), channel_id=1, source_target_pairs={{0,1},{1,0},{2,3},{3,2},{4,5},{5,4},{6,7},{7,6},{8,9},{9,8},{10,11... | collective-permute-start | bytes 1572872 | tf_op jit(solution)/shard_map/ppermute | solution.py:197
  82.3 1.9 %collective-permute-start.5 = (bf16[64,2,16,128]{3,2,1,0:T(8,128)(2,1)S(1)}, bf16[64,2,16,128]{3,2,1,0:T(8,128)(2,1)}, u32[]{:S(2)}, u32[]{:S(2)}) collective-permute-start(bf16[64,2,16,128]{3,2,1,0:T(8,128)(2,1)S(1)} %collective-permute-done.4.rest_2_), channel_id=1, source_target_pairs={{0,1},{1,0},{2,3},{3,2},{4,5},{5,4},{6,7},{7,6},{8,9},{9,8},{10,11... | collective-permute-start | bytes 1572872 | tf_op jit(solution)/shard_map/ppermute | solution.py:197
  84.2 0.0 copy-start
  84.2 0.0 copy-start.1
  84.3 0.1 pad_add_fusion.place
  84.3 0.0 collective-permute-done.3.rest_1_
  84.3 0.0 all-to-all-done.1.q_ref
  84.3 0.0 collective-permute-done.9.rest_7_
  84.4 1.9 %collective-permute-done.5.rest_3_ = bf16[64,2,16,128]{3,2,1,0:T(8,128)(2,1)} collective-permute-done((bf16[64,2,16,128]{3,2,1,0:T(8,128)(2,1)S(1)}, bf16[64,2,16,128]{3,2,1,0:T(8,128)(2,1)}, u32[]{:S(2)}, u32[]{:S(2)}) %collective-permute-start.5) | collective-permute-done | bytes 524320 | tf_op jit(solution)/shard_map/ppermute | solution.py:197
  86.2 10.9 %shard_map.56 = bf16[64,16,128]{2,1,0:T(8,128)(2,1)S(1)} custom-call(s32[4]{0:T(128)S(1)} %pad_add_fusion.place, s32[8,8]{1,0:T(8,128)S(1)} %copy-done, s32[8]{0:T(128)S(1)} %copy-done.1, bf16[16,4,16,128]{3,2,1,0:T(8,128)(2,1)S(1)} %all-to-all-done.1.q_ref, bf16[64,2,16,128]{3,2,1,0:T(8,128)(2,1)S(1)} %all-to-all-done.rest_0_, ...), custom_call_target="tpu_custom_call" | custom-call | flops 4294967296 | bytes 5242880 | tf_op jit(solution)/shard_map/pallas_call | solution.py:122
  97.2 28.6 %all_to_all.15 = bf16[64,16,128]{2,1,0:T(8,128)(2,1)S(1)} all-to-all(bf16[64,16,128]{2,1,0:T(8,128)(2,1)S(1)} %shard_map.56), channel_id=1, replica_groups=mesh['y'=4,'x_lo'=2,'x_hi'=2,'z'=16,'core'=2] {'y','z'}, dimensions={0} | all-to-all | bytes 524288 | tf_op jit(solution)/shard_map/all_to_all | solution.py:179
  125.8 0.1 copy.8
  125.9 0.8 reshape.12
  (8 shorter events, 0.1 us)
Async XLA Ops:
  1.9 19.5 %copy-start.2 = (bf16[1,16,8192]{2,1,0:T(8,128)(2,1)S(1)}, bf16[1,16,8192]{2,1,0:T(8,128)(2,1)}, u32[]{:S(2)}) copy-start(bf16[1,16,8192]{2,1,0:T(8,128)(2,1)} %param.5) | copy-start | bytes 786436
  1.9 48.8 %all-to-all-start = ((bf16[64,2,16,128]{3,2,1,0:T(8,128)(2,1)}), bf16[64,2,16,128]{3,2,1,0:T(8,128)(2,1)S(1)}, u32[]{:S(2)}, u32[]{:S(2)}) async-start(bf16[64,2,16,128]{3,2,1,0:T(8,128)(2,1)} %shard_map.55), calls=%async_computation | async-start | bytes 1048576 | tf_op jit(solution)/shard_map/all_to_all | solution.py:179
  21.7 9.2 %collective-permute-start.2 = (bf16[16,16,128]{2,1,0:T(8,128)(2,1)S(1)}, bf16[16,16,128]{2,1,0:T(8,128)(2,1)S(1)}, u32[]{:S(2)}, u32[]{:S(2)}) collective-permute-start(bf16[16,16,128]{2,1,0:T(8,128)(2,1)S(1)} %get-tuple-element.10), channel_id=1, source_target_pairs={{0,384},{128,0},{256,128},{384,256},{1,385},{129,1},{257,129},{385... | collective-permute-start | bytes 196616 | tf_op jit(solution)/shard_map/ppermute | solution.py:189
  26.0 7.1 %collective-permute-start.1 = (bf16[16,16,128]{2,1,0:T(8,128)(2,1)S(1)}, bf16[16,16,128]{2,1,0:T(8,128)(2,1)S(1)}, u32[]{:S(2)}, u32[]{:S(2)}) collective-permute-start(bf16[16,16,128]{2,1,0:T(8,128)(2,1)S(1)} %get-tuple-element.11), channel_id=1, source_target_pairs={{0,256},{128,384},{256,0},{384,128},{1,257},{129,385},{257,1},{385... | collective-permute-start | bytes 196616 | tf_op jit(solution)/shard_map/ppermute | solution.py:189
  28.3 7.6 %collective-permute-start = (bf16[16,16,128]{2,1,0:T(8,128)(2,1)S(1)}, bf16[16,16,128]{2,1,0:T(8,128)(2,1)S(1)}, u32[]{:S(2)}, u32[]{:S(2)}) collective-permute-start(bf16[16,16,128]{2,1,0:T(8,128)(2,1)S(1)} %get-tuple-element.12), channel_id=1, source_target_pairs={{0,128},{128,256},{256,384},{384,0},{1,129},{129,257},{257,385},{3... | collective-permute-start | bytes 196616 | tf_op jit(solution)/shard_map/ppermute | solution.py:189
  50.7 21.9 %collective-permute-start.8 = (bf16[64,2,16,128]{3,2,1,0:T(8,128)(2,1)S(1)}, bf16[64,2,16,128]{3,2,1,0:T(8,128)(2,1)S(1)}, u32[]{:S(2)}, u32[]{:S(2)}) collective-permute-start(bf16[64,2,16,128]{3,2,1,0:T(8,128)(2,1)S(1)} %all-to-all-done.rest_0_), channel_id=1, source_target_pairs={{0,64},{64,32},{32,96},{96,0},{1,65},{65,33},{33,97},{97,1},{2,66}... | collective-permute-start | bytes 1572872 | tf_op jit(solution)/shard_map/ppermute | solution.py:196
  53.8 22.4 %collective-permute-start.6 = (bf16[64,2,16,128]{3,2,1,0:T(8,128)(2,1)S(1)}, bf16[64,2,16,128]{3,2,1,0:T(8,128)(2,1)S(1)}, u32[]{:S(2)}, u32[]{:S(2)}) collective-permute-start(bf16[64,2,16,128]{3,2,1,0:T(8,128)(2,1)S(1)} %all-to-all-done.rest_0_), channel_id=1, source_target_pairs={{0,32},{64,96},{32,0},{96,64},{1,33},{65,97},{33,1},{97,65},{2,34}... | collective-permute-start | bytes 1572872 | tf_op jit(solution)/shard_map/ppermute | solution.py:196
  58.2 24.1 %collective-permute-start.4 = (bf16[64,2,16,128]{3,2,1,0:T(8,128)(2,1)S(1)}, bf16[64,2,16,128]{3,2,1,0:T(8,128)(2,1)S(1)}, u32[]{:S(2)}, u32[]{:S(2)}) collective-permute-start(bf16[64,2,16,128]{3,2,1,0:T(8,128)(2,1)S(1)} %all-to-all-done.rest_0_), channel_id=1, source_target_pairs={{0,96},{64,0},{32,64},{96,32},{1,97},{65,1},{33,65},{97,33},{2,98}... | collective-permute-start | bytes 1572872 | tf_op jit(solution)/shard_map/ppermute | solution.py:196
  61.3 23.1 %all-to-all-start.1 = ((bf16[16,4,16,128]{3,2,1,0:T(8,128)(2,1)}), bf16[16,4,16,128]{3,2,1,0:T(8,128)(2,1)S(1)}, u32[]{:S(2)}, u32[]{:S(2)}) async-start(bf16[16,4,16,128]{3,2,1,0:T(8,128)(2,1)} %pad_maximum_fusion), calls=%async_computation.1 | async-start | bytes 524288 | tf_op jit(solution)/shard_map/all_to_all | solution.py:192
  68.0 16.3 %collective-permute-start.3 = (bf16[64,2,16,128]{3,2,1,0:T(8,128)(2,1)S(1)}, bf16[64,2,16,128]{3,2,1,0:T(8,128)(2,1)S(1)}, u32[]{:S(2)}, u32[]{:S(2)}) collective-permute-start(bf16[64,2,16,128]{3,2,1,0:T(8,128)(2,1)S(1)} %all-to-all-done.rest_0_), channel_id=1, source_target_pairs={{0,1},{1,0},{2,3},{3,2},{4,5},{5,4},{6,7},{7,6},{8,9},{9,8},{10,11... | collective-permute-start | bytes 1572872 | tf_op jit(solution)/shard_map/ppermute | solution.py:197
  72.7 11.7 %collective-permute-start.9 = (bf16[64,2,16,128]{3,2,1,0:T(8,128)(2,1)S(1)}, bf16[64,2,16,128]{3,2,1,0:T(8,128)(2,1)S(1)}, u32[]{:S(2)}, u32[]{:S(2)}) collective-permute-start(bf16[64,2,16,128]{3,2,1,0:T(8,128)(2,1)S(1)} %collective-permute-done.8.rest_6_), channel_id=1, source_target_pairs={{0,1},{1,0},{2,3},{3,2},{4,5},{5,4},{6,7},{7,6},{8,9},{9,8},{10,11... | collective-permute-start | bytes 1572872 | tf_op jit(solution)/shard_map/ppermute | solution.py:197
  76.2 8.2 %collective-permute-start.7 = (bf16[64,2,16,128]{3,2,1,0:T(8,128)(2,1)S(1)}, bf16[64,2,16,128]{3,2,1,0:T(8,128)(2,1)}, u32[]{:S(2)}, u32[]{:S(2)}) collective-permute-start(bf16[64,2,16,128]{3,2,1,0:T(8,128)(2,1)S(1)} %collective-permute-done.6.rest_4_), channel_id=1, source_target_pairs={{0,1},{1,0},{2,3},{3,2},{4,5},{5,4},{6,7},{7,6},{8,9},{9,8},{10,11... | collective-permute-start | bytes 1572872 | tf_op jit(solution)/shard_map/ppermute | solution.py:197
  82.3 3.9 %collective-permute-start.5 = (bf16[64,2,16,128]{3,2,1,0:T(8,128)(2,1)S(1)}, bf16[64,2,16,128]{3,2,1,0:T(8,128)(2,1)}, u32[]{:S(2)}, u32[]{:S(2)}) collective-permute-start(bf16[64,2,16,128]{3,2,1,0:T(8,128)(2,1)S(1)} %collective-permute-done.4.rest_2_), channel_id=1, source_target_pairs={{0,1},{1,0},{2,3},{3,2},{4,5},{5,4},{6,7},{7,6},{8,9},{9,8},{10,11... | collective-permute-start | bytes 1572872 | tf_op jit(solution)/shard_map/ppermute | solution.py:197
  84.2 2.0 %copy-start = (s32[8,8]{1,0:T(8,128)S(1)}, s32[8,8]{1,0:T(8,128)}, u32[]{:S(2)}) copy-start(s32[8,8]{1,0:T(8,128)} %mask.1) | copy-start | bytes 772
  84.2 2.0 %copy-start.1 = (s32[8]{0:T(128)S(1)}, s32[8]{0:T(128)}, u32[]{:S(2)}) copy-start(s32[8]{0:T(128)} %counts.1) | copy-start | bytes 100

commit v6 on v5

--- a/solution.py
+++ b/solution.py
@@ -8,12 +8,14 @@
 HD = 128
 LOW = -1e30
 LOG2E = 1.4426950408889634
+UNROLL = 2
 
 
 def attend_kernel(place, mask, counts, q_ref, *rest):
     pieces = rest[:8]
-    out_ref, k_buf, v_buf, s_a, s_b, m_a, m_b, acc_ref, top_ref, total_ref, todo, sems = rest[8:]
-    scores, row_tops = (s_a, s_b), (m_a, m_b)
+    out_ref, k_buf, v_buf = rest[8:11]
+    scores, row_tops = rest[11 : 11 + 2 * UNROLL], rest[11 + 2 * UNROLL : 11 + 4 * UNROLL]
+    acc_ref, top_ref, total_ref, todo, sems = rest[11 + 4 * UNROLL :]
     x_lo, x_hi, core, y = place[0], place[1], place[2], place[3]
     x = x_hi * 2 + x_lo
     copies = {}
@@ -52,66 +54,75 @@
     late = 768 + lane // 16 * 32 + lane % 16
 
     def score(n, slot):
-        i = todo[n]
+        i = todo[jnp.minimum(n, count - 1)]
         side, iy, jy = i // 16, i // 4 % 4, i % 4
         live = counts[jy * 2 + (x_lo + side) % 2]
         q = q_ref[:, (y + 4 - iy) % 4].reshape(256, HD)
+        k = k_buf[side, :, :, pl.ds(jy * 16, 16)].reshape(1024, HD)
+        s = lax.dot_general(q, k, (((1,), (1,)), ((), ())), preferred_element_type=jnp.float32)
         top = None
-        for hi in range(2):
-            for c in range(2):
-                k = k_buf[side, hi, c, pl.ds(jy * 16, 16)].reshape(256, HD)
-                s = lax.dot_general(q, k, (((1,), (1,)), ((), ())), preferred_element_type=jnp.float32)
-                a, b = s[:, :128], s[:, 128:]
-                if hi == 1:
-                    b = jnp.where(late + c * 16 < live, b, LOW)
-                at = (hi * 2 + c) * 256
-                scores[slot][:, at : at + 128] = a
-                scores[slot][:, at + 128 : at + 256] = b
-                both = jnp.maximum(a, b)
-                top = both if top is None else jnp.maximum(top, both)
+        for g in range(8):
+            a = s[:, g * 128 : (g + 1) * 128]
+            if g >= 4 and g % 2 == 1:
+                a = jnp.where(late + g // 2 % 2 * 16 < live, a, LOW)
+            scores[slot][:, g * 128 : (g + 1) * 128] = a
+            top = a if top is None else jnp.maximum(top, a)
         row_tops[slot][...] = jnp.broadcast_to(jnp.max(top, axis=1, keepdims=True), (256, 128))
 
-    def half(n, slot):
-        i = todo[n]
-        side, iy, jy = i // 16, i // 4 % 4, i % 4
-
-        @pl.when(n + 1 == first)
-        def _():
-            wait(1, 0)
-            wait(1, 1)
-        old = top_ref[iy]
-        top = jnp.maximum(old, row_tops[slot][...])
-        shift = top * scale
-        factor = jnp.exp2(old * scale - shift)
-        total = total_ref[iy] * factor
-        acc = acc_ref[iy] * factor
-        score(jnp.minimum(n + 1, count - 1), 1 - slot)
+    def mix(n, slot):
+        i = todo[jnp.minimum(n, count - 1)]
+        side, jy = i // 16, i % 4
+        shift = row_tops[slot][...] * scale
+        total, weights = None, []
         for g in range(4):
             at = g * 256
             wa = jnp.exp2(scores[slot][:, at : at + 128] * scale - shift)
             wb = jnp.exp2(scores[slot][:, at + 128 : at + 256] * scale - shift)
-            total = total + wa + wb
             w = jnp.concatenate([wa.astype(jnp.bfloat16), wb.astype(jnp.bfloat16)], axis=1)
-            v = v_buf[side, g // 2, g % 2, pl.ds(jy * 16, 16)].reshape(256, HD)
-            acc = acc + jnp.dot(w, v, preferred_element_type=jnp.float32)
-        total_ref[iy] = total
-        top_ref[iy] = top
-        acc_ref[iy] = acc
+            weights.append(w)
+            total = wa + wb if total is None else total + (wa + wb)
+        v = v_buf[side, :, :, pl.ds(jy * 16, 16)].reshape(1024, HD)
+        acc = jnp.dot(jnp.concatenate(weights, axis=1), v, preferred_element_type=jnp.float32)
+        return row_tops[slot][...], total, acc
+
+    def merge(n, state):
+        top, total, acc = state
+        iy = todo[jnp.minimum(n, count - 1)] // 4 % 4
+        top = jnp.where(n < count, top, LOW)
+        old = top_ref[iy]
+        new = jnp.maximum(old, top)
+        keep, add = jnp.exp2((old - new) * scale), jnp.exp2((top - new) * scale)
+        total_ref[iy] = total_ref[iy] * keep + total * add
+        acc_ref[iy] = acc_ref[iy] * keep + acc * add
+        top_ref[iy] = new
+
+    def step(n, slot):
+        @pl.when((n + 2 * UNROLL > first) & (n + UNROLL <= first))
+        def _():
+            wait(1, 0)
+            wait(1, 1)
+
+        for u in range(UNROLL):
+            score(n + UNROLL + u, (1 - slot) * UNROLL + u)
+        states = [mix(n + u, slot * UNROLL + u) for u in range(UNROLL)]
+        for u in range(UNROLL):
+            merge(n + u, states[u])
 
     wait(0, 0)
-    score(0, 0)
+    for u in range(UNROLL):
+        score(u, u)
     wait(0, 1)
 
-    def pair(n, _):
-        half(2 * n, 0)
-
-        @pl.when(2 * n + 1 < count)
+    def pair(m, _):
+        step(2 * UNROLL * m, 0)
+
+        @pl.when(2 * UNROLL * m + UNROLL < count)
         def _():
-            half(2 * n + 1, 1)
+            step(2 * UNROLL * m + UNROLL, 1)
 
         return 0
 
-    lax.fori_loop(0, (count + 1) // 2, pair, 0)
+    lax.fori_loop(0, (count + 2 * UNROLL - 1) // (2 * UNROLL), pair, 0)
     for iy in range(4):
         total = jnp.sum(total_ref[iy], axis=1, keepdims=True)
         out_ref[iy * 16 : (iy + 1) * 16] = (acc_ref[iy] / total).astype(jnp.bfloat16).reshape(16, 16, HD)
@@ -127,10 +138,8 @@
         scratch_shapes=[
             pltpu.VMEM((2, 2, 2, 64, 16, HD), jnp.bfloat16),
             pltpu.VMEM((2, 2, 2, 64, 16, HD), jnp.bfloat16),
-            pltpu.VMEM((256, 1024), jnp.float32),
-            pltpu.VMEM((256, 1024), jnp.float32),
-            pltpu.VMEM((256, HD), jnp.float32),
-            pltpu.VMEM((256, HD), jnp.float32),
+            *[pltpu.VMEM((256, 1024), jnp.float32)] * (2 * UNROLL),
+            *[pltpu.VMEM((256, HD), jnp.float32)] * (2 * UNROLL),
             pltpu.VMEM((4, 256, HD), jnp.float32),
             pltpu.VMEM((4, 256, HD), jnp.float32),
             pltpu.VMEM((4, 256, HD), jnp.float32),
@@ -193,8 +202,9 @@
 
     x_axes = ("x_lo", "x_hi")
     pieces = []
-    for piece in [kv] + [lax.ppermute(kv, x_axes, ring(step)) for step in (-1, 2, 1)]:
+    for piece in [kv] + [lax.ppermute(kv, x_axes, ring(step)) for step in (-1, 1, 2)]:
         pieces += [piece, lax.ppermute(piece, "core", [(0, 1), (1, 0)])]
+    pieces = pieces[:4] + pieces[6:] + pieces[4:6]
     place = jnp.stack([lax.axis_index(name) for name in ("x_lo", "x_hi", "core", "y")])
     out = attend(place.astype(jnp.int32), span_mask, span_counts, q, pieces)
     back = exchange(out)

time: 127 us -> 127 us (level)
  the two profiles are of different devices: /device:TPU:1 before, /device:TPU:2 now
where the time goes in v6:
time: 127 us
  starting transfers between devices  53.1 us (42%)
  blocking collectives  29.7 us (23%)
  waiting for transfers between devices  29.2 us (23%)
  Pallas kernels  12.4 us (10%)
    all_to_all x1, blocking collectives, exchange(): lax.all_to_all(array, ('y', 'z'), split_axis=0, concat_axis=0, tiled=True)  29.7 us
    all_to_all x1, starting transfers between devices, exchange(): lax.all_to_all(array, ('y', 'z'), split_axis=0, concat_axis=0, tiled=True)  18.9 us
    all_to_all x1, waiting for transfers between devices, exchange(): lax.all_to_all(array, ('y', 'z'), split_axis=0, concat_axis=0, tiled=True)  15.6 us
    pallas_call x1, Pallas kernels, attend(): pl.pallas_call(attend_kernel, out_shape=jax.ShapeDtypeStruct((64, 16, HD)...  10.5 us
    ppermute x3, starting transfers between devices, per_device(): lax.ppermute(kv, x_axes, ring(step))  10.5 us
    ppermute x3, starting transfers between devices, per_device(): part = lax.ppermute(part, 'y', [(a, (a + d) % n_y) for a in range(n_y)])  10.3 us
    ppermute x4, starting transfers between devices, per_device(): pieces += [piece, lax.ppermute(piece, 'core', [(0, 1), (1, 0)])]  8.15 us
    ppermute x3, waiting for transfers between devices, per_device(): lax.ppermute(kv, x_axes, ring(step))  6.72 us
  transfers between devices with their start and end apart: 12, of which 6 were waited for; matrix products, arithmetic and copies ran while one was open for 1% of the time, Pallas kernels for 0%

profile of v6, /device:TPU:2, one launch (start us, length us, event | category | flops | bytes accessed | tf_op | source)
XLA Modules:
  0.0 126.7 jit_solution(5558678382250416721)
XLA Ops:
  0.0 1.9 %shard_map.55 = bf16[64,2,16,128]{3,2,1,0:T(8,128)(2,1)} custom-call(bf16[16,8192]{1,0:T(8,128)(2,1)} %bitcast.28, bf16[16,8192]{1,0:T(8,128)(2,1)} %bitcast.29), custom_call_target="tpu_custom_call" | custom-call | tf_op jit(solution)/shard_map/pallas_call | solution.py:165
  1.9 18.9 %all-to-all-start = ((bf16[64,2,16,128]{3,2,1,0:T(8,128)(2,1)}), bf16[64,2,16,128]{3,2,1,0:T(8,128)(2,1)S(1)}, u32[]{:S(2)}, u32[]{:S(2)}) async-start(bf16[64,2,16,128]{3,2,1,0:T(8,128)(2,1)} %shard_map.55), calls=%async_computation | async-start | bytes 1048576 | tf_op jit(solution)/shard_map/all_to_all | solution.py:188
  20.9 0.2 copy.7
  21.1 4.9 %collective-permute-start.2 = (bf16[16,16,128]{2,1,0:T(8,128)(2,1)S(1)}, bf16[16,16,128]{2,1,0:T(8,128)(2,1)S(1)}, u32[]{:S(2)}, u32[]{:S(2)}) collective-permute-start(bf16[16,16,128]{2,1,0:T(8,128)(2,1)S(1)} %get-tuple-element.10), channel_id=1, source_target_pairs={{0,384},{128,0},{256,128},{384,256},{1,385},{129,1},{257,129},{385... | collective-permute-start | bytes 196616 | tf_op jit(solution)/shard_map/ppermute | solution.py:198
  26.0 2.6 %collective-permute-start.1 = (bf16[16,16,128]{2,1,0:T(8,128)(2,1)S(1)}, bf16[16,16,128]{2,1,0:T(8,128)(2,1)S(1)}, u32[]{:S(2)}, u32[]{:S(2)}) collective-permute-start(bf16[16,16,128]{2,1,0:T(8,128)(2,1)S(1)} %get-tuple-element.11), channel_id=1, source_target_pairs={{0,256},{128,384},{256,0},{384,128},{1,257},{129,385},{257,1},{385... | collective-permute-start | bytes 196616 | tf_op jit(solution)/shard_map/ppermute | solution.py:198
  28.6 2.9 %collective-permute-start = (bf16[16,16,128]{2,1,0:T(8,128)(2,1)S(1)}, bf16[16,16,128]{2,1,0:T(8,128)(2,1)S(1)}, u32[]{:S(2)}, u32[]{:S(2)}) collective-permute-start(bf16[16,16,128]{2,1,0:T(8,128)(2,1)S(1)} %get-tuple-element.12), channel_id=1, source_target_pairs={{0,128},{128,256},{256,384},{384,0},{1,129},{129,257},{257,385},{3... | collective-permute-start | bytes 196616 | tf_op jit(solution)/shard_map/ppermute | solution.py:198
  31.5 0.0 collective-permute-done.2
  31.5 3.2 %collective-permute-done.1 = bf16[16,16,128]{2,1,0:T(8,128)(2,1)S(1)} collective-permute-done((bf16[16,16,128]{2,1,0:T(8,128)(2,1)S(1)}, bf16[16,16,128]{2,1,0:T(8,128)(2,1)S(1)}, u32[]{:S(2)}, u32[]{:S(2)}) %collective-permute-start.1) | collective-permute-done | bytes 65568 | tf_op jit(solution)/shard_map/ppermute | solution.py:198
  34.7 1.4 %collective-permute-done = bf16[16,16,128]{2,1,0:T(8,128)(2,1)S(1)} collective-permute-done((bf16[16,16,128]{2,1,0:T(8,128)(2,1)S(1)}, bf16[16,16,128]{2,1,0:T(8,128)(2,1)S(1)}, u32[]{:S(2)}, u32[]{:S(2)}) %collective-permute-start) | collective-permute-done | bytes 65568 | tf_op jit(solution)/shard_map/ppermute | solution.py:198
  36.1 0.7 pad_maximum_fusion
  36.9 15.6 %all-to-all-done.rest_0_ = bf16[64,2,16,128]{3,2,1,0:T(8,128)(2,1)S(1)} async-done(((bf16[64,2,16,128]{3,2,1,0:T(8,128)(2,1)}), bf16[64,2,16,128]{3,2,1,0:T(8,128)(2,1)S(1)}, u32[]{:S(2)}, u32[]{:S(2)}) %all-to-all-start) | async-done | bytes 524320 | tf_op jit(solution)/shard_map/all_to_all | solution.py:188
  52.5 3.4 %collective-permute-start.8 = (bf16[64,2,16,128]{3,2,1,0:T(8,128)(2,1)S(1)}, bf16[64,2,16,128]{3,2,1,0:T(8,128)(2,1)S(1)}, u32[]{:S(2)}, u32[]{:S(2)}) collective-permute-start(bf16[64,2,16,128]{3,2,1,0:T(8,128)(2,1)S(1)} %all-to-all-done.rest_0_), channel_id=1, source_target_pairs={{0,64},{64,32},{32,96},{96,0},{1,65},{65,33},{33,97},{97,1},{2,66}... | collective-permute-start | bytes 1572872 | tf_op jit(solution)/shard_map/ppermute | solution.py:205
  55.9 3.0 %collective-permute-start.6 = (bf16[64,2,16,128]{3,2,1,0:T(8,128)(2,1)S(1)}, bf16[64,2,16,128]{3,2,1,0:T(8,128)(2,1)S(1)}, u32[]{:S(2)}, u32[]{:S(2)}) collective-permute-start(bf16[64,2,16,128]{3,2,1,0:T(8,128)(2,1)S(1)} %all-to-all-done.rest_0_), channel_id=1, source_target_pairs={{0,32},{64,96},{32,0},{96,64},{1,33},{65,97},{33,1},{97,65},{2,34}... | collective-permute-start | bytes 1572872 | tf_op jit(solution)/shard_map/ppermute | solution.py:205
  58.9 4.1 %collective-permute-start.4 = (bf16[64,2,16,128]{3,2,1,0:T(8,128)(2,1)S(1)}, bf16[64,2,16,128]{3,2,1,0:T(8,128)(2,1)S(1)}, u32[]{:S(2)}, u32[]{:S(2)}) collective-permute-start(bf16[64,2,16,128]{3,2,1,0:T(8,128)(2,1)S(1)} %all-to-all-done.rest_0_), channel_id=1, source_target_pairs={{0,96},{64,0},{32,64},{96,32},{1,97},{65,1},{33,65},{97,33},{2,98}... | collective-permute-start | bytes 1572872 | tf_op jit(solution)/shard_map/ppermute | solution.py:205
  63.0 5.3 %all-to-all-start.1 = ((bf16[16,4,16,128]{3,2,1,0:T(8,128)(2,1)}), bf16[16,4,16,128]{3,2,1,0:T(8,128)(2,1)S(1)}, u32[]{:S(2)}, u32[]{:S(2)}) async-start(bf16[16,4,16,128]{3,2,1,0:T(8,128)(2,1)} %pad_maximum_fusion), calls=%async_computation.1 | async-start | bytes 524288 | tf_op jit(solution)/shard_map/all_to_all | solution.py:201
  68.3 1.9 %collective-permute-start.3 = (bf16[64,2,16,128]{3,2,1,0:T(8,128)(2,1)S(1)}, bf16[64,2,16,128]{3,2,1,0:T(8,128)(2,1)S(1)}, u32[]{:S(2)}, u32[]{:S(2)}) collective-permute-start(bf16[64,2,16,128]{3,2,1,0:T(8,128)(2,1)S(1)} %all-to-all-done.rest_0_), channel_id=1, source_target_pairs={{0,1},{1,0},{2,3},{3,2},{4,5},{5,4},{6,7},{7,6},{8,9},{9,8},{10,11... | collective-permute-start | bytes 1572872 | tf_op jit(solution)/shard_map/ppermute | solution.py:206
  70.3 0.0 collective-permute-done.8.rest_6_
  70.3 2.4 %collective-permute-start.9 = (bf16[64,2,16,128]{3,2,1,0:T(8,128)(2,1)S(1)}, bf16[64,2,16,128]{3,2,1,0:T(8,128)(2,1)S(1)}, u32[]{:S(2)}, u32[]{:S(2)}) collective-permute-start(bf16[64,2,16,128]{3,2,1,0:T(8,128)(2,1)S(1)} %collective-permute-done.8.rest_6_), channel_id=1, source_target_pairs={{0,1},{1,0},{2,3},{3,2},{4,5},{5,4},{6,7},{7,6},{8,9},{9,8},{10,11... | collective-permute-start | bytes 1572872 | tf_op jit(solution)/shard_map/ppermute | solution.py:206
  72.7 1.5 %collective-permute-done.6.rest_4_ = bf16[64,2,16,128]{3,2,1,0:T(8,128)(2,1)S(1)} collective-permute-done((bf16[64,2,16,128]{3,2,1,0:T(8,128)(2,1)S(1)}, bf16[64,2,16,128]{3,2,1,0:T(8,128)(2,1)S(1)}, u32[]{:S(2)}, u32[]{:S(2)}) %collective-permute-start.6) | collective-permute-done | bytes 524320 | tf_op jit(solution)/shard_map/ppermute | solution.py:205
  74.1 1.9 %collective-permute-start.7 = (bf16[64,2,16,128]{3,2,1,0:T(8,128)(2,1)S(1)}, bf16[64,2,16,128]{3,2,1,0:T(8,128)(2,1)}, u32[]{:S(2)}, u32[]{:S(2)}) collective-permute-start(bf16[64,2,16,128]{3,2,1,0:T(8,128)(2,1)S(1)} %collective-permute-done.6.rest_4_), channel_id=1, source_target_pairs={{0,1},{1,0},{2,3},{3,2},{4,5},{5,4},{6,7},{7,6},{8,9},{9,8},{10,11... | collective-permute-start | bytes 1572872 | tf_op jit(solution)/shard_map/ppermute | solution.py:206
  76.1 5.3 %collective-permute-done.4.rest_2_ = bf16[64,2,16,128]{3,2,1,0:T(8,128)(2,1)S(1)} collective-permute-done((bf16[64,2,16,128]{3,2,1,0:T(8,128)(2,1)S(1)}, bf16[64,2,16,128]{3,2,1,0:T(8,128)(2,1)S(1)}, u32[]{:S(2)}, u32[]{:S(2)}) %collective-permute-start.4) | collective-permute-done | bytes 524320 | tf_op jit(solution)/shard_map/ppermute | solution.py:205
  81.3 1.9 %collective-permute-start.5 = (bf16[64,2,16,128]{3,2,1,0:T(8,128)(2,1)S(1)}, bf16[64,2,16,128]{3,2,1,0:T(8,128)(2,1)}, u32[]{:S(2)}, u32[]{:S(2)}) collective-permute-start(bf16[64,2,16,128]{3,2,1,0:T(8,128)(2,1)S(1)} %collective-permute-done.4.rest_2_), channel_id=1, source_target_pairs={{0,1},{1,0},{2,3},{3,2},{4,5},{5,4},{6,7},{7,6},{8,9},{9,8},{10,11... | collective-permute-start | bytes 1572872 | tf_op jit(solution)/shard_map/ppermute | solution.py:206
  83.2 0.0 copy-start
  83.3 0.0 copy-start.1
  83.3 0.1 pad_add_fusion.place
  83.3 0.0 collective-permute-done.3.rest_1_
  83.4 2.2 %all-to-all-done.1.q_ref = bf16[16,4,16,128]{3,2,1,0:T(8,128)(2,1)S(1)} async-done(((bf16[16,4,16,128]{3,2,1,0:T(8,128)(2,1)}), bf16[16,4,16,128]{3,2,1,0:T(8,128)(2,1)S(1)}, u32[]{:S(2)}, u32[]{:S(2)}) %all-to-all-start.1) | async-done | bytes 262176 | tf_op jit(solution)/shard_map/all_to_all | solution.py:201
  85.5 0.0 collective-permute-done.9.rest_7_
  85.6 10.5 %shard_map.56 = bf16[64,16,128]{2,1,0:T(8,128)(2,1)S(1)} custom-call(s32[4]{0:T(128)S(1)} %pad_add_fusion.place, s32[8,8]{1,0:T(8,128)S(1)} %copy-done, s32[8]{0:T(128)S(1)} %copy-done.1, bf16[16,4,16,128]{3,2,1,0:T(8,128)(2,1)S(1)} %all-to-all-done.1.q_ref, bf16[64,2,16,128]{3,2,1,0:T(8,128)(2,1)S(1)} %all-to-all-done.rest_0_, ...), custom_call_target="tpu_custom_call" | custom-call | flops 4294967296 | bytes 5242880 | tf_op jit(solution)/shard_map/pallas_call | solution.py:133
  96.1 29.7 %all_to_all.15 = bf16[64,16,128]{2,1,0:T(8,128)(2,1)S(1)} all-to-all(bf16[64,16,128]{2,1,0:T(8,128)(2,1)S(1)} %shard_map.56), channel_id=1, replica_groups=mesh['y'=4,'x_lo'=2,'x_hi'=2,'z'=16,'core'=2] {'y','z'}, dimensions={0} | all-to-all | bytes 524288 | tf_op jit(solution)/shard_map/all_to_all | solution.py:188
  125.8 0.1 copy.8
  125.8 0.8 reshape.12
  (8 shorter events, 0.1 us)
Async XLA Ops:
  1.9 18.9 %copy-start.2 = (bf16[1,16,8192]{2,1,0:T(8,128)(2,1)S(1)}, bf16[1,16,8192]{2,1,0:T(8,128)(2,1)}, u32[]{:S(2)}) copy-start(bf16[1,16,8192]{2,1,0:T(8,128)(2,1)} %param.5) | copy-start | bytes 786436
  1.9 50.6 %all-to-all-start = ((bf16[64,2,16,128]{3,2,1,0:T(8,128)(2,1)}), bf16[64,2,16,128]{3,2,1,0:T(8,128)(2,1)S(1)}, u32[]{:S(2)}, u32[]{:S(2)}) async-start(bf16[64,2,16,128]{3,2,1,0:T(8,128)(2,1)} %shard_map.55), calls=%async_computation | async-start | bytes 1048576 | tf_op jit(solution)/shard_map/all_to_all | solution.py:188
  21.1 10.3 %collective-permute-start.2 = (bf16[16,16,128]{2,1,0:T(8,128)(2,1)S(1)}, bf16[16,16,128]{2,1,0:T(8,128)(2,1)S(1)}, u32[]{:S(2)}, u32[]{:S(2)}) collective-permute-start(bf16[16,16,128]{2,1,0:T(8,128)(2,1)S(1)} %get-tuple-element.10), channel_id=1, source_target_pairs={{0,384},{128,0},{256,128},{384,256},{1,385},{129,1},{257,129},{385... | collective-permute-start | bytes 196616 | tf_op jit(solution)/shard_map/ppermute | solution.py:198
  26.0 8.7 %collective-permute-start.1 = (bf16[16,16,128]{2,1,0:T(8,128)(2,1)S(1)}, bf16[16,16,128]{2,1,0:T(8,128)(2,1)S(1)}, u32[]{:S(2)}, u32[]{:S(2)}) collective-permute-start(bf16[16,16,128]{2,1,0:T(8,128)(2,1)S(1)} %get-tuple-element.11), channel_id=1, source_target_pairs={{0,256},{128,384},{256,0},{384,128},{1,257},{129,385},{257,1},{385... | collective-permute-start | bytes 196616 | tf_op jit(solution)/shard_map/ppermute | solution.py:198
  28.6 7.5 %collective-permute-start = (bf16[16,16,128]{2,1,0:T(8,128)(2,1)S(1)}, bf16[16,16,128]{2,1,0:T(8,128)(2,1)S(1)}, u32[]{:S(2)}, u32[]{:S(2)}) collective-permute-start(bf16[16,16,128]{2,1,0:T(8,128)(2,1)S(1)} %get-tuple-element.12), channel_id=1, source_target_pairs={{0,128},{128,256},{256,384},{384,0},{1,129},{129,257},{257,385},{3... | collective-permute-start | bytes 196616 | tf_op jit(solution)/shard_map/ppermute | solution.py:198
  52.5 17.8 %collective-permute-start.8 = (bf16[64,2,16,128]{3,2,1,0:T(8,128)(2,1)S(1)}, bf16[64,2,16,128]{3,2,1,0:T(8,128)(2,1)S(1)}, u32[]{:S(2)}, u32[]{:S(2)}) collective-permute-start(bf16[64,2,16,128]{3,2,1,0:T(8,128)(2,1)S(1)} %all-to-all-done.rest_0_), channel_id=1, source_target_pairs={{0,64},{64,32},{32,96},{96,0},{1,65},{65,33},{33,97},{97,1},{2,66}... | collective-permute-start | bytes 1572872 | tf_op jit(solution)/shard_map/ppermute | solution.py:205
  55.9 18.3 %collective-permute-start.6 = (bf16[64,2,16,128]{3,2,1,0:T(8,128)(2,1)S(1)}, bf16[64,2,16,128]{3,2,1,0:T(8,128)(2,1)S(1)}, u32[]{:S(2)}, u32[]{:S(2)}) collective-permute-start(bf16[64,2,16,128]{3,2,1,0:T(8,128)(2,1)S(1)} %all-to-all-done.rest_0_), channel_id=1, source_target_pairs={{0,32},{64,96},{32,0},{96,64},{1,33},{65,97},{33,1},{97,65},{2,34}... | collective-permute-start | bytes 1572872 | tf_op jit(solution)/shard_map/ppermute | solution.py:205
  58.9 22.4 %collective-permute-start.4 = (bf16[64,2,16,128]{3,2,1,0:T(8,128)(2,1)S(1)}, bf16[64,2,16,128]{3,2,1,0:T(8,128)(2,1)S(1)}, u32[]{:S(2)}, u32[]{:S(2)}) collective-permute-start(bf16[64,2,16,128]{3,2,1,0:T(8,128)(2,1)S(1)} %all-to-all-done.rest_0_), channel_id=1, source_target_pairs={{0,96},{64,0},{32,64},{96,32},{1,97},{65,1},{33,65},{97,33},{2,98}... | collective-permute-start | bytes 1572872 | tf_op jit(solution)/shard_map/ppermute | solution.py:205
  63.0 22.6 %all-to-all-start.1 = ((bf16[16,4,16,128]{3,2,1,0:T(8,128)(2,1)}), bf16[16,4,16,128]{3,2,1,0:T(8,128)(2,1)S(1)}, u32[]{:S(2)}, u32[]{:S(2)}) async-start(bf16[16,4,16,128]{3,2,1,0:T(8,128)(2,1)} %pad_maximum_fusion), calls=%async_computation.1 | async-start | bytes 524288 | tf_op jit(solution)/shard_map/all_to_all | solution.py:201
  68.3 15.0 %collective-permute-start.3 = (bf16[64,2,16,128]{3,2,1,0:T(8,128)(2,1)S(1)}, bf16[64,2,16,128]{3,2,1,0:T(8,128)(2,1)S(1)}, u32[]{:S(2)}, u32[]{:S(2)}) collective-permute-start(bf16[64,2,16,128]{3,2,1,0:T(8,128)(2,1)S(1)} %all-to-all-done.rest_0_), channel_id=1, source_target_pairs={{0,1},{1,0},{2,3},{3,2},{4,5},{5,4},{6,7},{7,6},{8,9},{9,8},{10,11... | collective-permute-start | bytes 1572872 | tf_op jit(solution)/shard_map/ppermute | solution.py:206
  70.3 15.3 %collective-permute-start.9 = (bf16[64,2,16,128]{3,2,1,0:T(8,128)(2,1)S(1)}, bf16[64,2,16,128]{3,2,1,0:T(8,128)(2,1)S(1)}, u32[]{:S(2)}, u32[]{:S(2)}) collective-permute-start(bf16[64,2,16,128]{3,2,1,0:T(8,128)(2,1)S(1)} %collective-permute-done.8.rest_6_), channel_id=1, source_target_pairs={{0,1},{1,0},{2,3},{3,2},{4,5},{5,4},{6,7},{7,6},{8,9},{9,8},{10,11... | collective-permute-start | bytes 1572872 | tf_op jit(solution)/shard_map/ppermute | solution.py:206
  74.1 11.4 %collective-permute-start.7 = (bf16[64,2,16,128]{3,2,1,0:T(8,128)(2,1)S(1)}, bf16[64,2,16,128]{3,2,1,0:T(8,128)(2,1)}, u32[]{:S(2)}, u32[]{:S(2)}) collective-permute-start(bf16[64,2,16,128]{3,2,1,0:T(8,128)(2,1)S(1)} %collective-permute-done.6.rest_4_), channel_id=1, source_target_pairs={{0,1},{1,0},{2,3},{3,2},{4,5},{5,4},{6,7},{7,6},{8,9},{9,8},{10,11... | collective-permute-start | bytes 1572872 | tf_op jit(solution)/shard_map/ppermute | solution.py:206
  81.3 4.2 %collective-permute-start.5 = (bf16[64,2,16,128]{3,2,1,0:T(8,128)(2,1)S(1)}, bf16[64,2,16,128]{3,2,1,0:T(8,128)(2,1)}, u32[]{:S(2)}, u32[]{:S(2)}) collective-permute-start(bf16[64,2,16,128]{3,2,1,0:T(8,128)(2,1)S(1)} %collective-permute-done.4.rest_2_), channel_id=1, source_target_pairs={{0,1},{1,0},{2,3},{3,2},{4,5},{5,4},{6,7},{7,6},{8,9},{9,8},{10,11... | collective-permute-start | bytes 1572872 | tf_op jit(solution)/shard_map/ppermute | solution.py:206
  83.2 2.3 %copy-start = (s32[8,8]{1,0:T(8,128)S(1)}, s32[8,8]{1,0:T(8,128)}, u32[]{:S(2)}) copy-start(s32[8,8]{1,0:T(8,128)} %mask.1) | copy-start | bytes 772
  83.3 2.3 %copy-start.1 = (s32[8]{0:T(128)S(1)}, s32[8]{0:T(128)}, u32[]{:S(2)}) copy-start(s32[8]{0:T(128)} %counts.1) | copy-start | bytes 100

commit v7 on v6

v7 whole, which is shorter than its diff:
```python
import jax
import jax.numpy as jnp
from jax import lax
from jax.experimental import pallas as pl
from jax.experimental.pallas import tpu as pltpu
from jax.sharding import Mesh, PartitionSpec as P

HD = 128
LOW = -1e30
LOG2E = 1.4426950408889634
UNROLL = 1


def attend_kernel(place, mask, counts, q_ref, *rest):
    pieces = rest[:8]
    out_ref, k_buf, v_buf = rest[8:11]
    scores, row_tops = rest[11 : 11 + 2 * UNROLL], rest[11 + 2 * UNROLL : 11 + 4 * UNROLL]
    acc_ref, top_ref, total_ref, todo, sems = rest[11 + 4 * UNROLL :]
    x, y, core = place[0], place[1], place[2]
    copies = {}
    for d in range(4):
        for part, buf in enumerate((k_buf, v_buf)):
            for e in range(2):
                copies[d, e, part] = pltpu.make_async_copy(
                    pieces[2 * d + e].at[:, :, :, part], buf.at[d, e], sems.at[2 * d + e, part]
                )
    for d in range(4):
        for part in range(2):
            for e in range(2):
                copies[d, e, part].start()

    def wait(d, part):
        for e in range(2):
            copies[d, e, part].wait()

    def list_block(i, n):
        d, rel, x_lo = i // 4, i // 2 % 2, i % 2
        todo[n] = i
        return n + mask[y * 2 + (x + rel) % 2, (y + d) % 4 * 2 + x_lo]

    first = lax.fori_loop(0, 4, list_block, 0)
    count = lax.fori_loop(4, 16, list_block, first)

    acc_ref[...] = jnp.zeros_like(acc_ref)
    top_ref[...] = jnp.full_like(top_ref, LOW)
    total_ref[...] = jnp.zeros_like(total_ref)
    scale = LOG2E / HD**0.5
    lane = lax.broadcasted_iota(jnp.int32, (1, 128), 1)
    slot_at = lane // 16 % 2 * 512 + lane // 32 * 32 + lane % 16

    def score(n, to):
        i = todo[jnp.minimum(n, count - 1)]
        d, rel, x_lo = i // 4, i // 2 % 2, i % 2
        live = counts[(y + d) % 4 * 2 + x_lo]
        q = q_ref[:, :, rel].reshape(512, HD)
        k = k_buf[d, :, :, :, x_lo].reshape(1024, HD)
        s = lax.dot_general(q, k, (((1,), (1,)), ((), ())), preferred_element_type=jnp.float32)
        top = None
        for g in range(8):
            a = s[:, g * 128 : (g + 1) * 128]
            if g % 4 >= 2:
                slot = slot_at + (g % 4 * 128 + (core + g // 4) % 2 * 16)
                a = jnp.where(slot < live, a, LOW)
            scores[to][:, g * 128 : (g + 1) * 128] = a
            top = a if top is None else jnp.maximum(top, a)
        row_tops[to][...] = jnp.broadcast_to(jnp.max(top, axis=1, keepdims=True), (512, 128))

    def mix(n, at):
        i = todo[jnp.minimum(n, count - 1)]
        d, x_lo = i // 4, i % 2
        shift = row_tops[at][...] * scale
        total, weights = None, []
        for g in range(8):
            w = jnp.exp2(scores[at][:, g * 128 : (g + 1) * 128] * scale - shift)
            weights.append(w.astype(jnp.bfloat16))
            total = w if total is None else total + w
        v = v_buf[d, :, :, :, x_lo].reshape(1024, HD)
        acc = jnp.dot(jnp.concatenate(weights, axis=1), v, preferred_element_type=jnp.float32)
        return row_tops[at][...], total, acc

    def merge(n, state):
        top, total, acc = state
        rel = todo[jnp.minimum(n, count - 1)] // 2 % 2
        if UNROLL > 1:
            top = jnp.where(n < count, top, LOW)
        old = top_ref[rel]
        new = jnp.maximum(old, top)
        keep, add = jnp.exp2((old - new) * scale), jnp.exp2((top - new) * scale)
        total_ref[rel] = total_ref[rel] * keep + total * add
        acc_ref[rel] = acc_ref[rel] * keep + acc * add
        top_ref[rel] = new

    def step(n, at):
        @pl.when((n + 2 * UNROLL > first) & (n + UNROLL <= first))
        def _():
            for d in range(1, 4):
                wait(d, 0)
                wait(d, 1)

        for u in range(UNROLL):
            score(n + UNROLL + u, (1 - at) * UNROLL + u)
        states = [mix(n + u, at * UNROLL + u) for u in range(UNROLL)]
        for u in range(UNROLL):
            merge(n + u, states[u])

    wait(0, 0)
    for u in range(UNROLL):
        score(u, u)
    wait(0, 1)

    def pair(m, _):
        step(2 * UNROLL * m, 0)

        @pl.when(2 * UNROLL * m + UNROLL < count)
        def _():
            step(2 * UNROLL * m + UNROLL, 1)

        return 0

    lax.fori_loop(0, (count + 2 * UNROLL - 1) // (2 * UNROLL), pair, 0)
    for rel in range(2):
        total = jnp.sum(total_ref[rel], axis=1, keepdims=True)
        result = (acc_ref[rel] / total).astype(jnp.bfloat16).reshape(16, 2, 16, HD)
        for far in range(2):
            out_ref[:, (x + 4 - rel - 2 * far) % 4] = result[:, far]


def attend(place, mask, counts, q, pieces):
    smem = pl.BlockSpec(memory_space=pltpu.SMEM)
    vmem = pl.BlockSpec(memory_space=pltpu.VMEM)
    return pl.pallas_call(
        attend_kernel,
        out_shape=jax.ShapeDtypeStruct((16, 4, 16, HD), jnp.bfloat16),
        in_specs=[smem, smem, smem, vmem] + [pl.BlockSpec(memory_space=pl.ANY)] * 8,
        out_specs=vmem,
        scratch_shapes=[
            pltpu.VMEM((4, 2, 16, 2, 2, 16, HD), jnp.bfloat16),
            pltpu.VMEM((4, 2, 16, 2, 2, 16, HD), jnp.bfloat16),
            *[pltpu.VMEM((512, 1024), jnp.float32)] * (2 * UNROLL),
            *[pltpu.VMEM((512, HD), jnp.float32)] * (2 * UNROLL),
            pltpu.VMEM((2, 512, HD), jnp.float32),
            pltpu.VMEM((2, 512, HD), jnp.float32),
            pltpu.VMEM((2, 512, HD), jnp.float32),
            pltpu.SMEM((17,), jnp.int32),
            pltpu.SemaphoreType.DMA((8, 2)),
        ],
        compiler_params=pltpu.CompilerParams(vmem_limit_bytes=40 * 1024 * 1024),
        cost_estimate=pl.CostEstimate(
            flops=4 * 1024 * 8192 * HD, bytes_accessed=5 << 20, transcendentals=1024 * 8192
        ),
    )(place, mask, counts, q, *pieces)


def pack_kernel(k_ref, v_ref, out_ref):
    for head in range(out_ref.shape[0]):
        at = head * HD
        out_ref[head, 0] = k_ref[:, at : at + HD]
        out_ref[head, 1] = v_ref[:, at : at + HD]


def pack(keys, values):
    rows, width = keys.shape
    return pl.pallas_call(
        pack_kernel,
        out_shape=jax.ShapeDtypeStruct((width // HD, 2, rows, HD), keys.dtype),
        in_specs=[pl.BlockSpec(memory_space=pltpu.VMEM)] * 2,
        out_specs=pl.BlockSpec(memory_space=pltpu.VMEM),
    )(keys, values)


def ring(step):
    def index(x):
        return (x % 2) * 2 + x // 2

    return [(index(x), index((x + step) % 4)) for x in range(4)]


def per_device(queries, keys, values, span_mask, span_counts):
    tok_rows, width = queries.shape[1], queries.shape[2]
    heads = width // HD

    def by_head(array):
        return array.reshape(tok_rows, heads, HD).transpose(1, 0, 2)

    def exchange(array):
        return lax.all_to_all(
            array, ("z", "x_hi", "x_lo"), split_axis=0, concat_axis=0, tiled=True
        )

    kv = exchange(pack(keys[0], values[0]))
    n_x, n_y = 4, lax.axis_size("y")
    x = lax.axis_index("x_hi") * 2 + lax.axis_index("x_lo")
    by_group = by_head(queries).reshape(heads // n_x, n_x, tok_rows, HD)
    parts = []
    for d in range(n_x):
        part = lax.dynamic_index_in_dim(by_group, (x + d) % n_x, 1, keepdims=False)
        if d > 0:
            part = lax.ppermute(part, ("x_lo", "x_hi"), ring(d))
        parts.append(part)
    q_in, kv = lax.optimization_barrier((jnp.stack(parts, axis=1), kv))
    q = lax.all_to_all(q_in, "z", split_axis=0, concat_axis=0, tiled=True)

    near = [lax.ppermute(kv, "y", [(a, (a - d) % n_y) for a in range(n_y)]) for d in (1, 3, 2)]
    pieces = []
    for piece in (kv, near[0], near[2], near[1]):
        pieces += [piece, lax.ppermute(piece, "core", [(0, 1), (1, 0)])]
    place = jnp.stack([x, lax.axis_index("y"), lax.axis_index("core")])
    out = attend(
        place.astype(jnp.int32),
        span_mask,
        span_counts,
        q.reshape(16, 2, 2, tok_rows, HD),
        [piece.reshape(16, 2, 2, 2, tok_rows, HD) for piece in pieces],
    )
    back = exchange(out.reshape(heads, tok_rows, HD))
    return back.transpose(1, 0, 2).reshape(1, tok_rows, width)


def solution(mesh):
    fine = Mesh(mesh.devices.reshape(4, 2, 2, 16, 2), ("y", "x_lo", "x_hi", "z", "core"))
    split = P(("y", "x_lo"), ("x_hi", "z", "core"), None)
    return jax.shard_map(
        per_device,
        mesh=fine,
        in_specs=(split, split, split, P(), P()),
        out_specs=split,
        check_vma=False,
    )
```

time: 127 us -> 129 us (1.016)
  the two profiles are of different devices: /device:TPU:2 before, /device:TPU:16 now
where the time goes in v7:
time: 129 us; the launch traced here: 128 us
  starting transfers between devices  49.9 us (39%)
  waiting for transfers between devices  32.3 us (25%)
  blocking collectives  30.7 us (24%)
  Pallas kernels  12.1 us (9%)
  local copies, waits for them, and re-layouts  1.84 us (1%)
    all_to_all x1, blocking collectives, exchange(): lax.all_to_all(array, ('z', 'x_hi', 'x_lo'), split_axis=0, concat_axis=0,...  30.7 us
    all_to_all x1, starting transfers between devices, exchange(): lax.all_to_all(array, ('z', 'x_hi', 'x_lo'), split_axis=0, concat_axis=0,...  18.7 us
    all_to_all x1, waiting for transfers between devices, exchange(): lax.all_to_all(array, ('z', 'x_hi', 'x_lo'), split_axis=0, concat_axis=0,...  16.5 us
    ppermute x3, starting transfers between devices, per_device(): part = lax.ppermute(part, ('x_lo', 'x_hi'), ring(d))  10.2 us
    pallas_call x1, Pallas kernels, attend(): pl.pallas_call(attend_kernel, out_shape=jax.ShapeDtypeStruct((16, 4, 16,...  10.1 us
    ppermute x3, waiting for transfers between devices, per_device(): lax.ppermute(kv, 'y', [(a, (a - d) % n_y) for a in range(n_y)])  8.92 us
    ppermute x3, starting transfers between devices, per_device(): lax.ppermute(kv, 'y', [(a, (a - d) % n_y) for a in range(n_y)])  8.68 us
    ppermute x4, starting transfers between devices, per_device(): pieces += [piece, lax.ppermute(piece, 'core', [(0, 1), (1, 0)])]  8.16 us
  transfers between devices with their start and end apart: 12, of which 5 were waited for; matrix products, arithmetic and copies ran while one was open for 1% of the time, Pallas kernels for 0%

profile of v7, /device:TPU:16, one launch (start us, length us, event | category | flops | bytes accessed | tf_op | source)
XLA Modules:
  0.0 127.9 jit_solution(14941675553821924965)
XLA Ops:
  0.0 1.9 %shard_map.55 = bf16[64,2,16,128]{3,2,1,0:T(8,128)(2,1)} custom-call(bf16[16,8192]{1,0:T(8,128)(2,1)} %bitcast.43, bf16[16,8192]{1,0:T(8,128)(2,1)} %bitcast.44), custom_call_target="tpu_custom_call" | custom-call | tf_op jit(solution)/shard_map/pallas_call | solution.py:163
  1.9 18.7 %all-to-all-start = ((bf16[64,2,16,128]{3,2,1,0:T(8,128)(2,1)}), bf16[64,2,16,128]{3,2,1,0:T(8,128)(2,1)S(1)}, u32[]{:S(2)}, u32[]{:S(2)}) async-start(bf16[64,2,16,128]{3,2,1,0:T(8,128)(2,1)} %shard_map.55), calls=%async_computation | async-start | bytes 1048576 | tf_op jit(solution)/shard_map/all_to_all | solution.py:186
  20.7 0.2 copy.6
  21.0 4.7 %collective-permute-start.2 = (bf16[16,16,128]{2,1,0:T(8,128)(2,1)S(1)}, bf16[16,16,128]{2,1,0:T(8,128)(2,1)S(1)}, u32[]{:S(2)}, u32[]{:S(2)}) collective-permute-start(bf16[16,16,128]{2,1,0:T(8,128)(2,1)S(1)} %get-tuple-element.10), channel_id=1, source_target_pairs={{0,96},{64,0},{32,64},{96,32},{1,97},{65,1},{33,65},{97,33},{2,98}... | collective-permute-start | bytes 196616 | tf_op jit(solution)/shard_map/ppermute | solution.py:198
  25.7 2.8 %collective-permute-start.1 = (bf16[16,16,128]{2,1,0:T(8,128)(2,1)S(1)}, bf16[16,16,128]{2,1,0:T(8,128)(2,1)S(1)}, u32[]{:S(2)}, u32[]{:S(2)}) collective-permute-start(bf16[16,16,128]{2,1,0:T(8,128)(2,1)S(1)} %get-tuple-element.11), channel_id=1, source_target_pairs={{0,32},{64,96},{32,0},{96,64},{1,33},{65,97},{33,1},{97,65},{2,34}... | collective-permute-start | bytes 196616 | tf_op jit(solution)/shard_map/ppermute | solution.py:198
  28.5 2.8 %collective-permute-start = (bf16[16,16,128]{2,1,0:T(8,128)(2,1)S(1)}, bf16[16,16,128]{2,1,0:T(8,128)(2,1)S(1)}, u32[]{:S(2)}, u32[]{:S(2)}) collective-permute-start(bf16[16,16,128]{2,1,0:T(8,128)(2,1)S(1)} %get-tuple-element.12), channel_id=1, source_target_pairs={{0,64},{64,32},{32,96},{96,0},{1,65},{65,33},{33,97},{97,1},{2,66}... | collective-permute-start | bytes 196616 | tf_op jit(solution)/shard_map/ppermute | solution.py:198
  31.2 0.0 collective-permute-done.2
  31.2 3.4 %collective-permute-done.1 = bf16[16,16,128]{2,1,0:T(8,128)(2,1)S(1)} collective-permute-done((bf16[16,16,128]{2,1,0:T(8,128)(2,1)S(1)}, bf16[16,16,128]{2,1,0:T(8,128)(2,1)S(1)}, u32[]{:S(2)}, u32[]{:S(2)}) %collective-permute-start.1) | collective-permute-done | bytes 65568 | tf_op jit(solution)/shard_map/ppermute | solution.py:198
  34.6 1.6 %collective-permute-done = bf16[16,16,128]{2,1,0:T(8,128)(2,1)S(1)} collective-permute-done((bf16[16,16,128]{2,1,0:T(8,128)(2,1)S(1)}, bf16[16,16,128]{2,1,0:T(8,128)(2,1)S(1)}, u32[]{:S(2)}, u32[]{:S(2)}) %collective-permute-start) | collective-permute-done | bytes 65568 | tf_op jit(solution)/shard_map/ppermute | solution.py:198
  36.2 0.7 pad_maximum_fusion
  37.0 16.5 %all-to-all-done = bf16[64,2,16,128]{3,2,1,0:T(8,128)(2,1)S(1)} async-done(((bf16[64,2,16,128]{3,2,1,0:T(8,128)(2,1)}), bf16[64,2,16,128]{3,2,1,0:T(8,128)(2,1)S(1)}, u32[]{:S(2)}, u32[]{:S(2)}) %all-to-all-start) | async-done | bytes 524320 | tf_op jit(solution)/shard_map/all_to_all | solution.py:186
  53.4 3.2 %collective-permute-start.8 = (bf16[64,2,16,128]{3,2,1,0:T(8,128)(2,1)S(1)}, bf16[64,2,16,128]{3,2,1,0:T(8,128)(2,1)S(1)}, u32[]{:S(2)}, u32[]{:S(2)}) collective-permute-start(bf16[64,2,16,128]{3,2,1,0:T(8,128)(2,1)S(1)} %all-to-all-done), channel_id=1, source_target_pairs={{0,128},{128,256},{256,384},{384,0},{1,129},{129,257},{257,385},{3... | collective-permute-start | bytes 1572872 | tf_op jit(solution)/shard_map/ppermute | solution.py:203
  56.6 2.5 %collective-permute-start.6 = (bf16[64,2,16,128]{3,2,1,0:T(8,128)(2,1)S(1)}, bf16[64,2,16,128]{3,2,1,0:T(8,128)(2,1)S(1)}, u32[]{:S(2)}, u32[]{:S(2)}) collective-permute-start(bf16[64,2,16,128]{3,2,1,0:T(8,128)(2,1)S(1)} %all-to-all-done), channel_id=1, source_target_pairs={{0,256},{128,384},{256,0},{384,128},{1,257},{129,385},{257,1},{385... | collective-permute-start | bytes 1572872 | tf_op jit(solution)/shard_map/ppermute | solution.py:203
  59.2 3.0 %collective-permute-start.4 = (bf16[64,2,16,128]{3,2,1,0:T(8,128)(2,1)S(1)}, bf16[64,2,16,128]{3,2,1,0:T(8,128)(2,1)S(1)}, u32[]{:S(2)}, u32[]{:S(2)}) collective-permute-start(bf16[64,2,16,128]{3,2,1,0:T(8,128)(2,1)S(1)} %all-to-all-done), channel_id=1, source_target_pairs={{0,384},{128,0},{256,128},{384,256},{1,385},{129,1},{257,129},{385... | collective-permute-start | bytes 1572872 | tf_op jit(solution)/shard_map/ppermute | solution.py:203
  62.1 4.1 %all-to-all-start.1 = ((bf16[16,4,16,128]{3,2,1,0:T(8,128)(2,1)}), bf16[16,4,16,128]{3,2,1,0:T(8,128)(2,1)S(1)}, u32[]{:S(2)}, u32[]{:S(2)}) async-start(bf16[16,4,16,128]{3,2,1,0:T(8,128)(2,1)} %pad_maximum_fusion), calls=%async_computation.1 | async-start | bytes 524288 | tf_op jit(solution)/shard_map/all_to_all | solution.py:201
  66.3 1.9 %collective-permute-start.3 = (bf16[64,2,16,128]{3,2,1,0:T(8,128)(2,1)S(1)}, bf16[64,2,16,128]{3,2,1,0:T(8,128)(2,1)S(1)}, u32[]{:S(2)}, u32[]{:S(2)}) collective-permute-start(bf16[64,2,16,128]{3,2,1,0:T(8,128)(2,1)S(1)} %all-to-all-done), channel_id=1, source_target_pairs={{0,1},{1,0},{2,3},{3,2},{4,5},{5,4},{6,7},{7,6},{8,9},{9,8},{10,11... | collective-permute-start | bytes 1572872 | tf_op jit(solution)/shard_map/ppermute | solution.py:206
  68.2 8.9 %collective-permute-done.8 = bf16[64,2,16,128]{3,2,1,0:T(8,128)(2,1)S(1)} collective-permute-done((bf16[64,2,16,128]{3,2,1,0:T(8,128)(2,1)S(1)}, bf16[64,2,16,128]{3,2,1,0:T(8,128)(2,1)S(1)}, u32[]{:S(2)}, u32[]{:S(2)}) %collective-permute-start.8) | collective-permute-done | bytes 524320 | tf_op jit(solution)/shard_map/ppermute | solution.py:203
  77.1 1.9 %collective-permute-start.9 = (bf16[64,2,16,128]{3,2,1,0:T(8,128)(2,1)S(1)}, bf16[64,2,16,128]{3,2,1,0:T(8,128)(2,1)S(1)}, u32[]{:S(2)}, u32[]{:S(2)}) collective-permute-start(bf16[64,2,16,128]{3,2,1,0:T(8,128)(2,1)S(1)} %collective-permute-done.8), channel_id=1, source_target_pairs={{0,1},{1,0},{2,3},{3,2},{4,5},{5,4},{6,7},{7,6},{8,9},{9,8},{10,11... | collective-permute-start | bytes 1572872 | tf_op jit(solution)/shard_map/ppermute | solution.py:206
  79.0 0.0 collective-permute-done.6
  79.1 2.4 %collective-permute-start.7 = (bf16[64,2,16,128]{3,2,1,0:T(8,128)(2,1)S(1)}, bf16[64,2,16,128]{3,2,1,0:T(8,128)(2,1)}, u32[]{:S(2)}, u32[]{:S(2)}) collective-permute-start(bf16[64,2,16,128]{3,2,1,0:T(8,128)(2,1)S(1)} %collective-permute-done.6), channel_id=1, source_target_pairs={{0,1},{1,0},{2,3},{3,2},{4,5},{5,4},{6,7},{7,6},{8,9},{9,8},{10,11... | collective-permute-start | bytes 1572872 | tf_op jit(solution)/shard_map/ppermute | solution.py:206
  81.5 0.0 collective-permute-done.4
  81.5 1.9 %collective-permute-start.5 = (bf16[64,2,16,128]{3,2,1,0:T(8,128)(2,1)S(1)}, bf16[64,2,16,128]{3,2,1,0:T(8,128)(2,1)}, u32[]{:S(2)}, u32[]{:S(2)}) collective-permute-start(bf16[64,2,16,128]{3,2,1,0:T(8,128)(2,1)S(1)} %collective-permute-done.4), channel_id=1, source_target_pairs={{0,1},{1,0},{2,3},{3,2},{4,5},{5,4},{6,7},{7,6},{8,9},{9,8},{10,11... | collective-permute-start | bytes 1572872 | tf_op jit(solution)/shard_map/ppermute | solution.py:206
  83.4 0.1 pad_add_fusion.place
  83.5 0.0 all-to-all-done.1
  83.5 0.0 collective-permute-done.9
  83.5 0.0 collective-permute-done.7
  83.5 1.9 %collective-permute-done.5 = bf16[64,2,16,128]{3,2,1,0:T(8,128)(2,1)} collective-permute-done((bf16[64,2,16,128]{3,2,1,0:T(8,128)(2,1)S(1)}, bf16[64,2,16,128]{3,2,1,0:T(8,128)(2,1)}, u32[]{:S(2)}, u32[]{:S(2)}) %collective-permute-start.5) | collective-permute-done | bytes 524320 | tf_op jit(solution)/shard_map/ppermute | solution.py:206
  85.4 0.7 copy-done
  86.1 10.1 %shard_map.56 = bf16[16,4,16,128]{3,2,1,0:T(8,128)(2,1)S(1)} custom-call(s32[3]{0:T(128)S(1)} %pad_add_fusion.place, s32[8,8]{1,0:T(8,128)S(1)} %copy-done, s32[8]{0:T(128)S(1)} %copy-done.1, bf16[16,2,2,16,128]{4,3,2,1,0:T(8,128)(2,1)S(1)} %bitcast.32, bf16[16,2,2,2,16,128]{5,4,3,2,1,0:T(8,128)(2,1)S(1)} %bitcast.31, ...), custom_call_target="tpu_custom_call" | custom-call | flops 4294967296 | bytes 5242880 | tf_op jit(solution)/shard_map/pallas_call | solution.py:131
  96.3 30.7 %all_to_all.15 = bf16[64,16,128]{2,1,0:T(8,128)(2,1)S(1)} all-to-all(bf16[64,16,128]{2,1,0:T(8,128)(2,1)S(1)} %bitcast.33), channel_id=1, replica_groups=mesh['y'=4,'x_lo'=2,'x_hi'=2,'z'=16,'core'=2] {'z','x_hi','x_lo'}, dimensions={0} | all-to-all | bytes 524288 | tf_op jit(solution)/shard_map/all_to_all | solution.py:186
  127.0 0.1 copy.7
  127.0 0.8 reshape.51
  (8 shorter events, 0.1 us)
Async XLA Ops:
  1.9 18.8 %copy-start.2 = (bf16[1,16,8192]{2,1,0:T(8,128)(2,1)S(1)}, bf16[1,16,8192]{2,1,0:T(8,128)(2,1)}, u32[]{:S(2)}) copy-start(bf16[1,16,8192]{2,1,0:T(8,128)(2,1)} %param.5) | copy-start | bytes 786436
  1.9 51.5 %all-to-all-start = ((bf16[64,2,16,128]{3,2,1,0:T(8,128)(2,1)}), bf16[64,2,16,128]{3,2,1,0:T(8,128)(2,1)S(1)}, u32[]{:S(2)}, u32[]{:S(2)}) async-start(bf16[64,2,16,128]{3,2,1,0:T(8,128)(2,1)} %shard_map.55), calls=%async_computation | async-start | bytes 1048576 | tf_op jit(solution)/shard_map/all_to_all | solution.py:186
  21.0 10.2 %collective-permute-start.2 = (bf16[16,16,128]{2,1,0:T(8,128)(2,1)S(1)}, bf16[16,16,128]{2,1,0:T(8,128)(2,1)S(1)}, u32[]{:S(2)}, u32[]{:S(2)}) collective-permute-start(bf16[16,16,128]{2,1,0:T(8,128)(2,1)S(1)} %get-tuple-element.10), channel_id=1, source_target_pairs={{0,96},{64,0},{32,64},{96,32},{1,97},{65,1},{33,65},{97,33},{2,98}... | collective-permute-start | bytes 196616 | tf_op jit(solution)/shard_map/ppermute | solution.py:198
  25.7 8.9 %collective-permute-start.1 = (bf16[16,16,128]{2,1,0:T(8,128)(2,1)S(1)}, bf16[16,16,128]{2,1,0:T(8,128)(2,1)S(1)}, u32[]{:S(2)}, u32[]{:S(2)}) collective-permute-start(bf16[16,16,128]{2,1,0:T(8,128)(2,1)S(1)} %get-tuple-element.11), channel_id=1, source_target_pairs={{0,32},{64,96},{32,0},{96,64},{1,33},{65,97},{33,1},{97,65},{2,34}... | collective-permute-start | bytes 196616 | tf_op jit(solution)/shard_map/ppermute | solution.py:198
  28.5 7.8 %collective-permute-start = (bf16[16,16,128]{2,1,0:T(8,128)(2,1)S(1)}, bf16[16,16,128]{2,1,0:T(8,128)(2,1)S(1)}, u32[]{:S(2)}, u32[]{:S(2)}) collective-permute-start(bf16[16,16,128]{2,1,0:T(8,128)(2,1)S(1)} %get-tuple-element.12), channel_id=1, source_target_pairs={{0,64},{64,32},{32,96},{96,0},{1,65},{65,33},{33,97},{97,1},{2,66}... | collective-permute-start | bytes 196616 | tf_op jit(solution)/shard_map/ppermute | solution.py:198
  53.4 23.7 %collective-permute-start.8 = (bf16[64,2,16,128]{3,2,1,0:T(8,128)(2,1)S(1)}, bf16[64,2,16,128]{3,2,1,0:T(8,128)(2,1)S(1)}, u32[]{:S(2)}, u32[]{:S(2)}) collective-permute-start(bf16[64,2,16,128]{3,2,1,0:T(8,128)(2,1)S(1)} %all-to-all-done), channel_id=1, source_target_pairs={{0,128},{128,256},{256,384},{384,0},{1,129},{129,257},{257,385},{3... | collective-permute-start | bytes 1572872 | tf_op jit(solution)/shard_map/ppermute | solution.py:203
  56.6 22.4 %collective-permute-start.6 = (bf16[64,2,16,128]{3,2,1,0:T(8,128)(2,1)S(1)}, bf16[64,2,16,128]{3,2,1,0:T(8,128)(2,1)S(1)}, u32[]{:S(2)}, u32[]{:S(2)}) collective-permute-start(bf16[64,2,16,128]{3,2,1,0:T(8,128)(2,1)S(1)} %all-to-all-done), channel_id=1, source_target_pairs={{0,256},{128,384},{256,0},{384,128},{1,257},{129,385},{257,1},{385... | collective-permute-start | bytes 1572872 | tf_op jit(solution)/shard_map/ppermute | solution.py:203
  59.2 22.3 %collective-permute-start.4 = (bf16[64,2,16,128]{3,2,1,0:T(8,128)(2,1)S(1)}, bf16[64,2,16,128]{3,2,1,0:T(8,128)(2,1)S(1)}, u32[]{:S(2)}, u32[]{:S(2)}) collective-permute-start(bf16[64,2,16,128]{3,2,1,0:T(8,128)(2,1)S(1)} %all-to-all-done), channel_id=1, source_target_pairs={{0,384},{128,0},{256,128},{384,256},{1,385},{129,1},{257,129},{385... | collective-permute-start | bytes 1572872 | tf_op jit(solution)/shard_map/ppermute | solution.py:203
  62.1 21.4 %all-to-all-start.1 = ((bf16[16,4,16,128]{3,2,1,0:T(8,128)(2,1)}), bf16[16,4,16,128]{3,2,1,0:T(8,128)(2,1)S(1)}, u32[]{:S(2)}, u32[]{:S(2)}) async-start(bf16[16,4,16,128]{3,2,1,0:T(8,128)(2,1)} %pad_maximum_fusion), calls=%async_computation.1 | async-start | bytes 524288 | tf_op jit(solution)/shard_map/all_to_all | solution.py:201
  66.3 17.2 %collective-permute-start.3 = (bf16[64,2,16,128]{3,2,1,0:T(8,128)(2,1)S(1)}, bf16[64,2,16,128]{3,2,1,0:T(8,128)(2,1)S(1)}, u32[]{:S(2)}, u32[]{:S(2)}) collective-permute-start(bf16[64,2,16,128]{3,2,1,0:T(8,128)(2,1)S(1)} %all-to-all-done), channel_id=1, source_target_pairs={{0,1},{1,0},{2,3},{3,2},{4,5},{5,4},{6,7},{7,6},{8,9},{9,8},{10,11... | collective-permute-start | bytes 1572872 | tf_op jit(solution)/shard_map/ppermute | solution.py:206
  77.1 6.4 %collective-permute-start.9 = (bf16[64,2,16,128]{3,2,1,0:T(8,128)(2,1)S(1)}, bf16[64,2,16,128]{3,2,1,0:T(8,128)(2,1)S(1)}, u32[]{:S(2)}, u32[]{:S(2)}) collective-permute-start(bf16[64,2,16,128]{3,2,1,0:T(8,128)(2,1)S(1)} %collective-permute-done.8), channel_id=1, source_target_pairs={{0,1},{1,0},{2,3},{3,2},{4,5},{5,4},{6,7},{7,6},{8,9},{9,8},{10,11... | collective-permute-start | bytes 1572872 | tf_op jit(solution)/shard_map/ppermute | solution.py:206
  79.1 4.5 %collective-permute-start.7 = (bf16[64,2,16,128]{3,2,1,0:T(8,128)(2,1)S(1)}, bf16[64,2,16,128]{3,2,1,0:T(8,128)(2,1)}, u32[]{:S(2)}, u32[]{:S(2)}) collective-permute-start(bf16[64,2,16,128]{3,2,1,0:T(8,128)(2,1)S(1)} %collective-permute-done.6), channel_id=1, source_target_pairs={{0,1},{1,0},{2,3},{3,2},{4,5},{5,4},{6,7},{7,6},{8,9},{9,8},{10,11... | collective-permute-start | bytes 1572872 | tf_op jit(solution)/shard_map/ppermute | solution.py:206
  81.5 3.9 %collective-permute-start.5 = (bf16[64,2,16,128]{3,2,1,0:T(8,128)(2,1)S(1)}, bf16[64,2,16,128]{3,2,1,0:T(8,128)(2,1)}, u32[]{:S(2)}, u32[]{:S(2)}) collective-permute-start(bf16[64,2,16,128]{3,2,1,0:T(8,128)(2,1)S(1)} %collective-permute-done.4), channel_id=1, source_target_pairs={{0,1},{1,0},{2,3},{3,2},{4,5},{5,4},{6,7},{7,6},{8,9},{9,8},{10,11... | collective-permute-start | bytes 1572872 | tf_op jit(solution)/shard_map/ppermute | solution.py:206
  85.4 0.7 copy-start
  85.4 0.7 copy-start.1

commit v8 on v6

--- a/solution.py
+++ b/solution.py
@@ -23,7 +23,7 @@
         for part, buf in enumerate((k_buf, v_buf)):
             for e in range(2):
                 copies[d, e, part] = pltpu.make_async_copy(
-                    pieces[2 * d + e].at[:, part],
+                    pieces[2 * d + e].at[:, :, part],
                     buf.at[d % 2, ((x + d) % 4) // 2, (core + e) % 2],
                     sems.at[2 * d + e, part],
                 )
@@ -58,7 +58,7 @@
         side, iy, jy = i // 16, i // 4 % 4, i % 4
         live = counts[jy * 2 + (x_lo + side) % 2]
         q = q_ref[:, (y + 4 - iy) % 4].reshape(256, HD)
-        k = k_buf[side, :, :, pl.ds(jy * 16, 16)].reshape(1024, HD)
+        k = k_buf[side, :, :, :, jy].reshape(1024, HD)
         s = lax.dot_general(q, k, (((1,), (1,)), ((), ())), preferred_element_type=jnp.float32)
         top = None
         for g in range(8):
@@ -81,7 +81,7 @@
             w = jnp.concatenate([wa.astype(jnp.bfloat16), wb.astype(jnp.bfloat16)], axis=1)
             weights.append(w)
             total = wa + wb if total is None else total + (wa + wb)
-        v = v_buf[side, :, :, pl.ds(jy * 16, 16)].reshape(1024, HD)
+        v = v_buf[side, :, :, :, jy].reshape(1024, HD)
         acc = jnp.dot(jnp.concatenate(weights, axis=1), v, preferred_element_type=jnp.float32)
         return row_tops[slot][...], total, acc
 
@@ -125,19 +125,19 @@
     lax.fori_loop(0, (count + 2 * UNROLL - 1) // (2 * UNROLL), pair, 0)
     for iy in range(4):
         total = jnp.sum(total_ref[iy], axis=1, keepdims=True)
-        out_ref[iy * 16 : (iy + 1) * 16] = (acc_ref[iy] / total).astype(jnp.bfloat16).reshape(16, 16, HD)
+        out_ref[:, iy] = (acc_ref[iy] / total).astype(jnp.bfloat16).reshape(16, 16, HD)
 
 def attend(place, mask, counts, q, pieces):
     smem = pl.BlockSpec(memory_space=pltpu.SMEM)
     vmem = pl.BlockSpec(memory_space=pltpu.VMEM)
     return pl.pallas_call(
         attend_kernel,
-        out_shape=jax.ShapeDtypeStruct((64, 16, HD), jnp.bfloat16),
+        out_shape=jax.ShapeDtypeStruct((16, 4, 16, HD), jnp.bfloat16),
         in_specs=[smem, smem, smem, vmem] + [pl.BlockSpec(memory_space=pl.ANY)] * 8,
         out_specs=vmem,
         scratch_shapes=[
-            pltpu.VMEM((2, 2, 2, 64, 16, HD), jnp.bfloat16),
-            pltpu.VMEM((2, 2, 2, 64, 16, HD), jnp.bfloat16),
+            pltpu.VMEM((2, 2, 2, 16, 4, 16, HD), jnp.bfloat16),
+            pltpu.VMEM((2, 2, 2, 16, 4, 16, HD), jnp.bfloat16),
             *[pltpu.VMEM((256, 1024), jnp.float32)] * (2 * UNROLL),
             *[pltpu.VMEM((256, HD), jnp.float32)] * (2 * UNROLL),
             pltpu.VMEM((4, 256, HD), jnp.float32),
@@ -185,15 +185,15 @@
         return array.reshape(tok_rows, heads, HD).transpose(1, 0, 2)
 
     def exchange(array):
-        return lax.all_to_all(array, ("y", "z"), split_axis=0, concat_axis=0, tiled=True)
+        return lax.all_to_all(array, ("z", "y"), split_axis=0, concat_axis=0, tiled=True)
 
     kv = exchange(pack(keys[0], values[0]))
     n_y = lax.axis_size("y")
     y = lax.axis_index("y")
-    by_group = by_head(queries).reshape(n_y, heads // n_y, tok_rows, HD)
+    by_group = by_head(queries).reshape(heads // n_y, n_y, tok_rows, HD)
     parts = []
     for d in range(n_y):
-        part = lax.dynamic_index_in_dim(by_group, (y + d) % n_y, 0, keepdims=False)
+        part = lax.dynamic_index_in_dim(by_group, (y + d) % n_y, 1, keepdims=False)
         if d > 0:
             part = lax.ppermute(part, "y", [(a, (a + d) % n_y) for a in range(n_y)])
         parts.append(part)
@@ -205,9 +205,10 @@
     for piece in [kv] + [lax.ppermute(kv, x_axes, ring(step)) for step in (-1, 1, 2)]:
         pieces += [piece, lax.ppermute(piece, "core", [(0, 1), (1, 0)])]
     pieces = pieces[:4] + pieces[6:] + pieces[4:6]
+    pieces = [piece.reshape(heads // n_y, n_y, 2, tok_rows, HD) for piece in pieces]
     place = jnp.stack([lax.axis_index(name) for name in ("x_lo", "x_hi", "core", "y")])
     out = attend(place.astype(jnp.int32), span_mask, span_counts, q, pieces)
-    back = exchange(out)
+    back = exchange(out.reshape(heads, tok_rows, HD))
     return back.transpose(1, 0, 2).reshape(1, tok_rows, width)
 
 

time: 127 us -> 130 us (1.024)
  the two profiles are of different devices: /device:TPU:2 before, /device:TPU:1 now
where the time goes in v8:
time: 130 us; the launch traced here: 128 us
  starting transfers between devices  60.1 us (46%)
  blocking collectives  28.4 us (22%)
  waiting for transfers between devices  23.5 us (18%)
  Pallas kernels  13.5 us (10%)
  local copies, waits for them, and re-layouts  1.84 us (1%)
    all_to_all x1, blocking collectives, exchange(): lax.all_to_all(array, ('z', 'y'), split_axis=0, concat_axis=0, tiled=True)  28.4 us
    all_to_all x1, starting transfers between devices, exchange(): lax.all_to_all(array, ('z', 'y'), split_axis=0, concat_axis=0, tiled=True)  19.4 us
    ppermute x4, starting transfers between devices, per_device(): pieces += [piece, lax.ppermute(piece, 'core', [(0, 1), (1, 0)])]  16.1 us
    all_to_all x1, waiting for transfers between devices, exchange(): lax.all_to_all(array, ('z', 'y'), split_axis=0, concat_axis=0, tiled=True)  14.6 us
    pallas_call x1, Pallas kernels, attend(): pl.pallas_call(attend_kernel, out_shape=jax.ShapeDtypeStruct((16, 4, 16,...  11.6 us
    ppermute x3, starting transfers between devices, per_device(): lax.ppermute(kv, x_axes, ring(step))  10.5 us
    ppermute x3, starting transfers between devices, per_device(): part = lax.ppermute(part, 'y', [(a, (a + d) % n_y) for a in range(n_y)])  9.1 us
    ppermute x3, waiting for transfers between devices, per_device(): part = lax.ppermute(part, 'y', [(a, (a + d) % n_y) for a in range(n_y)])  5.22 us
  transfers between devices with their start and end apart: 12, of which 5 were waited for; matrix products, arithmetic and copies ran while one was open for 1% of the time, Pallas kernels for 0%

profile of v8, /device:TPU:1, one launch (start us, length us, event | category | flops | bytes accessed | tf_op | source)
XLA Modules:
  0.0 128.4 jit_solution(15587479824796421739)
XLA Ops:
  0.0 1.9 %shard_map.55 = bf16[64,2,16,128]{3,2,1,0:T(8,128)(2,1)} custom-call(bf16[16,8192]{1,0:T(8,128)(2,1)} %bitcast.42, bf16[16,8192]{1,0:T(8,128)(2,1)} %bitcast.43), custom_call_target="tpu_custom_call" | custom-call | tf_op jit(solution)/shard_map/pallas_call | solution.py:165
  1.9 19.4 %all-to-all-start = ((bf16[64,2,16,128]{3,2,1,0:T(8,128)(2,1)}), bf16[64,2,16,128]{3,2,1,0:T(8,128)(2,1)S(1)}, u32[]{:S(2)}, u32[]{:S(2)}) async-start(bf16[64,2,16,128]{3,2,1,0:T(8,128)(2,1)} %shard_map.55), calls=%async_computation | async-start | bytes 1048576 | tf_op jit(solution)/shard_map/all_to_all | solution.py:188
  21.4 0.2 copy.6
  21.7 4.1 %collective-permute-start.2 = (bf16[16,16,128]{2,1,0:T(8,128)(2,1)S(1)}, bf16[16,16,128]{2,1,0:T(8,128)(2,1)S(1)}, u32[]{:S(2)}, u32[]{:S(2)}) collective-permute-start(bf16[16,16,128]{2,1,0:T(8,128)(2,1)S(1)} %get-tuple-element.10), channel_id=1, source_target_pairs={{0,384},{128,0},{256,128},{384,256},{1,385},{129,1},{257,129},{385... | collective-permute-start | bytes 196616 | tf_op jit(solution)/shard_map/ppermute | solution.py:198
  25.8 2.5 %collective-permute-start.1 = (bf16[16,16,128]{2,1,0:T(8,128)(2,1)S(1)}, bf16[16,16,128]{2,1,0:T(8,128)(2,1)S(1)}, u32[]{:S(2)}, u32[]{:S(2)}) collective-permute-start(bf16[16,16,128]{2,1,0:T(8,128)(2,1)S(1)} %get-tuple-element.11), channel_id=1, source_target_pairs={{0,256},{128,384},{256,0},{384,128},{1,257},{129,385},{257,1},{385... | collective-permute-start | bytes 196616 | tf_op jit(solution)/shard_map/ppermute | solution.py:198
  28.3 2.5 %collective-permute-start = (bf16[16,16,128]{2,1,0:T(8,128)(2,1)S(1)}, bf16[16,16,128]{2,1,0:T(8,128)(2,1)S(1)}, u32[]{:S(2)}, u32[]{:S(2)}) collective-permute-start(bf16[16,16,128]{2,1,0:T(8,128)(2,1)S(1)} %get-tuple-element.12), channel_id=1, source_target_pairs={{0,128},{128,256},{256,384},{384,0},{1,129},{129,257},{257,385},{3... | collective-permute-start | bytes 196616 | tf_op jit(solution)/shard_map/ppermute | solution.py:198
  30.8 0.0 collective-permute-done.2
  30.8 2.0 %collective-permute-done.1 = bf16[16,16,128]{2,1,0:T(8,128)(2,1)S(1)} collective-permute-done((bf16[16,16,128]{2,1,0:T(8,128)(2,1)S(1)}, bf16[16,16,128]{2,1,0:T(8,128)(2,1)S(1)}, u32[]{:S(2)}, u32[]{:S(2)}) %collective-permute-start.1) | collective-permute-done | bytes 65568 | tf_op jit(solution)/shard_map/ppermute | solution.py:198
  32.9 3.2 %collective-permute-done = bf16[16,16,128]{2,1,0:T(8,128)(2,1)S(1)} collective-permute-done((bf16[16,16,128]{2,1,0:T(8,128)(2,1)S(1)}, bf16[16,16,128]{2,1,0:T(8,128)(2,1)S(1)}, u32[]{:S(2)}, u32[]{:S(2)}) %collective-permute-start) | collective-permute-done | bytes 65568 | tf_op jit(solution)/shard_map/ppermute | solution.py:198
  36.1 0.7 pad_maximum_fusion
  36.8 14.6 %all-to-all-done = bf16[64,2,16,128]{3,2,1,0:T(8,128)(2,1)S(1)} async-done(((bf16[64,2,16,128]{3,2,1,0:T(8,128)(2,1)}), bf16[64,2,16,128]{3,2,1,0:T(8,128)(2,1)S(1)}, u32[]{:S(2)}, u32[]{:S(2)}) %all-to-all-start) | async-done | bytes 524320 | tf_op jit(solution)/shard_map/all_to_all | solution.py:188
  51.4 3.1 %collective-permute-start.8 = (bf16[64,2,16,128]{3,2,1,0:T(8,128)(2,1)S(1)}, bf16[64,2,16,128]{3,2,1,0:T(8,128)(2,1)S(1)}, u32[]{:S(2)}, u32[]{:S(2)}) collective-permute-start(bf16[64,2,16,128]{3,2,1,0:T(8,128)(2,1)S(1)} %all-to-all-done), channel_id=1, source_target_pairs={{0,64},{64,32},{32,96},{96,0},{1,65},{65,33},{33,97},{97,1},{2,66}... | collective-permute-start | bytes 1572872 | tf_op jit(solution)/shard_map/ppermute | solution.py:205
  54.5 4.4 %collective-permute-start.6 = (bf16[64,2,16,128]{3,2,1,0:T(8,128)(2,1)S(1)}, bf16[64,2,16,128]{3,2,1,0:T(8,128)(2,1)S(1)}, u32[]{:S(2)}, u32[]{:S(2)}) collective-permute-start(bf16[64,2,16,128]{3,2,1,0:T(8,128)(2,1)S(1)} %all-to-all-done), channel_id=1, source_target_pairs={{0,32},{64,96},{32,0},{96,64},{1,33},{65,97},{33,1},{97,65},{2,34}... | collective-permute-start | bytes 1572872 | tf_op jit(solution)/shard_map/ppermute | solution.py:205
  58.8 3.1 %collective-permute-start.4 = (bf16[64,2,16,128]{3,2,1,0:T(8,128)(2,1)S(1)}, bf16[64,2,16,128]{3,2,1,0:T(8,128)(2,1)S(1)}, u32[]{:S(2)}, u32[]{:S(2)}) collective-permute-start(bf16[64,2,16,128]{3,2,1,0:T(8,128)(2,1)S(1)} %all-to-all-done), channel_id=1, source_target_pairs={{0,96},{64,0},{32,64},{96,32},{1,97},{65,1},{33,65},{97,33},{2,98}... | collective-permute-start | bytes 1572872 | tf_op jit(solution)/shard_map/ppermute | solution.py:205
  61.9 5.0 %all-to-all-start.1 = ((bf16[16,4,16,128]{3,2,1,0:T(8,128)(2,1)}), bf16[16,4,16,128]{3,2,1,0:T(8,128)(2,1)S(1)}, u32[]{:S(2)}, u32[]{:S(2)}) async-start(bf16[16,4,16,128]{3,2,1,0:T(8,128)(2,1)} %pad_maximum_fusion), calls=%async_computation.1 | async-start | bytes 524288 | tf_op jit(solution)/shard_map/all_to_all | solution.py:201
  66.9 5.7 %collective-permute-start.3 = (bf16[64,2,16,128]{3,2,1,0:T(8,128)(2,1)S(1)}, bf16[64,2,16,128]{3,2,1,0:T(8,128)(2,1)S(1)}, u32[]{:S(2)}, u32[]{:S(2)}) collective-permute-start(bf16[64,2,16,128]{3,2,1,0:T(8,128)(2,1)S(1)} %all-to-all-done), channel_id=1, source_target_pairs={{0,1},{1,0},{2,3},{3,2},{4,5},{5,4},{6,7},{7,6},{8,9},{9,8},{10,11... | collective-permute-start | bytes 1572872 | tf_op jit(solution)/shard_map/ppermute | solution.py:206
  72.6 0.0 collective-permute-done.8
  72.6 1.9 %collective-permute-start.9 = (bf16[64,2,16,128]{3,2,1,0:T(8,128)(2,1)S(1)}, bf16[64,2,16,128]{3,2,1,0:T(8,128)(2,1)S(1)}, u32[]{:S(2)}, u32[]{:S(2)}) collective-permute-start(bf16[64,2,16,128]{3,2,1,0:T(8,128)(2,1)S(1)} %collective-permute-done.8), channel_id=1, source_target_pairs={{0,1},{1,0},{2,3},{3,2},{4,5},{5,4},{6,7},{7,6},{8,9},{9,8},{10,11... | collective-permute-start | bytes 1572872 | tf_op jit(solution)/shard_map/ppermute | solution.py:206
  74.5 1.8 %collective-permute-done.6 = bf16[64,2,16,128]{3,2,1,0:T(8,128)(2,1)S(1)} collective-permute-done((bf16[64,2,16,128]{3,2,1,0:T(8,128)(2,1)S(1)}, bf16[64,2,16,128]{3,2,1,0:T(8,128)(2,1)S(1)}, u32[]{:S(2)}, u32[]{:S(2)}) %collective-permute-start.6) | collective-permute-done | bytes 524320 | tf_op jit(solution)/shard_map/ppermute | solution.py:205
  76.3 6.6 %collective-permute-start.7 = (bf16[64,2,16,128]{3,2,1,0:T(8,128)(2,1)S(1)}, bf16[64,2,16,128]{3,2,1,0:T(8,128)(2,1)}, u32[]{:S(2)}, u32[]{:S(2)}) collective-permute-start(bf16[64,2,16,128]{3,2,1,0:T(8,128)(2,1)S(1)} %collective-permute-done.6), channel_id=1, source_target_pairs={{0,1},{1,0},{2,3},{3,2},{4,5},{5,4},{6,7},{7,6},{8,9},{9,8},{10,11... | collective-permute-start | bytes 1572872 | tf_op jit(solution)/shard_map/ppermute | solution.py:206
  82.9 0.0 collective-permute-done.4
  82.9 1.9 %collective-permute-start.5 = (bf16[64,2,16,128]{3,2,1,0:T(8,128)(2,1)S(1)}, bf16[64,2,16,128]{3,2,1,0:T(8,128)(2,1)}, u32[]{:S(2)}, u32[]{:S(2)}) collective-permute-start(bf16[64,2,16,128]{3,2,1,0:T(8,128)(2,1)S(1)} %collective-permute-done.4), channel_id=1, source_target_pairs={{0,1},{1,0},{2,3},{3,2},{4,5},{5,4},{6,7},{7,6},{8,9},{9,8},{10,11... | collective-permute-start | bytes 1572872 | tf_op jit(solution)/shard_map/ppermute | solution.py:206
  84.9 0.1 pad_add_fusion.place
  84.9 0.0 collective-permute-done.3
  84.9 0.0 all-to-all-done.1.q_ref
  84.9 0.0 collective-permute-done.9
  85.0 1.9 %collective-permute-done.5 = bf16[64,2,16,128]{3,2,1,0:T(8,128)(2,1)} collective-permute-done((bf16[64,2,16,128]{3,2,1,0:T(8,128)(2,1)S(1)}, bf16[64,2,16,128]{3,2,1,0:T(8,128)(2,1)}, u32[]{:S(2)}, u32[]{:S(2)}) %collective-permute-start.5) | collective-permute-done | bytes 524320 | tf_op jit(solution)/shard_map/ppermute | solution.py:206
  86.9 0.7 copy-done
  87.5 11.6 %shard_map.56 = bf16[16,4,16,128]{3,2,1,0:T(8,128)(2,1)S(1)} custom-call(s32[4]{0:T(128)S(1)} %pad_add_fusion.place, s32[8,8]{1,0:T(8,128)S(1)} %copy-done, s32[8]{0:T(128)S(1)} %copy-done.1, bf16[16,4,16,128]{3,2,1,0:T(8,128)(2,1)S(1)} %all-to-all-done.1.q_ref, bf16[16,4,2,16,128]{4,3,2,1,0:T(8,128)(2,1)S(1)} %bitcast.31, ...), custom_call_target="tpu_custom_call" | custom-call | flops 4294967296 | bytes 5242880 | tf_op jit(solution)/shard_map/pallas_call | solution.py:133
  99.1 28.4 %all_to_all.15 = bf16[64,16,128]{2,1,0:T(8,128)(2,1)S(1)} all-to-all(bf16[64,16,128]{2,1,0:T(8,128)(2,1)S(1)} %bitcast.32), channel_id=1, replica_groups=mesh['y'=4,'x_lo'=2,'x_hi'=2,'z'=16,'core'=2] {'z','y'}, dimensions={0} | all-to-all | bytes 524288 | tf_op jit(solution)/shard_map/all_to_all | solution.py:188
  127.5 0.1 copy.7
  127.6 0.8 reshape.47
  (8 shorter events, 0.1 us)
Async XLA Ops:
  1.9 19.5 %copy-start.2 = (bf16[1,16,8192]{2,1,0:T(8,128)(2,1)S(1)}, bf16[1,16,8192]{2,1,0:T(8,128)(2,1)}, u32[]{:S(2)}) copy-start(bf16[1,16,8192]{2,1,0:T(8,128)(2,1)} %param.5) | copy-start | bytes 786436
  1.9 49.4 %all-to-all-start = ((bf16[64,2,16,128]{3,2,1,0:T(8,128)(2,1)}), bf16[64,2,16,128]{3,2,1,0:T(8,128)(2,1)S(1)}, u32[]{:S(2)}, u32[]{:S(2)}) async-start(bf16[64,2,16,128]{3,2,1,0:T(8,128)(2,1)} %shard_map.55), calls=%async_computation | async-start | bytes 1048576 | tf_op jit(solution)/shard_map/all_to_all | solution.py:188
  21.7 9.1 %collective-permute-start.2 = (bf16[16,16,128]{2,1,0:T(8,128)(2,1)S(1)}, bf16[16,16,128]{2,1,0:T(8,128)(2,1)S(1)}, u32[]{:S(2)}, u32[]{:S(2)}) collective-permute-start(bf16[16,16,128]{2,1,0:T(8,128)(2,1)S(1)} %get-tuple-element.10), channel_id=1, source_target_pairs={{0,384},{128,0},{256,128},{384,256},{1,385},{129,1},{257,129},{385... | collective-permute-start | bytes 196616 | tf_op jit(solution)/shard_map/ppermute | solution.py:198
  25.8 7.0 %collective-permute-start.1 = (bf16[16,16,128]{2,1,0:T(8,128)(2,1)S(1)}, bf16[16,16,128]{2,1,0:T(8,128)(2,1)S(1)}, u32[]{:S(2)}, u32[]{:S(2)}) collective-permute-start(bf16[16,16,128]{2,1,0:T(8,128)(2,1)S(1)} %get-tuple-element.11), channel_id=1, source_target_pairs={{0,256},{128,384},{256,0},{384,128},{1,257},{129,385},{257,1},{385... | collective-permute-start | bytes 196616 | tf_op jit(solution)/shard_map/ppermute | solution.py:198
  28.3 7.7 %collective-permute-start = (bf16[16,16,128]{2,1,0:T(8,128)(2,1)S(1)}, bf16[16,16,128]{2,1,0:T(8,128)(2,1)S(1)}, u32[]{:S(2)}, u32[]{:S(2)}) collective-permute-start(bf16[16,16,128]{2,1,0:T(8,128)(2,1)S(1)} %get-tuple-element.12), channel_id=1, source_target_pairs={{0,128},{128,256},{256,384},{384,0},{1,129},{129,257},{257,385},{3... | collective-permute-start | bytes 196616 | tf_op jit(solution)/shard_map/ppermute | solution.py:198
  51.4 21.2 %collective-permute-start.8 = (bf16[64,2,16,128]{3,2,1,0:T(8,128)(2,1)S(1)}, bf16[64,2,16,128]{3,2,1,0:T(8,128)(2,1)S(1)}, u32[]{:S(2)}, u32[]{:S(2)}) collective-permute-start(bf16[64,2,16,128]{3,2,1,0:T(8,128)(2,1)S(1)} %all-to-all-done), channel_id=1, source_target_pairs={{0,64},{64,32},{32,96},{96,0},{1,65},{65,33},{33,97},{97,1},{2,66}... | collective-permute-start | bytes 1572872 | tf_op jit(solution)/shard_map/ppermute | solution.py:205
  54.5 21.9 %collective-permute-start.6 = (bf16[64,2,16,128]{3,2,1,0:T(8,128)(2,1)S(1)}, bf16[64,2,16,128]{3,2,1,0:T(8,128)(2,1)S(1)}, u32[]{:S(2)}, u32[]{:S(2)}) collective-permute-start(bf16[64,2,16,128]{3,2,1,0:T(8,128)(2,1)S(1)} %all-to-all-done), channel_id=1, source_target_pairs={{0,32},{64,96},{32,0},{96,64},{1,33},{65,97},{33,1},{97,65},{2,34}... | collective-permute-start | bytes 1572872 | tf_op jit(solution)/shard_map/ppermute | solution.py:205
  58.8 24.1 %collective-permute-start.4 = (bf16[64,2,16,128]{3,2,1,0:T(8,128)(2,1)S(1)}, bf16[64,2,16,128]{3,2,1,0:T(8,128)(2,1)S(1)}, u32[]{:S(2)}, u32[]{:S(2)}) collective-permute-start(bf16[64,2,16,128]{3,2,1,0:T(8,128)(2,1)S(1)} %all-to-all-done), channel_id=1, source_target_pairs={{0,96},{64,0},{32,64},{96,32},{1,97},{65,1},{33,65},{97,33},{2,98}... | collective-permute-start | bytes 1572872 | tf_op jit(solution)/shard_map/ppermute | solution.py:205
  61.9 23.0 %all-to-all-start.1 = ((bf16[16,4,16,128]{3,2,1,0:T(8,128)(2,1)}), bf16[16,4,16,128]{3,2,1,0:T(8,128)(2,1)S(1)}, u32[]{:S(2)}, u32[]{:S(2)}) async-start(bf16[16,4,16,128]{3,2,1,0:T(8,128)(2,1)} %pad_maximum_fusion), calls=%async_computation.1 | async-start | bytes 524288 | tf_op jit(solution)/shard_map/all_to_all | solution.py:201
  66.9 18.0 %collective-permute-start.3 = (bf16[64,2,16,128]{3,2,1,0:T(8,128)(2,1)S(1)}, bf16[64,2,16,128]{3,2,1,0:T(8,128)(2,1)S(1)}, u32[]{:S(2)}, u32[]{:S(2)}) collective-permute-start(bf16[64,2,16,128]{3,2,1,0:T(8,128)(2,1)S(1)} %all-to-all-done), channel_id=1, source_target_pairs={{0,1},{1,0},{2,3},{3,2},{4,5},{5,4},{6,7},{7,6},{8,9},{9,8},{10,11... | collective-permute-start | bytes 1572872 | tf_op jit(solution)/shard_map/ppermute | solution.py:206
  72.6 12.4 %collective-permute-start.9 = (bf16[64,2,16,128]{3,2,1,0:T(8,128)(2,1)S(1)}, bf16[64,2,16,128]{3,2,1,0:T(8,128)(2,1)S(1)}, u32[]{:S(2)}, u32[]{:S(2)}) collective-permute-start(bf16[64,2,16,128]{3,2,1,0:T(8,128)(2,1)S(1)} %collective-permute-done.8), channel_id=1, source_target_pairs={{0,1},{1,0},{2,3},{3,2},{4,5},{5,4},{6,7},{7,6},{8,9},{9,8},{10,11... | collective-permute-start | bytes 1572872 | tf_op jit(solution)/shard_map/ppermute | solution.py:206
  76.3 8.6 %collective-permute-start.7 = (bf16[64,2,16,128]{3,2,1,0:T(8,128)(2,1)S(1)}, bf16[64,2,16,128]{3,2,1,0:T(8,128)(2,1)}, u32[]{:S(2)}, u32[]{:S(2)}) collective-permute-start(bf16[64,2,16,128]{3,2,1,0:T(8,128)(2,1)S(1)} %collective-permute-done.6), channel_id=1, source_target_pairs={{0,1},{1,0},{2,3},{3,2},{4,5},{5,4},{6,7},{7,6},{8,9},{9,8},{10,11... | collective-permute-start | bytes 1572872 | tf_op jit(solution)/shard_map/ppermute | solution.py:206
  82.9 3.9 %collective-permute-start.5 = (bf16[64,2,16,128]{3,2,1,0:T(8,128)(2,1)S(1)}, bf16[64,2,16,128]{3,2,1,0:T(8,128)(2,1)}, u32[]{:S(2)}, u32[]{:S(2)}) collective-permute-start(bf16[64,2,16,128]{3,2,1,0:T(8,128)(2,1)S(1)} %collective-permute-done.4), channel_id=1, source_target_pairs={{0,1},{1,0},{2,3},{3,2},{4,5},{5,4},{6,7},{7,6},{8,9},{9,8},{10,11... | collective-permute-start | bytes 1572872 | tf_op jit(solution)/shard_map/ppermute | solution.py:206
  86.9 0.7 copy-start
  86.9 0.7 copy-start.1

commit v9 on v6

--- a/solution.py
+++ b/solution.py
@@ -8,23 +8,24 @@
 HD = 128
 LOW = -1e30
 LOG2E = 1.4426950408889634
-UNROLL = 2
+UNROLL = 1
 
 
 def attend_kernel(place, mask, counts, q_ref, *rest):
     pieces = rest[:8]
-    out_ref, k_buf, v_buf = rest[8:11]
-    scores, row_tops = rest[11 : 11 + 2 * UNROLL], rest[11 + 2 * UNROLL : 11 + 4 * UNROLL]
-    acc_ref, top_ref, total_ref, todo, sems = rest[11 + 4 * UNROLL :]
+    out_ref, q_buf, k_buf, v_buf = rest[8:12]
+    scores, row_tops = rest[12 : 12 + 2 * UNROLL], rest[12 + 2 * UNROLL : 12 + 4 * UNROLL]
+    acc_ref, top_ref, total_ref, todo, sems, q_sem = rest[12 + 4 * UNROLL :]
     x_lo, x_hi, core, y = place[0], place[1], place[2], place[3]
-    x = x_hi * 2 + x_lo
+    q_copy = pltpu.make_async_copy(q_ref, q_buf, q_sem)
+    q_copy.start()
     copies = {}
     for d in range(4):
         for part, buf in enumerate((k_buf, v_buf)):
             for e in range(2):
                 copies[d, e, part] = pltpu.make_async_copy(
                     pieces[2 * d + e].at[:, part],
-                    buf.at[d % 2, ((x + d) % 4) // 2, (core + e) % 2],
+                    buf.at[d % 2, x_hi ^ (d // 2), core ^ e],
                     sems.at[2 * d + e, part],
                 )
     for side in range(2):
@@ -50,51 +51,52 @@
     top_ref[...] = jnp.full_like(top_ref, LOW)
     total_ref[...] = jnp.zeros_like(total_ref)
     scale = LOG2E / HD**0.5
-    lane = lax.broadcasted_iota(jnp.int32, (1, 128), 1)
-    late = 768 + lane // 16 * 32 + lane % 16
+    row = lax.broadcasted_iota(jnp.int32, (128, 256), 0)
+    late = 768 + row // 16 * 32 + row % 16
 
     def score(n, slot):
         i = todo[jnp.minimum(n, count - 1)]
         side, iy, jy = i // 16, i // 4 % 4, i % 4
         live = counts[jy * 2 + (x_lo + side) % 2]
-        q = q_ref[:, (y + 4 - iy) % 4].reshape(256, HD)
+        q = q_buf[:, y ^ iy].reshape(256, HD)
         k = k_buf[side, :, :, pl.ds(jy * 16, 16)].reshape(1024, HD)
-        s = lax.dot_general(q, k, (((1,), (1,)), ((), ())), preferred_element_type=jnp.float32)
+        s = lax.dot_general(k, q, (((1,), (1,)), ((), ())), preferred_element_type=jnp.float32)
         top = None
         for g in range(8):
-            a = s[:, g * 128 : (g + 1) * 128]
+            a = s[g * 128 : (g + 1) * 128]
             if g >= 4 and g % 2 == 1:
                 a = jnp.where(late + g // 2 % 2 * 16 < live, a, LOW)
-            scores[slot][:, g * 128 : (g + 1) * 128] = a
+            scores[slot][g * 128 : (g + 1) * 128] = a
             top = a if top is None else jnp.maximum(top, a)
-        row_tops[slot][...] = jnp.broadcast_to(jnp.max(top, axis=1, keepdims=True), (256, 128))
+        row_tops[slot][...] = jnp.broadcast_to(jnp.max(top, axis=0, keepdims=True), (8, 256))
 
     def mix(n, slot):
         i = todo[jnp.minimum(n, count - 1)]
         side, jy = i // 16, i % 4
-        shift = row_tops[slot][...] * scale
+        shift = row_tops[slot][:1] * scale
         total, weights = None, []
-        for g in range(4):
-            at = g * 256
-            wa = jnp.exp2(scores[slot][:, at : at + 128] * scale - shift)
-            wb = jnp.exp2(scores[slot][:, at + 128 : at + 256] * scale - shift)
-            w = jnp.concatenate([wa.astype(jnp.bfloat16), wb.astype(jnp.bfloat16)], axis=1)
-            weights.append(w)
-            total = wa + wb if total is None else total + (wa + wb)
+        for g in range(8):
+            w = jnp.exp2(scores[slot][g * 128 : (g + 1) * 128] * scale - shift)
+            weights.append(w.astype(jnp.bfloat16))
+            total = w if total is None else total + w
+        total = jnp.sum(total, axis=0, keepdims=True)
         v = v_buf[side, :, :, pl.ds(jy * 16, 16)].reshape(1024, HD)
-        acc = jnp.dot(jnp.concatenate(weights, axis=1), v, preferred_element_type=jnp.float32)
-        return row_tops[slot][...], total, acc
+        weights = jnp.concatenate(weights, axis=0)
+        acc = lax.dot_general(
+            v, weights, (((0,), (0,)), ((), ())), preferred_element_type=jnp.float32
+        )
+        return row_tops[slot][:1], total, acc
 
     def merge(n, state):
         top, total, acc = state
         iy = todo[jnp.minimum(n, count - 1)] // 4 % 4
         top = jnp.where(n < count, top, LOW)
-        old = top_ref[iy]
+        old = top_ref[iy][:1]
         new = jnp.maximum(old, top)
         keep, add = jnp.exp2((old - new) * scale), jnp.exp2((top - new) * scale)
-        total_ref[iy] = total_ref[iy] * keep + total * add
+        total_ref[iy] = jnp.broadcast_to(total_ref[iy][:1] * keep + total * add, (8, 256))
         acc_ref[iy] = acc_ref[iy] * keep + acc * add
-        top_ref[iy] = new
+        top_ref[iy] = jnp.broadcast_to(new, (8, 256))
 
     def step(n, slot):
         @pl.when((n + 2 * UNROLL > first) & (n + UNROLL <= first))
@@ -108,6 +110,7 @@
         for u in range(UNROLL):
             merge(n + u, states[u])
 
+    q_copy.wait()
     wait(0, 0)
     for u in range(UNROLL):
         score(u, u)
@@ -124,8 +127,9 @@
 
     lax.fori_loop(0, (count + 2 * UNROLL - 1) // (2 * UNROLL), pair, 0)
     for iy in range(4):
-        total = jnp.sum(total_ref[iy], axis=1, keepdims=True)
-        out_ref[iy * 16 : (iy + 1) * 16] = (acc_ref[iy] / total).astype(jnp.bfloat16).reshape(16, 16, HD)
+        result = (acc_ref[iy] / total_ref[iy][:1]).T.astype(jnp.bfloat16)
+        out_ref[iy * 16 : (iy + 1) * 16] = result.reshape(16, 16, HD)
+
 
 def attend(place, mask, counts, q, pieces):
     smem = pl.BlockSpec(memory_space=pltpu.SMEM)
@@ -133,18 +137,20 @@
     return pl.pallas_call(
         attend_kernel,
         out_shape=jax.ShapeDtypeStruct((64, 16, HD), jnp.bfloat16),
-        in_specs=[smem, smem, smem, vmem] + [pl.BlockSpec(memory_space=pl.ANY)] * 8,
+        in_specs=[smem, smem, smem] + [pl.BlockSpec(memory_space=pl.ANY)] * 9,
         out_specs=vmem,
         scratch_shapes=[
+            pltpu.VMEM(q.shape, jnp.bfloat16),
             pltpu.VMEM((2, 2, 2, 64, 16, HD), jnp.bfloat16),
             pltpu.VMEM((2, 2, 2, 64, 16, HD), jnp.bfloat16),
-            *[pltpu.VMEM((256, 1024), jnp.float32)] * (2 * UNROLL),
-            *[pltpu.VMEM((256, HD), jnp.float32)] * (2 * UNROLL),
-            pltpu.VMEM((4, 256, HD), jnp.float32),
-            pltpu.VMEM((4, 256, HD), jnp.float32),
-            pltpu.VMEM((4, 256, HD), jnp.float32),
+            *[pltpu.VMEM((1024, 256), jnp.float32)] * (2 * UNROLL),
+            *[pltpu.VMEM((8, 256), jnp.float32)] * (2 * UNROLL),
+            pltpu.VMEM((4, HD, 256), jnp.float32),
+            pltpu.VMEM((4, 8, 256), jnp.float32),
+            pltpu.VMEM((4, 8, 256), jnp.float32),
             pltpu.SMEM((33,), jnp.int32),
             pltpu.SemaphoreType.DMA((8, 2)),
+            pltpu.SemaphoreType.DMA(()),
         ],
         compiler_params=pltpu.CompilerParams(vmem_limit_bytes=40 * 1024 * 1024),
         cost_estimate=pl.CostEstimate(
@@ -170,11 +176,11 @@
     )(keys, values)
 
 
-def ring(step):
+def x_pairs(flip):
     def index(x):
-        return (x % 2) * 2 + x // 2
-
-    return [(index(x), index((x + step) % 4)) for x in range(4)]
+        return x % 2 * 2 + x // 2
+
+    return [(index(x), index(x ^ flip)) for x in range(4)]
 
 
 def per_device(queries, keys, values, span_mask, span_counts):
@@ -193,16 +199,16 @@
     by_group = by_head(queries).reshape(n_y, heads // n_y, tok_rows, HD)
     parts = []
     for d in range(n_y):
-        part = lax.dynamic_index_in_dim(by_group, (y + d) % n_y, 0, keepdims=False)
+        part = lax.dynamic_index_in_dim(by_group, y ^ d, 0, keepdims=False)
         if d > 0:
-            part = lax.ppermute(part, "y", [(a, (a + d) % n_y) for a in range(n_y)])
+            part = lax.ppermute(part, "y", [(a, a ^ d) for a in range(n_y)])
         parts.append(part)
     q_in, kv = lax.optimization_barrier((jnp.stack(parts, axis=1), kv))
     q = lax.all_to_all(q_in, "z", split_axis=0, concat_axis=0, tiled=True)
 
     x_axes = ("x_lo", "x_hi")
     pieces = []
-    for piece in [kv] + [lax.ppermute(kv, x_axes, ring(step)) for step in (-1, 1, 2)]:
+    for piece in [kv] + [lax.ppermute(kv, x_axes, x_pairs(flip)) for flip in (1, 3, 2)]:
         pieces += [piece, lax.ppermute(piece, "core", [(0, 1), (1, 0)])]
     pieces = pieces[:4] + pieces[6:] + pieces[4:6]
     place = jnp.stack([lax.axis_index(name) for name in ("x_lo", "x_hi", "core", "y")])

time: 127 us -> 127 us (level)
  the two profiles are of different devices: /device:TPU:2 before, /device:TPU:1 now
where the time goes in v9:
time: 127 us; the launch traced here: 126 us
  starting transfers between devices  58.8 us (46%)
  blocking collectives  28.3 us (22%)
  waiting for transfers between devices  25.3 us (20%)
  Pallas kernels  11.6 us (9%)
    all_to_all x1, blocking collectives, exchange(): lax.all_to_all(array, ('y', 'z'), split_axis=0, concat_axis=0, tiled=True)  28.3 us
    all_to_all x1, starting transfers between devices, exchange(): lax.all_to_all(array, ('y', 'z'), split_axis=0, concat_axis=0, tiled=True)  19.4 us
    all_to_all x1, waiting for transfers between devices, exchange(): lax.all_to_all(array, ('y', 'z'), split_axis=0, concat_axis=0, tiled=True)  16.2 us
    ppermute x4, starting transfers between devices, per_device(): pieces += [piece, lax.ppermute(piece, 'core', [(0, 1), (1, 0)])]  14.7 us
    pallas_call x1, Pallas kernels, attend(): pl.pallas_call(attend_kernel, out_shape=jax.ShapeDtypeStruct((64, 16, HD)...  9.67 us
    ppermute x3, starting transfers between devices, per_device(): part = lax.ppermute(part, 'y', [(a, a ^ d) for a in range(n_y)])  8.98 us
    ppermute x3, starting transfers between devices, per_device(): lax.ppermute(kv, x_axes, x_pairs(flip))  8.97 us
    all_to_all x1, starting transfers between devices, per_device(): q = lax.all_to_all(q_in, 'z', split_axis=0, concat_axis=0, tiled=True)  6.75 us
  transfers between devices with their start and end apart: 12, of which 5 were waited for; matrix products, arithmetic and copies ran while one was open for 1% of the time, Pallas kernels for 0%

profile of v9, /device:TPU:1, one launch (start us, length us, event | category | flops | bytes accessed | tf_op | source)
XLA Modules:
  0.0 126.2 jit_solution(5289160990726216417)
XLA Ops:
  0.0 1.9 %shard_map.55 = bf16[64,2,16,128]{3,2,1,0:T(8,128)(2,1)} custom-call(bf16[16,8192]{1,0:T(8,128)(2,1)} %bitcast.28, bf16[16,8192]{1,0:T(8,128)(2,1)} %bitcast.29), custom_call_target="tpu_custom_call" | custom-call | tf_op jit(solution)/shard_map/pallas_call | solution.py:171
  1.9 19.4 %all-to-all-start = ((bf16[64,2,16,128]{3,2,1,0:T(8,128)(2,1)}), bf16[64,2,16,128]{3,2,1,0:T(8,128)(2,1)S(1)}, u32[]{:S(2)}, u32[]{:S(2)}) async-start(bf16[64,2,16,128]{3,2,1,0:T(8,128)(2,1)} %shard_map.55), calls=%async_computation | async-start | bytes 1048576 | tf_op jit(solution)/shard_map/all_to_all | solution.py:194
  21.4 0.2 copy.7
  21.6 4.3 %collective-permute-start.2 = (bf16[16,16,128]{2,1,0:T(8,128)(2,1)S(1)}, bf16[16,16,128]{2,1,0:T(8,128)(2,1)S(1)}, u32[]{:S(2)}, u32[]{:S(2)}) collective-permute-start(bf16[16,16,128]{2,1,0:T(8,128)(2,1)S(1)} %get-tuple-element.10), channel_id=1, source_target_pairs={{0,384},{128,256},{256,128},{384,0},{1,385},{129,257},{257,129},{3... | collective-permute-start | bytes 196616 | tf_op jit(solution)/shard_map/ppermute | solution.py:204
  26.0 2.3 %collective-permute-start.1 = (bf16[16,16,128]{2,1,0:T(8,128)(2,1)S(1)}, bf16[16,16,128]{2,1,0:T(8,128)(2,1)S(1)}, u32[]{:S(2)}, u32[]{:S(2)}) collective-permute-start(bf16[16,16,128]{2,1,0:T(8,128)(2,1)S(1)} %get-tuple-element.11), channel_id=1, source_target_pairs={{0,256},{128,384},{256,0},{384,128},{1,257},{129,385},{257,1},{385... | collective-permute-start | bytes 196616 | tf_op jit(solution)/shard_map/ppermute | solution.py:204
  28.3 2.4 %collective-permute-start = (bf16[16,16,128]{2,1,0:T(8,128)(2,1)S(1)}, bf16[16,16,128]{2,1,0:T(8,128)(2,1)S(1)}, u32[]{:S(2)}, u32[]{:S(2)}) collective-permute-start(bf16[16,16,128]{2,1,0:T(8,128)(2,1)S(1)} %get-tuple-element.12), channel_id=1, source_target_pairs={{0,128},{128,0},{256,384},{384,256},{1,129},{129,1},{257,385},{385... | collective-permute-start | bytes 196616 | tf_op jit(solution)/shard_map/ppermute | solution.py:204
  30.6 0.0 collective-permute-done.2
  30.7 2.4 %collective-permute-done.1 = bf16[16,16,128]{2,1,0:T(8,128)(2,1)S(1)} collective-permute-done((bf16[16,16,128]{2,1,0:T(8,128)(2,1)S(1)}, bf16[16,16,128]{2,1,0:T(8,128)(2,1)S(1)}, u32[]{:S(2)}, u32[]{:S(2)}) %collective-permute-start.1) | collective-permute-done | bytes 65568 | tf_op jit(solution)/shard_map/ppermute | solution.py:204
  33.1 0.7 collective-permute-done
  33.8 0.7 pad_maximum_fusion
  34.5 16.2 %all-to-all-done.rest_0_ = bf16[64,2,16,128]{3,2,1,0:T(8,128)(2,1)S(1)} async-done(((bf16[64,2,16,128]{3,2,1,0:T(8,128)(2,1)}), bf16[64,2,16,128]{3,2,1,0:T(8,128)(2,1)S(1)}, u32[]{:S(2)}, u32[]{:S(2)}) %all-to-all-start) | async-done | bytes 524320 | tf_op jit(solution)/shard_map/all_to_all | solution.py:194
  50.7 4.4 %collective-permute-start.8 = (bf16[64,2,16,128]{3,2,1,0:T(8,128)(2,1)S(1)}, bf16[64,2,16,128]{3,2,1,0:T(8,128)(2,1)S(1)}, u32[]{:S(2)}, u32[]{:S(2)}) collective-permute-start(bf16[64,2,16,128]{3,2,1,0:T(8,128)(2,1)S(1)} %all-to-all-done.rest_0_), channel_id=1, source_target_pairs={{0,96},{64,32},{32,64},{96,0},{1,97},{65,33},{33,65},{97,1},{2,98}... | collective-permute-start | bytes 1572872 | tf_op jit(solution)/shard_map/ppermute | solution.py:211
  55.1 2.4 %collective-permute-start.6 = (bf16[64,2,16,128]{3,2,1,0:T(8,128)(2,1)S(1)}, bf16[64,2,16,128]{3,2,1,0:T(8,128)(2,1)S(1)}, u32[]{:S(2)}, u32[]{:S(2)}) collective-permute-start(bf16[64,2,16,128]{3,2,1,0:T(8,128)(2,1)S(1)} %all-to-all-done.rest_0_), channel_id=1, source_target_pairs={{0,32},{64,96},{32,0},{96,64},{1,33},{65,97},{33,1},{97,65},{2,34}... | collective-permute-start | bytes 1572872 | tf_op jit(solution)/shard_map/ppermute | solution.py:211
  57.6 2.2 %collective-permute-start.4 = (bf16[64,2,16,128]{3,2,1,0:T(8,128)(2,1)S(1)}, bf16[64,2,16,128]{3,2,1,0:T(8,128)(2,1)S(1)}, u32[]{:S(2)}, u32[]{:S(2)}) collective-permute-start(bf16[64,2,16,128]{3,2,1,0:T(8,128)(2,1)S(1)} %all-to-all-done.rest_0_), channel_id=1, source_target_pairs={{0,64},{64,0},{32,96},{96,32},{1,65},{65,1},{33,97},{97,33},{2,66}... | collective-permute-start | bytes 1572872 | tf_op jit(solution)/shard_map/ppermute | solution.py:211
  59.7 6.7 %all-to-all-start.1 = ((bf16[16,4,16,128]{3,2,1,0:T(8,128)(2,1)}), bf16[16,4,16,128]{3,2,1,0:T(8,128)(2,1)S(1)}, u32[]{:S(2)}, u32[]{:S(2)}) async-start(bf16[16,4,16,128]{3,2,1,0:T(8,128)(2,1)} %pad_maximum_fusion), calls=%async_computation.1 | async-start | bytes 524288 | tf_op jit(solution)/shard_map/all_to_all | solution.py:207
  66.5 4.6 %collective-permute-start.3 = (bf16[64,2,16,128]{3,2,1,0:T(8,128)(2,1)S(1)}, bf16[64,2,16,128]{3,2,1,0:T(8,128)(2,1)S(1)}, u32[]{:S(2)}, u32[]{:S(2)}) collective-permute-start(bf16[64,2,16,128]{3,2,1,0:T(8,128)(2,1)S(1)} %all-to-all-done.rest_0_), channel_id=1, source_target_pairs={{0,1},{1,0},{2,3},{3,2},{4,5},{5,4},{6,7},{7,6},{8,9},{9,8},{10,11... | collective-permute-start | bytes 1572872 | tf_op jit(solution)/shard_map/ppermute | solution.py:212
  71.1 4.4 %collective-permute-done.8.rest_6_ = bf16[64,2,16,128]{3,2,1,0:T(8,128)(2,1)S(1)} collective-permute-done((bf16[64,2,16,128]{3,2,1,0:T(8,128)(2,1)S(1)}, bf16[64,2,16,128]{3,2,1,0:T(8,128)(2,1)S(1)}, u32[]{:S(2)}, u32[]{:S(2)}) %collective-permute-start.8) | collective-permute-done | bytes 524320 | tf_op jit(solution)/shard_map/ppermute | solution.py:211
  75.5 5.8 %collective-permute-start.9 = (bf16[64,2,16,128]{3,2,1,0:T(8,128)(2,1)S(1)}, bf16[64,2,16,128]{3,2,1,0:T(8,128)(2,1)S(1)}, u32[]{:S(2)}, u32[]{:S(2)}) collective-permute-start(bf16[64,2,16,128]{3,2,1,0:T(8,128)(2,1)S(1)} %collective-permute-done.8.rest_6_), channel_id=1, source_target_pairs={{0,1},{1,0},{2,3},{3,2},{4,5},{5,4},{6,7},{7,6},{8,9},{9,8},{10,11... | collective-permute-start | bytes 1572872 | tf_op jit(solution)/shard_map/ppermute | solution.py:212
  81.3 0.0 collective-permute-done.6.rest_4_
  81.3 1.9 %collective-permute-start.7 = (bf16[64,2,16,128]{3,2,1,0:T(8,128)(2,1)S(1)}, bf16[64,2,16,128]{3,2,1,0:T(8,128)(2,1)}, u32[]{:S(2)}, u32[]{:S(2)}) collective-permute-start(bf16[64,2,16,128]{3,2,1,0:T(8,128)(2,1)S(1)} %collective-permute-done.6.rest_4_), channel_id=1, source_target_pairs={{0,1},{1,0},{2,3},{3,2},{4,5},{5,4},{6,7},{7,6},{8,9},{9,8},{10,11... | collective-permute-start | bytes 1572872 | tf_op jit(solution)/shard_map/ppermute | solution.py:212
  83.2 0.0 collective-permute-done.4.rest_2_
  83.3 2.4 %collective-permute-start.5 = (bf16[64,2,16,128]{3,2,1,0:T(8,128)(2,1)S(1)}, bf16[64,2,16,128]{3,2,1,0:T(8,128)(2,1)}, u32[]{:S(2)}, u32[]{:S(2)}) collective-permute-start(bf16[64,2,16,128]{3,2,1,0:T(8,128)(2,1)S(1)} %collective-permute-done.4.rest_2_), channel_id=1, source_target_pairs={{0,1},{1,0},{2,3},{3,2},{4,5},{5,4},{6,7},{7,6},{8,9},{9,8},{10,11... | collective-permute-start | bytes 1572872 | tf_op jit(solution)/shard_map/ppermute | solution.py:212
  85.7 0.0 copy-start
  85.7 0.0 copy-start.1
  85.7 0.1 pad_add_fusion.place
  85.8 0.0 collective-permute-done.3.rest_1_
  85.8 0.0 all-to-all-done.1.q_ref
  85.8 1.5 %collective-permute-done.5.rest_3_ = bf16[64,2,16,128]{3,2,1,0:T(8,128)(2,1)} collective-permute-done((bf16[64,2,16,128]{3,2,1,0:T(8,128)(2,1)S(1)}, bf16[64,2,16,128]{3,2,1,0:T(8,128)(2,1)}, u32[]{:S(2)}, u32[]{:S(2)}) %collective-permute-start.5) | collective-permute-done | bytes 524320 | tf_op jit(solution)/shard_map/ppermute | solution.py:212
  87.3 9.7 %shard_map.56 = bf16[64,16,128]{2,1,0:T(8,128)(2,1)S(1)} custom-call(s32[4]{0:T(128)S(1)} %pad_add_fusion.place, s32[8,8]{1,0:T(8,128)S(1)} %copy-done, s32[8]{0:T(128)S(1)} %copy-done.1, bf16[16,4,16,128]{3,2,1,0:T(8,128)(2,1)S(1)} %all-to-all-done.1.q_ref, bf16[64,2,16,128]{3,2,1,0:T(8,128)(2,1)S(1)} %all-to-all-done.rest_0_, ...), custom_call_target="tpu_custom_call" | custom-call | flops 4294967296 | bytes 5242880 | tf_op jit(solution)/shard_map/pallas_call | solution.py:137
  97.0 28.3 %all_to_all.15 = bf16[64,16,128]{2,1,0:T(8,128)(2,1)S(1)} all-to-all(bf16[64,16,128]{2,1,0:T(8,128)(2,1)S(1)} %shard_map.56), channel_id=1, replica_groups=mesh['y'=4,'x_lo'=2,'x_hi'=2,'z'=16,'core'=2] {'y','z'}, dimensions={0} | all-to-all | bytes 524288 | tf_op jit(solution)/shard_map/all_to_all | solution.py:194
  125.3 0.1 copy.8
  125.3 0.8 reshape.12
  (8 shorter events, 0.1 us)
Async XLA Ops:
  1.9 19.4 %copy-start.2 = (bf16[1,16,8192]{2,1,0:T(8,128)(2,1)S(1)}, bf16[1,16,8192]{2,1,0:T(8,128)(2,1)}, u32[]{:S(2)}) copy-start(bf16[1,16,8192]{2,1,0:T(8,128)(2,1)} %param.5) | copy-start | bytes 786436
  1.9 48.8 %all-to-all-start = ((bf16[64,2,16,128]{3,2,1,0:T(8,128)(2,1)}), bf16[64,2,16,128]{3,2,1,0:T(8,128)(2,1)S(1)}, u32[]{:S(2)}, u32[]{:S(2)}) async-start(bf16[64,2,16,128]{3,2,1,0:T(8,128)(2,1)} %shard_map.55), calls=%async_computation | async-start | bytes 1048576 | tf_op jit(solution)/shard_map/all_to_all | solution.py:194
  21.6 9.0 %collective-permute-start.2 = (bf16[16,16,128]{2,1,0:T(8,128)(2,1)S(1)}, bf16[16,16,128]{2,1,0:T(8,128)(2,1)S(1)}, u32[]{:S(2)}, u32[]{:S(2)}) collective-permute-start(bf16[16,16,128]{2,1,0:T(8,128)(2,1)S(1)} %get-tuple-element.10), channel_id=1, source_target_pairs={{0,384},{128,256},{256,128},{384,0},{1,385},{129,257},{257,129},{3... | collective-permute-start | bytes 196616 | tf_op jit(solution)/shard_map/ppermute | solution.py:204
  26.0 7.1 %collective-permute-start.1 = (bf16[16,16,128]{2,1,0:T(8,128)(2,1)S(1)}, bf16[16,16,128]{2,1,0:T(8,128)(2,1)S(1)}, u32[]{:S(2)}, u32[]{:S(2)}) collective-permute-start(bf16[16,16,128]{2,1,0:T(8,128)(2,1)S(1)} %get-tuple-element.11), channel_id=1, source_target_pairs={{0,256},{128,384},{256,0},{384,128},{1,257},{129,385},{257,1},{385... | collective-permute-start | bytes 196616 | tf_op jit(solution)/shard_map/ppermute | solution.py:204
  28.3 5.5 %collective-permute-start = (bf16[16,16,128]{2,1,0:T(8,128)(2,1)S(1)}, bf16[16,16,128]{2,1,0:T(8,128)(2,1)S(1)}, u32[]{:S(2)}, u32[]{:S(2)}) collective-permute-start(bf16[16,16,128]{2,1,0:T(8,128)(2,1)S(1)} %get-tuple-element.12), channel_id=1, source_target_pairs={{0,128},{128,0},{256,384},{384,256},{1,129},{129,1},{257,385},{385... | collective-permute-start | bytes 196616 | tf_op jit(solution)/shard_map/ppermute | solution.py:204
  50.7 24.8 %collective-permute-start.8 = (bf16[64,2,16,128]{3,2,1,0:T(8,128)(2,1)S(1)}, bf16[64,2,16,128]{3,2,1,0:T(8,128)(2,1)S(1)}, u32[]{:S(2)}, u32[]{:S(2)}) collective-permute-start(bf16[64,2,16,128]{3,2,1,0:T(8,128)(2,1)S(1)} %all-to-all-done.rest_0_), channel_id=1, source_target_pairs={{0,96},{64,32},{32,64},{96,0},{1,97},{65,33},{33,65},{97,1},{2,98}... | collective-permute-start | bytes 1572872 | tf_op jit(solution)/shard_map/ppermute | solution.py:211
  55.1 26.2 %collective-permute-start.6 = (bf16[64,2,16,128]{3,2,1,0:T(8,128)(2,1)S(1)}, bf16[64,2,16,128]{3,2,1,0:T(8,128)(2,1)S(1)}, u32[]{:S(2)}, u32[]{:S(2)}) collective-permute-start(bf16[64,2,16,128]{3,2,1,0:T(8,128)(2,1)S(1)} %all-to-all-done.rest_0_), channel_id=1, source_target_pairs={{0,32},{64,96},{32,0},{96,64},{1,33},{65,97},{33,1},{97,65},{2,34}... | collective-permute-start | bytes 1572872 | tf_op jit(solution)/shard_map/ppermute | solution.py:211
  57.6 25.7 %collective-permute-start.4 = (bf16[64,2,16,128]{3,2,1,0:T(8,128)(2,1)S(1)}, bf16[64,2,16,128]{3,2,1,0:T(8,128)(2,1)S(1)}, u32[]{:S(2)}, u32[]{:S(2)}) collective-permute-start(bf16[64,2,16,128]{3,2,1,0:T(8,128)(2,1)S(1)} %all-to-all-done.rest_0_), channel_id=1, source_target_pairs={{0,64},{64,0},{32,96},{96,32},{1,65},{65,1},{33,97},{97,33},{2,66}... | collective-permute-start | bytes 1572872 | tf_op jit(solution)/shard_map/ppermute | solution.py:211
  59.7 26.1 %all-to-all-start.1 = ((bf16[16,4,16,128]{3,2,1,0:T(8,128)(2,1)}), bf16[16,4,16,128]{3,2,1,0:T(8,128)(2,1)S(1)}, u32[]{:S(2)}, u32[]{:S(2)}) async-start(bf16[16,4,16,128]{3,2,1,0:T(8,128)(2,1)} %pad_maximum_fusion), calls=%async_computation.1 | async-start | bytes 524288 | tf_op jit(solution)/shard_map/all_to_all | solution.py:207
  66.5 19.3 %collective-permute-start.3 = (bf16[64,2,16,128]{3,2,1,0:T(8,128)(2,1)S(1)}, bf16[64,2,16,128]{3,2,1,0:T(8,128)(2,1)S(1)}, u32[]{:S(2)}, u32[]{:S(2)}) collective-permute-start(bf16[64,2,16,128]{3,2,1,0:T(8,128)(2,1)S(1)} %all-to-all-done.rest_0_), channel_id=1, source_target_pairs={{0,1},{1,0},{2,3},{3,2},{4,5},{5,4},{6,7},{7,6},{8,9},{9,8},{10,11... | collective-permute-start | bytes 1572872 | tf_op jit(solution)/shard_map/ppermute | solution.py:212
  75.5 10.3 %collective-permute-start.9 = (bf16[64,2,16,128]{3,2,1,0:T(8,128)(2,1)S(1)}, bf16[64,2,16,128]{3,2,1,0:T(8,128)(2,1)S(1)}, u32[]{:S(2)}, u32[]{:S(2)}) collective-permute-start(bf16[64,2,16,128]{3,2,1,0:T(8,128)(2,1)S(1)} %collective-permute-done.8.rest_6_), channel_id=1, source_target_pairs={{0,1},{1,0},{2,3},{3,2},{4,5},{5,4},{6,7},{7,6},{8,9},{9,8},{10,11... | collective-permute-start | bytes 1572872 | tf_op jit(solution)/shard_map/ppermute | solution.py:212
  81.3 4.5 %collective-permute-start.7 = (bf16[64,2,16,128]{3,2,1,0:T(8,128)(2,1)S(1)}, bf16[64,2,16,128]{3,2,1,0:T(8,128)(2,1)}, u32[]{:S(2)}, u32[]{:S(2)}) collective-permute-start(bf16[64,2,16,128]{3,2,1,0:T(8,128)(2,1)S(1)} %collective-permute-done.6.rest_4_), channel_id=1, source_target_pairs={{0,1},{1,0},{2,3},{3,2},{4,5},{5,4},{6,7},{7,6},{8,9},{9,8},{10,11... | collective-permute-start | bytes 1572872 | tf_op jit(solution)/shard_map/ppermute | solution.py:212
  83.3 4.1 %collective-permute-start.5 = (bf16[64,2,16,128]{3,2,1,0:T(8,128)(2,1)S(1)}, bf16[64,2,16,128]{3,2,1,0:T(8,128)(2,1)}, u32[]{:S(2)}, u32[]{:S(2)}) collective-permute-start(bf16[64,2,16,128]{3,2,1,0:T(8,128)(2,1)S(1)} %collective-permute-done.4.rest_2_), channel_id=1, source_target_pairs={{0,1},{1,0},{2,3},{3,2},{4,5},{5,4},{6,7},{7,6},{8,9},{9,8},{10,11... | collective-permute-start | bytes 1572872 | tf_op jit(solution)/shard_map/ppermute | solution.py:212
  85.7 1.6 %copy-start = (s32[8,8]{1,0:T(8,128)S(1)}, s32[8,8]{1,0:T(8,128)}, u32[]{:S(2)}) copy-start(s32[8,8]{1,0:T(8,128)} %mask.1) | copy-start | bytes 772
  85.7 1.6 %copy-start.1 = (s32[8]{0:T(128)S(1)}, s32[8]{0:T(128)}, u32[]{:S(2)}) copy-start(s32[8]{0:T(128)} %counts.1) | copy-start | bytes 100

commit v10 on v9

--- a/solution.py
+++ b/solution.py
@@ -25,7 +25,7 @@
             for e in range(2):
                 copies[d, e, part] = pltpu.make_async_copy(
                     pieces[2 * d + e].at[:, part],
-                    buf.at[d % 2, x_hi ^ (d // 2), core ^ e],
+                    buf.at[d % 2, (x_hi * 2 + x_lo + d) % 4 // 2, core ^ e],
                     sems.at[2 * d + e, part],
                 )
     for side in range(2):
@@ -176,11 +176,11 @@
     )(keys, values)
 
 
-def x_pairs(flip):
+def ring(step):
     def index(x):
         return x % 2 * 2 + x // 2
 
-    return [(index(x), index(x ^ flip)) for x in range(4)]
+    return [(index(x), index((x + step) % 4)) for x in range(4)]
 
 
 def per_device(queries, keys, values, span_mask, span_counts):
@@ -208,7 +208,7 @@
 
     x_axes = ("x_lo", "x_hi")
     pieces = []
-    for piece in [kv] + [lax.ppermute(kv, x_axes, x_pairs(flip)) for flip in (1, 3, 2)]:
+    for piece in [kv] + [lax.ppermute(kv, x_axes, ring(step)) for step in (-1, 1, 2)]:
         pieces += [piece, lax.ppermute(piece, "core", [(0, 1), (1, 0)])]
     pieces = pieces[:4] + pieces[6:] + pieces[4:6]
     place = jnp.stack([lax.axis_index(name) for name in ("x_lo", "x_hi", "core", "y")])

time: 127 us -> 126 us (level)
  the two profiles are of different devices: /device:TPU:1 before, /device:TPU:2 now
where the time goes in v10:
time: 126 us; the launch traced here: 125 us
  starting transfers between devices  52.6 us (42%)
  waiting for transfers between devices  29.7 us (24%)
  blocking collectives  29.6 us (23%)
  Pallas kernels  10.8 us (9%)
    all_to_all x1, blocking collectives, exchange(): lax.all_to_all(array, ('y', 'z'), split_axis=0, concat_axis=0, tiled=True)  29.6 us
    all_to_all x1, starting transfers between devices, exchange(): lax.all_to_all(array, ('y', 'z'), split_axis=0, concat_axis=0, tiled=True)  18.9 us
    all_to_all x1, waiting for transfers between devices, exchange(): lax.all_to_all(array, ('y', 'z'), split_axis=0, concat_axis=0, tiled=True)  16.5 us
    ppermute x3, starting transfers between devices, per_device(): lax.ppermute(kv, x_axes, ring(step))  10.5 us
    ppermute x3, starting transfers between devices, per_device(): part = lax.ppermute(part, 'y', [(a, a ^ d) for a in range(n_y)])  9.82 us
    pallas_call x1, Pallas kernels, attend(): pl.pallas_call(attend_kernel, out_shape=jax.ShapeDtypeStruct((64, 16, HD)...  8.86 us
    ppermute x4, starting transfers between devices, per_device(): pieces += [piece, lax.ppermute(piece, 'core', [(0, 1), (1, 0)])]  8.15 us
    ppermute x3, waiting for transfers between devices, per_device(): lax.ppermute(kv, x_axes, ring(step))  6.72 us
  transfers between devices with their start and end apart: 12, of which 6 were waited for; matrix products, arithmetic and copies ran while one was open for 1% of the time, Pallas kernels for 0%

profile of v10, /device:TPU:2, one launch (start us, length us, event | category | flops | bytes accessed | tf_op | source)
XLA Modules:
  0.0 125.0 jit_solution(1941644136821459400)
XLA Ops:
  0.0 1.9 %shard_map.55 = bf16[64,2,16,128]{3,2,1,0:T(8,128)(2,1)} custom-call(bf16[16,8192]{1,0:T(8,128)(2,1)} %bitcast.28, bf16[16,8192]{1,0:T(8,128)(2,1)} %bitcast.29), custom_call_target="tpu_custom_call" | custom-call | tf_op jit(solution)/shard_map/pallas_call | solution.py:171
  1.9 18.9 %all-to-all-start = ((bf16[64,2,16,128]{3,2,1,0:T(8,128)(2,1)}), bf16[64,2,16,128]{3,2,1,0:T(8,128)(2,1)S(1)}, u32[]{:S(2)}, u32[]{:S(2)}) async-start(bf16[64,2,16,128]{3,2,1,0:T(8,128)(2,1)} %shard_map.55), calls=%async_computation | async-start | bytes 1048576 | tf_op jit(solution)/shard_map/all_to_all | solution.py:194
  20.9 0.2 copy.7
  21.1 4.9 %collective-permute-start.2 = (bf16[16,16,128]{2,1,0:T(8,128)(2,1)S(1)}, bf16[16,16,128]{2,1,0:T(8,128)(2,1)S(1)}, u32[]{:S(2)}, u32[]{:S(2)}) collective-permute-start(bf16[16,16,128]{2,1,0:T(8,128)(2,1)S(1)} %get-tuple-element.10), channel_id=1, source_target_pairs={{0,384},{128,256},{256,128},{384,0},{1,385},{129,257},{257,129},{3... | collective-permute-start | bytes 196616 | tf_op jit(solution)/shard_map/ppermute | solution.py:204
  26.0 2.6 %collective-permute-start.1 = (bf16[16,16,128]{2,1,0:T(8,128)(2,1)S(1)}, bf16[16,16,128]{2,1,0:T(8,128)(2,1)S(1)}, u32[]{:S(2)}, u32[]{:S(2)}) collective-permute-start(bf16[16,16,128]{2,1,0:T(8,128)(2,1)S(1)} %get-tuple-element.11), channel_id=1, source_target_pairs={{0,256},{128,384},{256,0},{384,128},{1,257},{129,385},{257,1},{385... | collective-permute-start | bytes 196616 | tf_op jit(solution)/shard_map/ppermute | solution.py:204
  28.6 2.4 %collective-permute-start = (bf16[16,16,128]{2,1,0:T(8,128)(2,1)S(1)}, bf16[16,16,128]{2,1,0:T(8,128)(2,1)S(1)}, u32[]{:S(2)}, u32[]{:S(2)}) collective-permute-start(bf16[16,16,128]{2,1,0:T(8,128)(2,1)S(1)} %get-tuple-element.12), channel_id=1, source_target_pairs={{0,128},{128,0},{256,384},{384,256},{1,129},{129,1},{257,385},{385... | collective-permute-start | bytes 196616 | tf_op jit(solution)/shard_map/ppermute | solution.py:204
  30.9 0.0 collective-permute-done.2
  30.9 3.3 %collective-permute-done.1 = bf16[16,16,128]{2,1,0:T(8,128)(2,1)S(1)} collective-permute-done((bf16[16,16,128]{2,1,0:T(8,128)(2,1)S(1)}, bf16[16,16,128]{2,1,0:T(8,128)(2,1)S(1)}, u32[]{:S(2)}, u32[]{:S(2)}) %collective-permute-start.1) | collective-permute-done | bytes 65568 | tf_op jit(solution)/shard_map/ppermute | solution.py:204
  34.3 1.0 collective-permute-done
  35.3 0.7 pad_maximum_fusion
  36.0 16.5 %all-to-all-done.rest_0_ = bf16[64,2,16,128]{3,2,1,0:T(8,128)(2,1)S(1)} async-done(((bf16[64,2,16,128]{3,2,1,0:T(8,128)(2,1)}), bf16[64,2,16,128]{3,2,1,0:T(8,128)(2,1)S(1)}, u32[]{:S(2)}, u32[]{:S(2)}) %all-to-all-start) | async-done | bytes 524320 | tf_op jit(solution)/shard_map/all_to_all | solution.py:194
  52.5 3.4 %collective-permute-start.8 = (bf16[64,2,16,128]{3,2,1,0:T(8,128)(2,1)S(1)}, bf16[64,2,16,128]{3,2,1,0:T(8,128)(2,1)S(1)}, u32[]{:S(2)}, u32[]{:S(2)}) collective-permute-start(bf16[64,2,16,128]{3,2,1,0:T(8,128)(2,1)S(1)} %all-to-all-done.rest_0_), channel_id=1, source_target_pairs={{0,64},{64,32},{32,96},{96,0},{1,65},{65,33},{33,97},{97,1},{2,66}... | collective-permute-start | bytes 1572872 | tf_op jit(solution)/shard_map/ppermute | solution.py:211
  55.9 3.0 %collective-permute-start.6 = (bf16[64,2,16,128]{3,2,1,0:T(8,128)(2,1)S(1)}, bf16[64,2,16,128]{3,2,1,0:T(8,128)(2,1)S(1)}, u32[]{:S(2)}, u32[]{:S(2)}) collective-permute-start(bf16[64,2,16,128]{3,2,1,0:T(8,128)(2,1)S(1)} %all-to-all-done.rest_0_), channel_id=1, source_target_pairs={{0,32},{64,96},{32,0},{96,64},{1,33},{65,97},{33,1},{97,65},{2,34}... | collective-permute-start | bytes 1572872 | tf_op jit(solution)/shard_map/ppermute | solution.py:211
  58.9 4.1 %collective-permute-start.4 = (bf16[64,2,16,128]{3,2,1,0:T(8,128)(2,1)S(1)}, bf16[64,2,16,128]{3,2,1,0:T(8,128)(2,1)S(1)}, u32[]{:S(2)}, u32[]{:S(2)}) collective-permute-start(bf16[64,2,16,128]{3,2,1,0:T(8,128)(2,1)S(1)} %all-to-all-done.rest_0_), channel_id=1, source_target_pairs={{0,96},{64,0},{32,64},{96,32},{1,97},{65,1},{33,65},{97,33},{2,98}... | collective-permute-start | bytes 1572872 | tf_op jit(solution)/shard_map/ppermute | solution.py:211
  63.0 5.3 %all-to-all-start.1 = ((bf16[16,4,16,128]{3,2,1,0:T(8,128)(2,1)}), bf16[16,4,16,128]{3,2,1,0:T(8,128)(2,1)S(1)}, u32[]{:S(2)}, u32[]{:S(2)}) async-start(bf16[16,4,16,128]{3,2,1,0:T(8,128)(2,1)} %pad_maximum_fusion), calls=%async_computation.1 | async-start | bytes 524288 | tf_op jit(solution)/shard_map/all_to_all | solution.py:207
  68.3 1.9 %collective-permute-start.3 = (bf16[64,2,16,128]{3,2,1,0:T(8,128)(2,1)S(1)}, bf16[64,2,16,128]{3,2,1,0:T(8,128)(2,1)S(1)}, u32[]{:S(2)}, u32[]{:S(2)}) collective-permute-start(bf16[64,2,16,128]{3,2,1,0:T(8,128)(2,1)S(1)} %all-to-all-done.rest_0_), channel_id=1, source_target_pairs={{0,1},{1,0},{2,3},{3,2},{4,5},{5,4},{6,7},{7,6},{8,9},{9,8},{10,11... | collective-permute-start | bytes 1572872 | tf_op jit(solution)/shard_map/ppermute | solution.py:212
  70.3 0.0 collective-permute-done.8.rest_6_
  70.3 2.4 %collective-permute-start.9 = (bf16[64,2,16,128]{3,2,1,0:T(8,128)(2,1)S(1)}, bf16[64,2,16,128]{3,2,1,0:T(8,128)(2,1)S(1)}, u32[]{:S(2)}, u32[]{:S(2)}) collective-permute-start(bf16[64,2,16,128]{3,2,1,0:T(8,128)(2,1)S(1)} %collective-permute-done.8.rest_6_), channel_id=1, source_target_pairs={{0,1},{1,0},{2,3},{3,2},{4,5},{5,4},{6,7},{7,6},{8,9},{9,8},{10,11... | collective-permute-start | bytes 1572872 | tf_op jit(solution)/shard_map/ppermute | solution.py:212
  72.7 1.5 %collective-permute-done.6.rest_4_ = bf16[64,2,16,128]{3,2,1,0:T(8,128)(2,1)S(1)} collective-permute-done((bf16[64,2,16,128]{3,2,1,0:T(8,128)(2,1)S(1)}, bf16[64,2,16,128]{3,2,1,0:T(8,128)(2,1)S(1)}, u32[]{:S(2)}, u32[]{:S(2)}) %collective-permute-start.6) | collective-permute-done | bytes 524320 | tf_op jit(solution)/shard_map/ppermute | solution.py:211
  74.1 1.9 %collective-permute-start.7 = (bf16[64,2,16,128]{3,2,1,0:T(8,128)(2,1)S(1)}, bf16[64,2,16,128]{3,2,1,0:T(8,128)(2,1)}, u32[]{:S(2)}, u32[]{:S(2)}) collective-permute-start(bf16[64,2,16,128]{3,2,1,0:T(8,128)(2,1)S(1)} %collective-permute-done.6.rest_4_), channel_id=1, source_target_pairs={{0,1},{1,0},{2,3},{3,2},{4,5},{5,4},{6,7},{7,6},{8,9},{9,8},{10,11... | collective-permute-start | bytes 1572872 | tf_op jit(solution)/shard_map/ppermute | solution.py:212
  76.1 5.3 %collective-permute-done.4.rest_2_ = bf16[64,2,16,128]{3,2,1,0:T(8,128)(2,1)S(1)} collective-permute-done((bf16[64,2,16,128]{3,2,1,0:T(8,128)(2,1)S(1)}, bf16[64,2,16,128]{3,2,1,0:T(8,128)(2,1)S(1)}, u32[]{:S(2)}, u32[]{:S(2)}) %collective-permute-start.4) | collective-permute-done | bytes 524320 | tf_op jit(solution)/shard_map/ppermute | solution.py:211
  81.3 1.9 %collective-permute-start.5 = (bf16[64,2,16,128]{3,2,1,0:T(8,128)(2,1)S(1)}, bf16[64,2,16,128]{3,2,1,0:T(8,128)(2,1)}, u32[]{:S(2)}, u32[]{:S(2)}) collective-permute-start(bf16[64,2,16,128]{3,2,1,0:T(8,128)(2,1)S(1)} %collective-permute-done.4.rest_2_), channel_id=1, source_target_pairs={{0,1},{1,0},{2,3},{3,2},{4,5},{5,4},{6,7},{7,6},{8,9},{9,8},{10,11... | collective-permute-start | bytes 1572872 | tf_op jit(solution)/shard_map/ppermute | solution.py:212
  83.2 0.0 copy-start
  83.3 0.0 copy-start.1
  83.3 0.1 pad_add_fusion.place
  83.3 0.0 collective-permute-done.3.rest_1_
  83.4 2.2 %all-to-all-done.1.q_ref = bf16[16,4,16,128]{3,2,1,0:T(8,128)(2,1)S(1)} async-done(((bf16[16,4,16,128]{3,2,1,0:T(8,128)(2,1)}), bf16[16,4,16,128]{3,2,1,0:T(8,128)(2,1)S(1)}, u32[]{:S(2)}, u32[]{:S(2)}) %all-to-all-start.1) | async-done | bytes 262176 | tf_op jit(solution)/shard_map/all_to_all | solution.py:207
  85.5 0.0 collective-permute-done.9.rest_7_
  85.6 8.9 %shard_map.56 = bf16[64,16,128]{2,1,0:T(8,128)(2,1)S(1)} custom-call(s32[4]{0:T(128)S(1)} %pad_add_fusion.place, s32[8,8]{1,0:T(8,128)S(1)} %copy-done, s32[8]{0:T(128)S(1)} %copy-done.1, bf16[16,4,16,128]{3,2,1,0:T(8,128)(2,1)S(1)} %all-to-all-done.1.q_ref, bf16[64,2,16,128]{3,2,1,0:T(8,128)(2,1)S(1)} %all-to-all-done.rest_0_, ...), custom_call_target="tpu_custom_call" | custom-call | flops 4294967296 | bytes 5242880 | tf_op jit(solution)/shard_map/pallas_call | solution.py:137
  94.4 29.6 %all_to_all.15 = bf16[64,16,128]{2,1,0:T(8,128)(2,1)S(1)} all-to-all(bf16[64,16,128]{2,1,0:T(8,128)(2,1)S(1)} %shard_map.56), channel_id=1, replica_groups=mesh['y'=4,'x_lo'=2,'x_hi'=2,'z'=16,'core'=2] {'y','z'}, dimensions={0} | all-to-all | bytes 524288 | tf_op jit(solution)/shard_map/all_to_all | solution.py:194
  124.1 0.1 copy.8
  124.2 0.8 reshape.12
  (8 shorter events, 0.1 us)
Async XLA Ops:
  1.9 18.9 %copy-start.2 = (bf16[1,16,8192]{2,1,0:T(8,128)(2,1)S(1)}, bf16[1,16,8192]{2,1,0:T(8,128)(2,1)}, u32[]{:S(2)}) copy-start(bf16[1,16,8192]{2,1,0:T(8,128)(2,1)} %param.5) | copy-start | bytes 786436
  1.9 50.6 %all-to-all-start = ((bf16[64,2,16,128]{3,2,1,0:T(8,128)(2,1)}), bf16[64,2,16,128]{3,2,1,0:T(8,128)(2,1)S(1)}, u32[]{:S(2)}, u32[]{:S(2)}) async-start(bf16[64,2,16,128]{3,2,1,0:T(8,128)(2,1)} %shard_map.55), calls=%async_computation | async-start | bytes 1048576 | tf_op jit(solution)/shard_map/all_to_all | solution.py:194
  21.1 9.8 %collective-permute-start.2 = (bf16[16,16,128]{2,1,0:T(8,128)(2,1)S(1)}, bf16[16,16,128]{2,1,0:T(8,128)(2,1)S(1)}, u32[]{:S(2)}, u32[]{:S(2)}) collective-permute-start(bf16[16,16,128]{2,1,0:T(8,128)(2,1)S(1)} %get-tuple-element.10), channel_id=1, source_target_pairs={{0,384},{128,256},{256,128},{384,0},{1,385},{129,257},{257,129},{3... | collective-permute-start | bytes 196616 | tf_op jit(solution)/shard_map/ppermute | solution.py:204
  26.0 8.3 %collective-permute-start.1 = (bf16[16,16,128]{2,1,0:T(8,128)(2,1)S(1)}, bf16[16,16,128]{2,1,0:T(8,128)(2,1)S(1)}, u32[]{:S(2)}, u32[]{:S(2)}) collective-permute-start(bf16[16,16,128]{2,1,0:T(8,128)(2,1)S(1)} %get-tuple-element.11), channel_id=1, source_target_pairs={{0,256},{128,384},{256,0},{384,128},{1,257},{129,385},{257,1},{385... | collective-permute-start | bytes 196616 | tf_op jit(solution)/shard_map/ppermute | solution.py:204
  28.6 6.7 %collective-permute-start = (bf16[16,16,128]{2,1,0:T(8,128)(2,1)S(1)}, bf16[16,16,128]{2,1,0:T(8,128)(2,1)S(1)}, u32[]{:S(2)}, u32[]{:S(2)}) collective-permute-start(bf16[16,16,128]{2,1,0:T(8,128)(2,1)S(1)} %get-tuple-element.12), channel_id=1, source_target_pairs={{0,128},{128,0},{256,384},{384,256},{1,129},{129,1},{257,385},{385... | collective-permute-start | bytes 196616 | tf_op jit(solution)/shard_map/ppermute | solution.py:204
  52.5 17.8 %collective-permute-start.8 = (bf16[64,2,16,128]{3,2,1,0:T(8,128)(2,1)S(1)}, bf16[64,2,16,128]{3,2,1,0:T(8,128)(2,1)S(1)}, u32[]{:S(2)}, u32[]{:S(2)}) collective-permute-start(bf16[64,2,16,128]{3,2,1,0:T(8,128)(2,1)S(1)} %all-to-all-done.rest_0_), channel_id=1, source_target_pairs={{0,64},{64,32},{32,96},{96,0},{1,65},{65,33},{33,97},{97,1},{2,66}... | collective-permute-start | bytes 1572872 | tf_op jit(solution)/shard_map/ppermute | solution.py:211
  55.9 18.3 %collective-permute-start.6 = (bf16[64,2,16,128]{3,2,1,0:T(8,128)(2,1)S(1)}, bf16[64,2,16,128]{3,2,1,0:T(8,128)(2,1)S(1)}, u32[]{:S(2)}, u32[]{:S(2)}) collective-permute-start(bf16[64,2,16,128]{3,2,1,0:T(8,128)(2,1)S(1)} %all-to-all-done.rest_0_), channel_id=1, source_target_pairs={{0,32},{64,96},{32,0},{96,64},{1,33},{65,97},{33,1},{97,65},{2,34}... | collective-permute-start | bytes 1572872 | tf_op jit(solution)/shard_map/ppermute | solution.py:211
  58.9 22.4 %collective-permute-start.4 = (bf16[64,2,16,128]{3,2,1,0:T(8,128)(2,1)S(1)}, bf16[64,2,16,128]{3,2,1,0:T(8,128)(2,1)S(1)}, u32[]{:S(2)}, u32[]{:S(2)}) collective-permute-start(bf16[64,2,16,128]{3,2,1,0:T(8,128)(2,1)S(1)} %all-to-all-done.rest_0_), channel_id=1, source_target_pairs={{0,96},{64,0},{32,64},{96,32},{1,97},{65,1},{33,65},{97,33},{2,98}... | collective-permute-start | bytes 1572872 | tf_op jit(solution)/shard_map/ppermute | solution.py:211
  63.0 22.6 %all-to-all-start.1 = ((bf16[16,4,16,128]{3,2,1,0:T(8,128)(2,1)}), bf16[16,4,16,128]{3,2,1,0:T(8,128)(2,1)S(1)}, u32[]{:S(2)}, u32[]{:S(2)}) async-start(bf16[16,4,16,128]{3,2,1,0:T(8,128)(2,1)} %pad_maximum_fusion), calls=%async_computation.1 | async-start | bytes 524288 | tf_op jit(solution)/shard_map/all_to_all | solution.py:207
  68.3 15.0 %collective-permute-start.3 = (bf16[64,2,16,128]{3,2,1,0:T(8,128)(2,1)S(1)}, bf16[64,2,16,128]{3,2,1,0:T(8,128)(2,1)S(1)}, u32[]{:S(2)}, u32[]{:S(2)}) collective-permute-start(bf16[64,2,16,128]{3,2,1,0:T(8,128)(2,1)S(1)} %all-to-all-done.rest_0_), channel_id=1, source_target_pairs={{0,1},{1,0},{2,3},{3,2},{4,5},{5,4},{6,7},{7,6},{8,9},{9,8},{10,11... | collective-permute-start | bytes 1572872 | tf_op jit(solution)/shard_map/ppermute | solution.py:212
  70.3 15.3 %collective-permute-start.9 = (bf16[64,2,16,128]{3,2,1,0:T(8,128)(2,1)S(1)}, bf16[64,2,16,128]{3,2,1,0:T(8,128)(2,1)S(1)}, u32[]{:S(2)}, u32[]{:S(2)}) collective-permute-start(bf16[64,2,16,128]{3,2,1,0:T(8,128)(2,1)S(1)} %collective-permute-done.8.rest_6_), channel_id=1, source_target_pairs={{0,1},{1,0},{2,3},{3,2},{4,5},{5,4},{6,7},{7,6},{8,9},{9,8},{10,11... | collective-permute-start | bytes 1572872 | tf_op jit(solution)/shard_map/ppermute | solution.py:212
  74.1 11.4 %collective-permute-start.7 = (bf16[64,2,16,128]{3,2,1,0:T(8,128)(2,1)S(1)}, bf16[64,2,16,128]{3,2,1,0:T(8,128)(2,1)}, u32[]{:S(2)}, u32[]{:S(2)}) collective-permute-start(bf16[64,2,16,128]{3,2,1,0:T(8,128)(2,1)S(1)} %collective-permute-done.6.rest_4_), channel_id=1, source_target_pairs={{0,1},{1,0},{2,3},{3,2},{4,5},{5,4},{6,7},{7,6},{8,9},{9,8},{10,11... | collective-permute-start | bytes 1572872 | tf_op jit(solution)/shard_map/ppermute | solution.py:212
  81.3 4.2 %collective-permute-start.5 = (bf16[64,2,16,128]{3,2,1,0:T(8,128)(2,1)S(1)}, bf16[64,2,16,128]{3,2,1,0:T(8,128)(2,1)}, u32[]{:S(2)}, u32[]{:S(2)}) collective-permute-start(bf16[64,2,16,128]{3,2,1,0:T(8,128)(2,1)S(1)} %collective-permute-done.4.rest_2_), channel_id=1, source_target_pairs={{0,1},{1,0},{2,3},{3,2},{4,5},{5,4},{6,7},{7,6},{8,9},{9,8},{10,11... | collective-permute-start | bytes 1572872 | tf_op jit(solution)/shard_map/ppermute | solution.py:212
  83.2 2.3 %copy-start = (s32[8,8]{1,0:T(8,128)S(1)}, s32[8,8]{1,0:T(8,128)}, u32[]{:S(2)}) copy-start(s32[8,8]{1,0:T(8,128)} %mask.1) | copy-start | bytes 772
  83.3 2.3 %copy-start.1 = (s32[8]{0:T(128)S(1)}, s32[8]{0:T(128)}, u32[]{:S(2)}) copy-start(s32[8]{0:T(128)} %counts.1) | copy-start | bytes 100

commit v11 on v10

--- a/solution.py
+++ b/solution.py
@@ -13,31 +13,18 @@
 
 def attend_kernel(place, mask, counts, q_ref, *rest):
     pieces = rest[:8]
-    out_ref, q_buf, k_buf, v_buf = rest[8:12]
-    scores, row_tops = rest[12 : 12 + 2 * UNROLL], rest[12 + 2 * UNROLL : 12 + 4 * UNROLL]
-    acc_ref, top_ref, total_ref, todo, sems, q_sem = rest[12 + 4 * UNROLL :]
+    out_ref = rest[8]
+    scores, row_tops = rest[9 : 9 + 2 * UNROLL], rest[9 + 2 * UNROLL : 9 + 4 * UNROLL]
+    acc_ref, top_ref, total_ref, todo = rest[9 + 4 * UNROLL :]
     x_lo, x_hi, core, y = place[0], place[1], place[2], place[3]
-    q_copy = pltpu.make_async_copy(q_ref, q_buf, q_sem)
-    q_copy.start()
-    copies = {}
-    for d in range(4):
-        for part, buf in enumerate((k_buf, v_buf)):
-            for e in range(2):
-                copies[d, e, part] = pltpu.make_async_copy(
-                    pieces[2 * d + e].at[:, part],
-                    buf.at[d % 2, (x_hi * 2 + x_lo + d) % 4 // 2, core ^ e],
-                    sems.at[2 * d + e, part],
-                )
-    for side in range(2):
-        for part in range(2):
-            for d in (side, side + 2):
-                for e in range(2):
-                    copies[d, e, part].start()
-
-    def wait(side, part):
-        for d in (side, side + 2):
-            for e in range(2):
-                copies[d, e, part].wait()
+
+    def slab(side, part, jy):
+        blocks = [
+            pieces[2 * d + e][pl.ds(jy * 16, 16), part].reshape(256, HD)
+            for d in (side, side + 2)
+            for e in range(2)
+        ]
+        return jnp.concatenate(blocks, axis=0)
 
     def list_block(i, n):
         side, iy, jy = i // 16, i // 4 % 4, i % 4
@@ -52,27 +39,27 @@
     total_ref[...] = jnp.zeros_like(total_ref)
     scale = LOG2E / HD**0.5
     row = lax.broadcasted_iota(jnp.int32, (128, 256), 0)
-    late = 768 + row // 16 * 32 + row % 16
-
-    def score(n, slot):
-        i = todo[jnp.minimum(n, count - 1)]
-        side, iy, jy = i // 16, i // 4 % 4, i % 4
+    late = 256 + row // 16 * 32 + row % 16
+
+    def score(n, slot, side, end):
+        i = todo[jnp.minimum(n, end - 1)]
+        iy, jy = i // 4 % 4, i % 4
         live = counts[jy * 2 + (x_lo + side) % 2]
-        q = q_buf[:, y ^ iy].reshape(256, HD)
-        k = k_buf[side, :, :, pl.ds(jy * 16, 16)].reshape(1024, HD)
-        s = lax.dot_general(k, q, (((1,), (1,)), ((), ())), preferred_element_type=jnp.float32)
+        q = q_ref[:, y ^ iy].reshape(256, HD)
+        s = lax.dot_general(
+            slab(side, 0, jy), q, (((1,), (1,)), ((), ())), preferred_element_type=jnp.float32
+        )
         top = None
         for g in range(8):
             a = s[g * 128 : (g + 1) * 128]
-            if g >= 4 and g % 2 == 1:
-                a = jnp.where(late + g // 2 % 2 * 16 < live, a, LOW)
+            if g % 2 == 1:
+                hi = (x_hi * 2 + x_lo + side + g // 4 * 2) % 4 // 2
+                a = jnp.where(late + (hi * 512 + (core ^ (g // 2 % 2)) * 16) < live, a, LOW)
             scores[slot][g * 128 : (g + 1) * 128] = a
             top = a if top is None else jnp.maximum(top, a)
         row_tops[slot][...] = jnp.broadcast_to(jnp.max(top, axis=0, keepdims=True), (8, 256))
 
-    def mix(n, slot):
-        i = todo[jnp.minimum(n, count - 1)]
-        side, jy = i // 16, i % 4
+    def mix(n, slot, side):
         shift = row_tops[slot][:1] * scale
         total, weights = None, []
         for g in range(8):
@@ -80,17 +67,18 @@
             weights.append(w.astype(jnp.bfloat16))
             total = w if total is None else total + w
         total = jnp.sum(total, axis=0, keepdims=True)
-        v = v_buf[side, :, :, pl.ds(jy * 16, 16)].reshape(1024, HD)
         weights = jnp.concatenate(weights, axis=0)
         acc = lax.dot_general(
-            v, weights, (((0,), (0,)), ((), ())), preferred_element_type=jnp.float32
+            slab(side, 1, todo[n] % 4),
+            weights,
+            (((0,), (0,)), ((), ())),
+            preferred_element_type=jnp.float32,
         )
         return row_tops[slot][:1], total, acc
 
     def merge(n, state):
         top, total, acc = state
-        iy = todo[jnp.minimum(n, count - 1)] // 4 % 4
-        top = jnp.where(n < count, top, LOW)
+        iy = todo[n] // 4 % 4
         old = top_ref[iy][:1]
         new = jnp.maximum(old, top)
         keep, add = jnp.exp2((old - new) * scale), jnp.exp2((top - new) * scale)
@@ -98,34 +86,30 @@
         acc_ref[iy] = acc_ref[iy] * keep + acc * add
         top_ref[iy] = jnp.broadcast_to(new, (8, 256))
 
-    def step(n, slot):
-        @pl.when((n + 2 * UNROLL > first) & (n + UNROLL <= first))
-        def _():
-            wait(1, 0)
-            wait(1, 1)
-
-        for u in range(UNROLL):
-            score(n + UNROLL + u, (1 - slot) * UNROLL + u)
-        states = [mix(n + u, slot * UNROLL + u) for u in range(UNROLL)]
-        for u in range(UNROLL):
-            merge(n + u, states[u])
-
-    q_copy.wait()
-    wait(0, 0)
-    for u in range(UNROLL):
-        score(u, u)
-    wait(0, 1)
-
-    def pair(m, _):
-        step(2 * UNROLL * m, 0)
-
-        @pl.when(2 * UNROLL * m + UNROLL < count)
-        def _():
-            step(2 * UNROLL * m + UNROLL, 1)
-
-        return 0
-
-    lax.fori_loop(0, (count + 2 * UNROLL - 1) // (2 * UNROLL), pair, 0)
+    def run(side, begin, end):
+        def step(n, slot):
+            score(n + 1, 1 - slot, side, end)
+            merge(n, mix(n, slot, side))
+
+        def pair(m, _):
+            n = begin + 2 * m
+            step(n, 0)
+
+            @pl.when(n + 1 < end)
+            def _():
+                step(n + 1, 1)
+
+            return 0
+
+        score(begin, 0, side, end)
+        lax.fori_loop(0, (end - begin + 1) // 2, pair, 0)
+
+    run(0, 0, first)
+
+    @pl.when(count > first)
+    def _():
+        run(1, first, count)
+
     for iy in range(4):
         result = (acc_ref[iy] / total_ref[iy][:1]).T.astype(jnp.bfloat16)
         out_ref[iy * 16 : (iy + 1) * 16] = result.reshape(16, 16, HD)
@@ -137,20 +121,15 @@
     return pl.pallas_call(
         attend_kernel,
         out_shape=jax.ShapeDtypeStruct((64, 16, HD), jnp.bfloat16),
-        in_specs=[smem, smem, smem] + [pl.BlockSpec(memory_space=pl.ANY)] * 9,
+        in_specs=[smem, smem, smem] + [vmem] * 9,
         out_specs=vmem,
         scratch_shapes=[
-            pltpu.VMEM(q.shape, jnp.bfloat16),
-            pltpu.VMEM((2, 2, 2, 64, 16, HD), jnp.bfloat16),
-            pltpu.VMEM((2, 2, 2, 64, 16, HD), jnp.bfloat16),
             *[pltpu.VMEM((1024, 256), jnp.float32)] * (2 * UNROLL),
             *[pltpu.VMEM((8, 256), jnp.float32)] * (2 * UNROLL),
             pltpu.VMEM((4, HD, 256), jnp.float32),
             pltpu.VMEM((4, 8, 256), jnp.float32),
             pltpu.VMEM((4, 8, 256), jnp.float32),
             pltpu.SMEM((33,), jnp.int32),
-            pltpu.SemaphoreType.DMA((8, 2)),
-            pltpu.SemaphoreType.DMA(()),
         ],
         compiler_params=pltpu.CompilerParams(vmem_limit_bytes=40 * 1024 * 1024),
         cost_estimate=pl.CostEstimate(

time: 126 us -> 125 us (level)
  the two profiles are of different devices: /device:TPU:2 before, /device:TPU:1 now
where the time goes in v11:
time: 125 us; the launch traced here: 124 us
  starting transfers between devices  60.2 us (48%)
  blocking collectives  28.1 us (22%)
  waiting for transfers between devices  22.8 us (18%)
  Pallas kernels  10.8 us (9%)
    all_to_all x1, blocking collectives, exchange(): lax.all_to_all(array, ('y', 'z'), split_axis=0, concat_axis=0, tiled=True)  28.1 us
    all_to_all x1, starting transfers between devices, exchange(): lax.all_to_all(array, ('y', 'z'), split_axis=0, concat_axis=0, tiled=True)  19.4 us
    all_to_all x1, waiting for transfers between devices, exchange(): lax.all_to_all(array, ('y', 'z'), split_axis=0, concat_axis=0, tiled=True)  16.2 us
    ppermute x4, starting transfers between devices, per_device(): pieces += [piece, lax.ppermute(piece, 'core', [(0, 1), (1, 0)])]  14.5 us
    ppermute x3, starting transfers between devices, per_device(): lax.ppermute(kv, x_axes, ring(step))  10.5 us
    ppermute x3, starting transfers between devices, per_device(): part = lax.ppermute(part, 'y', [(a, a ^ d) for a in range(n_y)])  8.98 us
    pallas_call x1, Pallas kernels, attend(): pl.pallas_call(attend_kernel, out_shape=jax.ShapeDtypeStruct((64, 16, HD)...  8.9 us
    all_to_all x1, starting transfers between devices, per_device(): q = lax.all_to_all(q_in, 'z', split_axis=0, concat_axis=0, tiled=True)  6.75 us
  transfers between devices with their start and end apart: 12, of which 5 were waited for; matrix products, arithmetic and copies ran while one was open for 1% of the time, Pallas kernels for 0%

profile of v11, /device:TPU:1, one launch (start us, length us, event | category | flops | bytes accessed | tf_op | source)
XLA Modules:
  0.0 124.2 jit_solution(508196264730745657)
XLA Ops:
  0.0 1.9 %shard_map.55 = bf16[64,2,16,128]{3,2,1,0:T(8,128)(2,1)} custom-call(bf16[16,8192]{1,0:T(8,128)(2,1)} %bitcast.28, bf16[16,8192]{1,0:T(8,128)(2,1)} %bitcast.29), custom_call_target="tpu_custom_call" | custom-call | tf_op jit(solution)/shard_map/pallas_call | solution.py:150
  1.9 19.4 %all-to-all-start = ((bf16[64,2,16,128]{3,2,1,0:T(8,128)(2,1)}), bf16[64,2,16,128]{3,2,1,0:T(8,128)(2,1)S(1)}, u32[]{:S(2)}, u32[]{:S(2)}) async-start(bf16[64,2,16,128]{3,2,1,0:T(8,128)(2,1)} %shard_map.55), calls=%async_computation | async-start | bytes 1048576 | tf_op jit(solution)/shard_map/all_to_all | solution.py:173
  21.4 0.2 copy.7
  21.6 4.3 %collective-permute-start.2 = (bf16[16,16,128]{2,1,0:T(8,128)(2,1)S(1)}, bf16[16,16,128]{2,1,0:T(8,128)(2,1)S(1)}, u32[]{:S(2)}, u32[]{:S(2)}) collective-permute-start(bf16[16,16,128]{2,1,0:T(8,128)(2,1)S(1)} %get-tuple-element.10), channel_id=1, source_target_pairs={{0,384},{128,256},{256,128},{384,0},{1,385},{129,257},{257,129},{3... | collective-permute-start | bytes 196616 | tf_op jit(solution)/shard_map/ppermute | solution.py:183
  26.0 2.3 %collective-permute-start.1 = (bf16[16,16,128]{2,1,0:T(8,128)(2,1)S(1)}, bf16[16,16,128]{2,1,0:T(8,128)(2,1)S(1)}, u32[]{:S(2)}, u32[]{:S(2)}) collective-permute-start(bf16[16,16,128]{2,1,0:T(8,128)(2,1)S(1)} %get-tuple-element.11), channel_id=1, source_target_pairs={{0,256},{128,384},{256,0},{384,128},{1,257},{129,385},{257,1},{385... | collective-permute-start | bytes 196616 | tf_op jit(solution)/shard_map/ppermute | solution.py:183
  28.3 2.4 %collective-permute-start = (bf16[16,16,128]{2,1,0:T(8,128)(2,1)S(1)}, bf16[16,16,128]{2,1,0:T(8,128)(2,1)S(1)}, u32[]{:S(2)}, u32[]{:S(2)}) collective-permute-start(bf16[16,16,128]{2,1,0:T(8,128)(2,1)S(1)} %get-tuple-element.12), channel_id=1, source_target_pairs={{0,128},{128,0},{256,384},{384,256},{1,129},{129,1},{257,385},{385... | collective-permute-start | bytes 196616 | tf_op jit(solution)/shard_map/ppermute | solution.py:183
  30.6 0.0 collective-permute-done.2
  30.7 2.4 %collective-permute-done.1 = bf16[16,16,128]{2,1,0:T(8,128)(2,1)S(1)} collective-permute-done((bf16[16,16,128]{2,1,0:T(8,128)(2,1)S(1)}, bf16[16,16,128]{2,1,0:T(8,128)(2,1)S(1)}, u32[]{:S(2)}, u32[]{:S(2)}) %collective-permute-start.1) | collective-permute-done | bytes 65568 | tf_op jit(solution)/shard_map/ppermute | solution.py:183
  33.1 0.7 collective-permute-done
  33.8 0.7 pad_maximum_fusion
  34.5 16.2 %all-to-all-done.rest_0_ = bf16[64,2,16,128]{3,2,1,0:T(8,128)(2,1)S(1)} async-done(((bf16[64,2,16,128]{3,2,1,0:T(8,128)(2,1)}), bf16[64,2,16,128]{3,2,1,0:T(8,128)(2,1)S(1)}, u32[]{:S(2)}, u32[]{:S(2)}) %all-to-all-start) | async-done | bytes 524320 | tf_op jit(solution)/shard_map/all_to_all | solution.py:173
  50.7 3.1 %collective-permute-start.8 = (bf16[64,2,16,128]{3,2,1,0:T(8,128)(2,1)S(1)}, bf16[64,2,16,128]{3,2,1,0:T(8,128)(2,1)S(1)}, u32[]{:S(2)}, u32[]{:S(2)}) collective-permute-start(bf16[64,2,16,128]{3,2,1,0:T(8,128)(2,1)S(1)} %all-to-all-done.rest_0_), channel_id=1, source_target_pairs={{0,64},{64,32},{32,96},{96,0},{1,65},{65,33},{33,97},{97,1},{2,66}... | collective-permute-start | bytes 1572872 | tf_op jit(solution)/shard_map/ppermute | solution.py:190
  53.8 4.4 %collective-permute-start.6 = (bf16[64,2,16,128]{3,2,1,0:T(8,128)(2,1)S(1)}, bf16[64,2,16,128]{3,2,1,0:T(8,128)(2,1)S(1)}, u32[]{:S(2)}, u32[]{:S(2)}) collective-permute-start(bf16[64,2,16,128]{3,2,1,0:T(8,128)(2,1)S(1)} %all-to-all-done.rest_0_), channel_id=1, source_target_pairs={{0,32},{64,96},{32,0},{96,64},{1,33},{65,97},{33,1},{97,65},{2,34}... | collective-permute-start | bytes 1572872 | tf_op jit(solution)/shard_map/ppermute | solution.py:190
  58.2 3.1 %collective-permute-start.4 = (bf16[64,2,16,128]{3,2,1,0:T(8,128)(2,1)S(1)}, bf16[64,2,16,128]{3,2,1,0:T(8,128)(2,1)S(1)}, u32[]{:S(2)}, u32[]{:S(2)}) collective-permute-start(bf16[64,2,16,128]{3,2,1,0:T(8,128)(2,1)S(1)} %all-to-all-done.rest_0_), channel_id=1, source_target_pairs={{0,96},{64,0},{32,64},{96,32},{1,97},{65,1},{33,65},{97,33},{2,98}... | collective-permute-start | bytes 1572872 | tf_op jit(solution)/shard_map/ppermute | solution.py:190
  61.3 6.7 %all-to-all-start.1 = ((bf16[16,4,16,128]{3,2,1,0:T(8,128)(2,1)}), bf16[16,4,16,128]{3,2,1,0:T(8,128)(2,1)S(1)}, u32[]{:S(2)}, u32[]{:S(2)}) async-start(bf16[16,4,16,128]{3,2,1,0:T(8,128)(2,1)} %pad_maximum_fusion), calls=%async_computation.1 | async-start | bytes 524288 | tf_op jit(solution)/shard_map/all_to_all | solution.py:186
  68.0 4.6 %collective-permute-start.3 = (bf16[64,2,16,128]{3,2,1,0:T(8,128)(2,1)S(1)}, bf16[64,2,16,128]{3,2,1,0:T(8,128)(2,1)S(1)}, u32[]{:S(2)}, u32[]{:S(2)}) collective-permute-start(bf16[64,2,16,128]{3,2,1,0:T(8,128)(2,1)S(1)} %all-to-all-done.rest_0_), channel_id=1, source_target_pairs={{0,1},{1,0},{2,3},{3,2},{4,5},{5,4},{6,7},{7,6},{8,9},{9,8},{10,11... | collective-permute-start | bytes 1572872 | tf_op jit(solution)/shard_map/ppermute | solution.py:191
  72.6 0.0 collective-permute-done.8.rest_6_
  72.7 1.9 %collective-permute-start.9 = (bf16[64,2,16,128]{3,2,1,0:T(8,128)(2,1)S(1)}, bf16[64,2,16,128]{3,2,1,0:T(8,128)(2,1)S(1)}, u32[]{:S(2)}, u32[]{:S(2)}) collective-permute-start(bf16[64,2,16,128]{3,2,1,0:T(8,128)(2,1)S(1)} %collective-permute-done.8.rest_6_), channel_id=1, source_target_pairs={{0,1},{1,0},{2,3},{3,2},{4,5},{5,4},{6,7},{7,6},{8,9},{9,8},{10,11... | collective-permute-start | bytes 1572872 | tf_op jit(solution)/shard_map/ppermute | solution.py:191
  74.6 1.6 %collective-permute-done.6.rest_4_ = bf16[64,2,16,128]{3,2,1,0:T(8,128)(2,1)S(1)} collective-permute-done((bf16[64,2,16,128]{3,2,1,0:T(8,128)(2,1)S(1)}, bf16[64,2,16,128]{3,2,1,0:T(8,128)(2,1)S(1)}, u32[]{:S(2)}, u32[]{:S(2)}) %collective-permute-start.6) | collective-permute-done | bytes 524320 | tf_op jit(solution)/shard_map/ppermute | solution.py:190
  76.2 6.1 %collective-permute-start.7 = (bf16[64,2,16,128]{3,2,1,0:T(8,128)(2,1)S(1)}, bf16[64,2,16,128]{3,2,1,0:T(8,128)(2,1)}, u32[]{:S(2)}, u32[]{:S(2)}) collective-permute-start(bf16[64,2,16,128]{3,2,1,0:T(8,128)(2,1)S(1)} %collective-permute-done.6.rest_4_), channel_id=1, source_target_pairs={{0,1},{1,0},{2,3},{3,2},{4,5},{5,4},{6,7},{7,6},{8,9},{9,8},{10,11... | collective-permute-start | bytes 1572872 | tf_op jit(solution)/shard_map/ppermute | solution.py:191
  82.3 1.9 %collective-permute-start.5 = (bf16[64,2,16,128]{3,2,1,0:T(8,128)(2,1)S(1)}, bf16[64,2,16,128]{3,2,1,0:T(8,128)(2,1)}, u32[]{:S(2)}, u32[]{:S(2)}) collective-permute-start(bf16[64,2,16,128]{3,2,1,0:T(8,128)(2,1)S(1)} %collective-permute-done.4.rest_2_), channel_id=1, source_target_pairs={{0,1},{1,0},{2,3},{3,2},{4,5},{5,4},{6,7},{7,6},{8,9},{9,8},{10,11... | collective-permute-start | bytes 1572872 | tf_op jit(solution)/shard_map/ppermute | solution.py:191
  84.2 0.0 copy-start
  84.2 0.0 copy-start.1
  84.3 0.1 pad_add_fusion.place
  84.3 0.0 collective-permute-done.3.rest_1_
  84.3 0.0 all-to-all-done.1.q_ref
  84.3 0.0 collective-permute-done.9.rest_7_
  84.4 1.9 %collective-permute-done.5.rest_3_ = bf16[64,2,16,128]{3,2,1,0:T(8,128)(2,1)} collective-permute-done((bf16[64,2,16,128]{3,2,1,0:T(8,128)(2,1)S(1)}, bf16[64,2,16,128]{3,2,1,0:T(8,128)(2,1)}, u32[]{:S(2)}, u32[]{:S(2)}) %collective-permute-start.5) | collective-permute-done | bytes 524320 | tf_op jit(solution)/shard_map/ppermute | solution.py:191
  86.2 8.9 %shard_map.56 = bf16[64,16,128]{2,1,0:T(8,128)(2,1)S(1)} custom-call(s32[4]{0:T(128)S(1)} %pad_add_fusion.place, s32[8,8]{1,0:T(8,128)S(1)} %copy-done, s32[8]{0:T(128)S(1)} %copy-done.1, bf16[16,4,16,128]{3,2,1,0:T(8,128)(2,1)S(1)} %all-to-all-done.1.q_ref, bf16[64,2,16,128]{3,2,1,0:T(8,128)(2,1)S(1)} %all-to-all-done.rest_0_, ...), custom_call_target="tpu_custom_call" | custom-call | flops 4294967296 | bytes 5242880 | tf_op jit(solution)/shard_map/pallas_call | solution.py:121
  95.2 28.1 %all_to_all.15 = bf16[64,16,128]{2,1,0:T(8,128)(2,1)S(1)} all-to-all(bf16[64,16,128]{2,1,0:T(8,128)(2,1)S(1)} %shard_map.56), channel_id=1, replica_groups=mesh['y'=4,'x_lo'=2,'x_hi'=2,'z'=16,'core'=2] {'y','z'}, dimensions={0} | all-to-all | bytes 524288 | tf_op jit(solution)/shard_map/all_to_all | solution.py:173
  123.3 0.1 copy.8
  123.4 0.8 reshape.12
  (8 shorter events, 0.1 us)
Async XLA Ops:
  1.9 19.4 %copy-start.2 = (bf16[1,16,8192]{2,1,0:T(8,128)(2,1)S(1)}, bf16[1,16,8192]{2,1,0:T(8,128)(2,1)}, u32[]{:S(2)}) copy-start(bf16[1,16,8192]{2,1,0:T(8,128)(2,1)} %param.5) | copy-start | bytes 786436
  1.9 48.8 %all-to-all-start = ((bf16[64,2,16,128]{3,2,1,0:T(8,128)(2,1)}), bf16[64,2,16,128]{3,2,1,0:T(8,128)(2,1)S(1)}, u32[]{:S(2)}, u32[]{:S(2)}) async-start(bf16[64,2,16,128]{3,2,1,0:T(8,128)(2,1)} %shard_map.55), calls=%async_computation | async-start | bytes 1048576 | tf_op jit(solution)/shard_map/all_to_all | solution.py:173
  21.6 9.0 %collective-permute-start.2 = (bf16[16,16,128]{2,1,0:T(8,128)(2,1)S(1)}, bf16[16,16,128]{2,1,0:T(8,128)(2,1)S(1)}, u32[]{:S(2)}, u32[]{:S(2)}) collective-permute-start(bf16[16,16,128]{2,1,0:T(8,128)(2,1)S(1)} %get-tuple-element.10), channel_id=1, source_target_pairs={{0,384},{128,256},{256,128},{384,0},{1,385},{129,257},{257,129},{3... | collective-permute-start | bytes 196616 | tf_op jit(solution)/shard_map/ppermute | solution.py:183
  26.0 7.1 %collective-permute-start.1 = (bf16[16,16,128]{2,1,0:T(8,128)(2,1)S(1)}, bf16[16,16,128]{2,1,0:T(8,128)(2,1)S(1)}, u32[]{:S(2)}, u32[]{:S(2)}) collective-permute-start(bf16[16,16,128]{2,1,0:T(8,128)(2,1)S(1)} %get-tuple-element.11), channel_id=1, source_target_pairs={{0,256},{128,384},{256,0},{384,128},{1,257},{129,385},{257,1},{385... | collective-permute-start | bytes 196616 | tf_op jit(solution)/shard_map/ppermute | solution.py:183
  28.3 5.5 %collective-permute-start = (bf16[16,16,128]{2,1,0:T(8,128)(2,1)S(1)}, bf16[16,16,128]{2,1,0:T(8,128)(2,1)S(1)}, u32[]{:S(2)}, u32[]{:S(2)}) collective-permute-start(bf16[16,16,128]{2,1,0:T(8,128)(2,1)S(1)} %get-tuple-element.12), channel_id=1, source_target_pairs={{0,128},{128,0},{256,384},{384,256},{1,129},{129,1},{257,385},{385... | collective-permute-start | bytes 196616 | tf_op jit(solution)/shard_map/ppermute | solution.py:183
  50.7 21.9 %collective-permute-start.8 = (bf16[64,2,16,128]{3,2,1,0:T(8,128)(2,1)S(1)}, bf16[64,2,16,128]{3,2,1,0:T(8,128)(2,1)S(1)}, u32[]{:S(2)}, u32[]{:S(2)}) collective-permute-start(bf16[64,2,16,128]{3,2,1,0:T(8,128)(2,1)S(1)} %all-to-all-done.rest_0_), channel_id=1, source_target_pairs={{0,64},{64,32},{32,96},{96,0},{1,65},{65,33},{33,97},{97,1},{2,66}... | collective-permute-start | bytes 1572872 | tf_op jit(solution)/shard_map/ppermute | solution.py:190
  53.8 22.4 %collective-permute-start.6 = (bf16[64,2,16,128]{3,2,1,0:T(8,128)(2,1)S(1)}, bf16[64,2,16,128]{3,2,1,0:T(8,128)(2,1)S(1)}, u32[]{:S(2)}, u32[]{:S(2)}) collective-permute-start(bf16[64,2,16,128]{3,2,1,0:T(8,128)(2,1)S(1)} %all-to-all-done.rest_0_), channel_id=1, source_target_pairs={{0,32},{64,96},{32,0},{96,64},{1,33},{65,97},{33,1},{97,65},{2,34}... | collective-permute-start | bytes 1572872 | tf_op jit(solution)/shard_map/ppermute | solution.py:190
  58.2 24.1 %collective-permute-start.4 = (bf16[64,2,16,128]{3,2,1,0:T(8,128)(2,1)S(1)}, bf16[64,2,16,128]{3,2,1,0:T(8,128)(2,1)S(1)}, u32[]{:S(2)}, u32[]{:S(2)}) collective-permute-start(bf16[64,2,16,128]{3,2,1,0:T(8,128)(2,1)S(1)} %all-to-all-done.rest_0_), channel_id=1, source_target_pairs={{0,96},{64,0},{32,64},{96,32},{1,97},{65,1},{33,65},{97,33},{2,98}... | collective-permute-start | bytes 1572872 | tf_op jit(solution)/shard_map/ppermute | solution.py:190
  61.3 23.1 %all-to-all-start.1 = ((bf16[16,4,16,128]{3,2,1,0:T(8,128)(2,1)}), bf16[16,4,16,128]{3,2,1,0:T(8,128)(2,1)S(1)}, u32[]{:S(2)}, u32[]{:S(2)}) async-start(bf16[16,4,16,128]{3,2,1,0:T(8,128)(2,1)} %pad_maximum_fusion), calls=%async_computation.1 | async-start | bytes 524288 | tf_op jit(solution)/shard_map/all_to_all | solution.py:186
  68.0 16.3 %collective-permute-start.3 = (bf16[64,2,16,128]{3,2,1,0:T(8,128)(2,1)S(1)}, bf16[64,2,16,128]{3,2,1,0:T(8,128)(2,1)S(1)}, u32[]{:S(2)}, u32[]{:S(2)}) collective-permute-start(bf16[64,2,16,128]{3,2,1,0:T(8,128)(2,1)S(1)} %all-to-all-done.rest_0_), channel_id=1, source_target_pairs={{0,1},{1,0},{2,3},{3,2},{4,5},{5,4},{6,7},{7,6},{8,9},{9,8},{10,11... | collective-permute-start | bytes 1572872 | tf_op jit(solution)/shard_map/ppermute | solution.py:191
  72.7 11.7 %collective-permute-start.9 = (bf16[64,2,16,128]{3,2,1,0:T(8,128)(2,1)S(1)}, bf16[64,2,16,128]{3,2,1,0:T(8,128)(2,1)S(1)}, u32[]{:S(2)}, u32[]{:S(2)}) collective-permute-start(bf16[64,2,16,128]{3,2,1,0:T(8,128)(2,1)S(1)} %collective-permute-done.8.rest_6_), channel_id=1, source_target_pairs={{0,1},{1,0},{2,3},{3,2},{4,5},{5,4},{6,7},{7,6},{8,9},{9,8},{10,11... | collective-permute-start | bytes 1572872 | tf_op jit(solution)/shard_map/ppermute | solution.py:191
  76.2 8.2 %collective-permute-start.7 = (bf16[64,2,16,128]{3,2,1,0:T(8,128)(2,1)S(1)}, bf16[64,2,16,128]{3,2,1,0:T(8,128)(2,1)}, u32[]{:S(2)}, u32[]{:S(2)}) collective-permute-start(bf16[64,2,16,128]{3,2,1,0:T(8,128)(2,1)S(1)} %collective-permute-done.6.rest_4_), channel_id=1, source_target_pairs={{0,1},{1,0},{2,3},{3,2},{4,5},{5,4},{6,7},{7,6},{8,9},{9,8},{10,11... | collective-permute-start | bytes 1572872 | tf_op jit(solution)/shard_map/ppermute | solution.py:191
  82.3 3.9 %collective-permute-start.5 = (bf16[64,2,16,128]{3,2,1,0:T(8,128)(2,1)S(1)}, bf16[64,2,16,128]{3,2,1,0:T(8,128)(2,1)}, u32[]{:S(2)}, u32[]{:S(2)}) collective-permute-start(bf16[64,2,16,128]{3,2,1,0:T(8,128)(2,1)S(1)} %collective-permute-done.4.rest_2_), channel_id=1, source_target_pairs={{0,1},{1,0},{2,3},{3,2},{4,5},{5,4},{6,7},{7,6},{8,9},{9,8},{10,11... | collective-permute-start | bytes 1572872 | tf_op jit(solution)/shard_map/ppermute | solution.py:191
  84.2 2.0 %copy-start = (s32[8,8]{1,0:T(8,128)S(1)}, s32[8,8]{1,0:T(8,128)}, u32[]{:S(2)}) copy-start(s32[8,8]{1,0:T(8,128)} %mask.1) | copy-start | bytes 772
  84.2 2.0 %copy-start.1 = (s32[8]{0:T(128)S(1)}, s32[8]{0:T(128)}, u32[]{:S(2)}) copy-start(s32[8]{0:T(128)} %counts.1) | copy-start | bytes 100

commit v12 on v11

--- a/solution.py
+++ b/solution.py
@@ -8,14 +8,13 @@
 HD = 128
 LOW = -1e30
 LOG2E = 1.4426950408889634
-UNROLL = 1
 
 
 def attend_kernel(place, mask, counts, q_ref, *rest):
     pieces = rest[:8]
     out_ref = rest[8]
-    scores, row_tops = rest[9 : 9 + 2 * UNROLL], rest[9 + 2 * UNROLL : 9 + 4 * UNROLL]
-    acc_ref, top_ref, total_ref, todo = rest[9 + 4 * UNROLL :]
+    scores, row_tops = rest[9:12], rest[12:15]
+    acc_ref, top_ref, total_ref, todo = rest[15:]
     x_lo, x_hi, core, y = place[0], place[1], place[2], place[3]
 
     def slab(side, part, jy):
@@ -86,7 +85,9 @@
         acc_ref[iy] = acc_ref[iy] * keep + acc * add
         top_ref[iy] = jnp.broadcast_to(new, (8, 256))
 
-    def run(side, begin, end):
+    def run(side, begin, end, ahead):
+        last = end - 1
+
         def step(n, slot):
             score(n + 1, 1 - slot, side, end)
             merge(n, mix(n, slot, side))
@@ -95,20 +96,31 @@
             n = begin + 2 * m
             step(n, 0)
 
-            @pl.when(n + 1 < end)
+            @pl.when(n + 1 < last)
             def _():
                 step(n + 1, 1)
 
             return 0
 
-        score(begin, 0, side, end)
-        lax.fori_loop(0, (end - begin + 1) // 2, pair, 0)
-
-    run(0, 0, first)
+        lax.fori_loop(0, (last - begin + 1) // 2, pair, 0)
+        for slot in range(2):
+
+            @pl.when((last - begin) % 2 == slot)
+            def _():
+                ahead()
+                merge(last, mix(last, slot, side))
+
+    score(0, 0, 0, first)
+    run(0, 0, first, lambda: score(first, 2, 1, first + 1))
 
     @pl.when(count > first)
     def _():
-        run(1, first, count)
+        score(first + 1, 0, 1, count)
+        merge(first, mix(first, 2, 1))
+
+        @pl.when(count > first + 1)
+        def _():
+            run(1, first + 1, count, lambda: None)
 
     for iy in range(4):
         result = (acc_ref[iy] / total_ref[iy][:1]).T.astype(jnp.bfloat16)
@@ -124,8 +136,8 @@
         in_specs=[smem, smem, smem] + [vmem] * 9,
         out_specs=vmem,
         scratch_shapes=[
-            *[pltpu.VMEM((1024, 256), jnp.float32)] * (2 * UNROLL),
-            *[pltpu.VMEM((8, 256), jnp.float32)] * (2 * UNROLL),
+            *[pltpu.VMEM((1024, 256), jnp.float32)] * 3,
+            *[pltpu.VMEM((8, 256), jnp.float32)] * 3,
             pltpu.VMEM((4, HD, 256), jnp.float32),
             pltpu.VMEM((4, 8, 256), jnp.float32),
             pltpu.VMEM((4, 8, 256), jnp.float32),

time: 125 us -> 126 us (level)
  no operation moved by 1% of the time
where the time goes in v12:
time: 126 us; the launch traced here: 125 us
  starting transfers between devices  60.2 us (48%)
  blocking collectives  28.5 us (23%)
  waiting for transfers between devices  22.8 us (18%)
  Pallas kernels  10.9 us (9%)
    all_to_all x1, blocking collectives, exchange(): lax.all_to_all(array, ('y', 'z'), split_axis=0, concat_axis=0, tiled=True)  28.5 us
    all_to_all x1, starting transfers between devices, exchange(): lax.all_to_all(array, ('y', 'z'), split_axis=0, concat_axis=0, tiled=True)  19.4 us
    all_to_all x1, waiting for transfers between devices, exchange(): lax.all_to_all(array, ('y', 'z'), split_axis=0, concat_axis=0, tiled=True)  16.2 us
    ppermute x4, starting transfers between devices, per_device(): pieces += [piece, lax.ppermute(piece, 'core', [(0, 1), (1, 0)])]  14.5 us
    ppermute x3, starting transfers between devices, per_device(): lax.ppermute(kv, x_axes, ring(step))  10.5 us
    pallas_call x1, Pallas kernels, attend(): pl.pallas_call(attend_kernel, out_shape=jax.ShapeDtypeStruct((64, 16, HD)...  9.04 us
    ppermute x3, starting transfers between devices, per_device(): part = lax.ppermute(part, 'y', [(a, a ^ d) for a in range(n_y)])  8.98 us
    all_to_all x1, starting transfers between devices, per_device(): q = lax.all_to_all(q_in, 'z', split_axis=0, concat_axis=0, tiled=True)  6.75 us
  transfers between devices with their start and end apart: 12, of which 5 were waited for; matrix products, arithmetic and copies ran while one was open for 1% of the time, Pallas kernels for 0%

profile of v12, /device:TPU:1, one launch (start us, length us, event | category | flops | bytes accessed | tf_op | source)
XLA Modules:
  0.0 124.7 jit_solution(114253800456733026)
XLA Ops:
  0.0 1.9 %shard_map.55 = bf16[64,2,16,128]{3,2,1,0:T(8,128)(2,1)} custom-call(bf16[16,8192]{1,0:T(8,128)(2,1)} %bitcast.28, bf16[16,8192]{1,0:T(8,128)(2,1)} %bitcast.29), custom_call_target="tpu_custom_call" | custom-call | tf_op jit(solution)/shard_map/pallas_call | solution.py:162
  1.9 19.4 %all-to-all-start = ((bf16[64,2,16,128]{3,2,1,0:T(8,128)(2,1)}), bf16[64,2,16,128]{3,2,1,0:T(8,128)(2,1)S(1)}, u32[]{:S(2)}, u32[]{:S(2)}) async-start(bf16[64,2,16,128]{3,2,1,0:T(8,128)(2,1)} %shard_map.55), calls=%async_computation | async-start | bytes 1048576 | tf_op jit(solution)/shard_map/all_to_all | solution.py:185
  21.4 0.2 copy.7
  21.6 4.3 %collective-permute-start.2 = (bf16[16,16,128]{2,1,0:T(8,128)(2,1)S(1)}, bf16[16,16,128]{2,1,0:T(8,128)(2,1)S(1)}, u32[]{:S(2)}, u32[]{:S(2)}) collective-permute-start(bf16[16,16,128]{2,1,0:T(8,128)(2,1)S(1)} %get-tuple-element.10), channel_id=1, source_target_pairs={{0,384},{128,256},{256,128},{384,0},{1,385},{129,257},{257,129},{3... | collective-permute-start | bytes 196616 | tf_op jit(solution)/shard_map/ppermute | solution.py:195
  26.0 2.3 %collective-permute-start.1 = (bf16[16,16,128]{2,1,0:T(8,128)(2,1)S(1)}, bf16[16,16,128]{2,1,0:T(8,128)(2,1)S(1)}, u32[]{:S(2)}, u32[]{:S(2)}) collective-permute-start(bf16[16,16,128]{2,1,0:T(8,128)(2,1)S(1)} %get-tuple-element.11), channel_id=1, source_target_pairs={{0,256},{128,384},{256,0},{384,128},{1,257},{129,385},{257,1},{385... | collective-permute-start | bytes 196616 | tf_op jit(solution)/shard_map/ppermute | solution.py:195
  28.3 2.4 %collective-permute-start = (bf16[16,16,128]{2,1,0:T(8,128)(2,1)S(1)}, bf16[16,16,128]{2,1,0:T(8,128)(2,1)S(1)}, u32[]{:S(2)}, u32[]{:S(2)}) collective-permute-start(bf16[16,16,128]{2,1,0:T(8,128)(2,1)S(1)} %get-tuple-element.12), channel_id=1, source_target_pairs={{0,128},{128,0},{256,384},{384,256},{1,129},{129,1},{257,385},{385... | collective-permute-start | bytes 196616 | tf_op jit(solution)/shard_map/ppermute | solution.py:195
  30.6 0.0 collective-permute-done.2
  30.7 2.4 %collective-permute-done.1 = bf16[16,16,128]{2,1,0:T(8,128)(2,1)S(1)} collective-permute-done((bf16[16,16,128]{2,1,0:T(8,128)(2,1)S(1)}, bf16[16,16,128]{2,1,0:T(8,128)(2,1)S(1)}, u32[]{:S(2)}, u32[]{:S(2)}) %collective-permute-start.1) | collective-permute-done | bytes 65568 | tf_op jit(solution)/shard_map/ppermute | solution.py:195
  33.1 0.7 collective-permute-done
  33.8 0.7 pad_maximum_fusion
  34.5 16.2 %all-to-all-done.rest_0_ = bf16[64,2,16,128]{3,2,1,0:T(8,128)(2,1)S(1)} async-done(((bf16[64,2,16,128]{3,2,1,0:T(8,128)(2,1)}), bf16[64,2,16,128]{3,2,1,0:T(8,128)(2,1)S(1)}, u32[]{:S(2)}, u32[]{:S(2)}) %all-to-all-start) | async-done | bytes 524320 | tf_op jit(solution)/shard_map/all_to_all | solution.py:185
  50.7 3.1 %collective-permute-start.8 = (bf16[64,2,16,128]{3,2,1,0:T(8,128)(2,1)S(1)}, bf16[64,2,16,128]{3,2,1,0:T(8,128)(2,1)S(1)}, u32[]{:S(2)}, u32[]{:S(2)}) collective-permute-start(bf16[64,2,16,128]{3,2,1,0:T(8,128)(2,1)S(1)} %all-to-all-done.rest_0_), channel_id=1, source_target_pairs={{0,64},{64,32},{32,96},{96,0},{1,65},{65,33},{33,97},{97,1},{2,66}... | collective-permute-start | bytes 1572872 | tf_op jit(solution)/shard_map/ppermute | solution.py:202
  53.8 4.4 %collective-permute-start.6 = (bf16[64,2,16,128]{3,2,1,0:T(8,128)(2,1)S(1)}, bf16[64,2,16,128]{3,2,1,0:T(8,128)(2,1)S(1)}, u32[]{:S(2)}, u32[]{:S(2)}) collective-permute-start(bf16[64,2,16,128]{3,2,1,0:T(8,128)(2,1)S(1)} %all-to-all-done.rest_0_), channel_id=1, source_target_pairs={{0,32},{64,96},{32,0},{96,64},{1,33},{65,97},{33,1},{97,65},{2,34}... | collective-permute-start | bytes 1572872 | tf_op jit(solution)/shard_map/ppermute | solution.py:202
  58.2 3.1 %collective-permute-start.4 = (bf16[64,2,16,128]{3,2,1,0:T(8,128)(2,1)S(1)}, bf16[64,2,16,128]{3,2,1,0:T(8,128)(2,1)S(1)}, u32[]{:S(2)}, u32[]{:S(2)}) collective-permute-start(bf16[64,2,16,128]{3,2,1,0:T(8,128)(2,1)S(1)} %all-to-all-done.rest_0_), channel_id=1, source_target_pairs={{0,96},{64,0},{32,64},{96,32},{1,97},{65,1},{33,65},{97,33},{2,98}... | collective-permute-start | bytes 1572872 | tf_op jit(solution)/shard_map/ppermute | solution.py:202
  61.3 6.7 %all-to-all-start.1 = ((bf16[16,4,16,128]{3,2,1,0:T(8,128)(2,1)}), bf16[16,4,16,128]{3,2,1,0:T(8,128)(2,1)S(1)}, u32[]{:S(2)}, u32[]{:S(2)}) async-start(bf16[16,4,16,128]{3,2,1,0:T(8,128)(2,1)} %pad_maximum_fusion), calls=%async_computation.1 | async-start | bytes 524288 | tf_op jit(solution)/shard_map/all_to_all | solution.py:198
  68.0 4.6 %collective-permute-start.3 = (bf16[64,2,16,128]{3,2,1,0:T(8,128)(2,1)S(1)}, bf16[64,2,16,128]{3,2,1,0:T(8,128)(2,1)S(1)}, u32[]{:S(2)}, u32[]{:S(2)}) collective-permute-start(bf16[64,2,16,128]{3,2,1,0:T(8,128)(2,1)S(1)} %all-to-all-done.rest_0_), channel_id=1, source_target_pairs={{0,1},{1,0},{2,3},{3,2},{4,5},{5,4},{6,7},{7,6},{8,9},{9,8},{10,11... | collective-permute-start | bytes 1572872 | tf_op jit(solution)/shard_map/ppermute | solution.py:203
  72.6 0.0 collective-permute-done.8.rest_6_
  72.7 1.9 %collective-permute-start.9 = (bf16[64,2,16,128]{3,2,1,0:T(8,128)(2,1)S(1)}, bf16[64,2,16,128]{3,2,1,0:T(8,128)(2,1)S(1)}, u32[]{:S(2)}, u32[]{:S(2)}) collective-permute-start(bf16[64,2,16,128]{3,2,1,0:T(8,128)(2,1)S(1)} %collective-permute-done.8.rest_6_), channel_id=1, source_target_pairs={{0,1},{1,0},{2,3},{3,2},{4,5},{5,4},{6,7},{7,6},{8,9},{9,8},{10,11... | collective-permute-start | bytes 1572872 | tf_op jit(solution)/shard_map/ppermute | solution.py:203
  74.6 1.6 %collective-permute-done.6.rest_4_ = bf16[64,2,16,128]{3,2,1,0:T(8,128)(2,1)S(1)} collective-permute-done((bf16[64,2,16,128]{3,2,1,0:T(8,128)(2,1)S(1)}, bf16[64,2,16,128]{3,2,1,0:T(8,128)(2,1)S(1)}, u32[]{:S(2)}, u32[]{:S(2)}) %collective-permute-start.6) | collective-permute-done | bytes 524320 | tf_op jit(solution)/shard_map/ppermute | solution.py:202
  76.2 6.1 %collective-permute-start.7 = (bf16[64,2,16,128]{3,2,1,0:T(8,128)(2,1)S(1)}, bf16[64,2,16,128]{3,2,1,0:T(8,128)(2,1)}, u32[]{:S(2)}, u32[]{:S(2)}) collective-permute-start(bf16[64,2,16,128]{3,2,1,0:T(8,128)(2,1)S(1)} %collective-permute-done.6.rest_4_), channel_id=1, source_target_pairs={{0,1},{1,0},{2,3},{3,2},{4,5},{5,4},{6,7},{7,6},{8,9},{9,8},{10,11... | collective-permute-start | bytes 1572872 | tf_op jit(solution)/shard_map/ppermute | solution.py:203
  82.3 0.0 collective-permute-done.4.rest_2_
  82.3 1.9 %collective-permute-start.5 = (bf16[64,2,16,128]{3,2,1,0:T(8,128)(2,1)S(1)}, bf16[64,2,16,128]{3,2,1,0:T(8,128)(2,1)}, u32[]{:S(2)}, u32[]{:S(2)}) collective-permute-start(bf16[64,2,16,128]{3,2,1,0:T(8,128)(2,1)S(1)} %collective-permute-done.4.rest_2_), channel_id=1, source_target_pairs={{0,1},{1,0},{2,3},{3,2},{4,5},{5,4},{6,7},{7,6},{8,9},{9,8},{10,11... | collective-permute-start | bytes 1572872 | tf_op jit(solution)/shard_map/ppermute | solution.py:203
  84.2 0.0 copy-start
  84.2 0.0 copy-start.1
  84.3 0.1 pad_add_fusion.place
  84.3 0.0 collective-permute-done.3.rest_1_
  84.4 0.0 collective-permute-done.7.rest_5_
  84.4 1.9 %collective-permute-done.5.rest_3_ = bf16[64,2,16,128]{3,2,1,0:T(8,128)(2,1)} collective-permute-done((bf16[64,2,16,128]{3,2,1,0:T(8,128)(2,1)S(1)}, bf16[64,2,16,128]{3,2,1,0:T(8,128)(2,1)}, u32[]{:S(2)}, u32[]{:S(2)}) %collective-permute-start.5) | collective-permute-done | bytes 524320 | tf_op jit(solution)/shard_map/ppermute | solution.py:203
  86.2 9.0 %shard_map.56 = bf16[64,16,128]{2,1,0:T(8,128)(2,1)S(1)} custom-call(s32[4]{0:T(128)S(1)} %pad_add_fusion.place, s32[8,8]{1,0:T(8,128)S(1)} %copy-done, s32[8]{0:T(128)S(1)} %copy-done.1, bf16[16,4,16,128]{3,2,1,0:T(8,128)(2,1)S(1)} %all-to-all-done.1.q_ref, bf16[64,2,16,128]{3,2,1,0:T(8,128)(2,1)S(1)} %all-to-all-done.rest_0_, ...), custom_call_target="tpu_custom_call" | custom-call | flops 4294967296 | bytes 5242880 | tf_op jit(solution)/shard_map/pallas_call | solution.py:133
  95.3 28.5 %all_to_all.15 = bf16[64,16,128]{2,1,0:T(8,128)(2,1)S(1)} all-to-all(bf16[64,16,128]{2,1,0:T(8,128)(2,1)S(1)} %shard_map.56), channel_id=1, replica_groups=mesh['y'=4,'x_lo'=2,'x_hi'=2,'z'=16,'core'=2] {'y','z'}, dimensions={0} | all-to-all | bytes 524288 | tf_op jit(solution)/shard_map/all_to_all | solution.py:185
  123.8 0.1 copy.8
  123.9 0.8 reshape.12
  (8 shorter events, 0.1 us)
Async XLA Ops:
  1.9 19.4 %copy-start.2 = (bf16[1,16,8192]{2,1,0:T(8,128)(2,1)S(1)}, bf16[1,16,8192]{2,1,0:T(8,128)(2,1)}, u32[]{:S(2)}) copy-start(bf16[1,16,8192]{2,1,0:T(8,128)(2,1)} %param.5) | copy-start | bytes 786436
  1.9 48.8 %all-to-all-start = ((bf16[64,2,16,128]{3,2,1,0:T(8,128)(2,1)}), bf16[64,2,16,128]{3,2,1,0:T(8,128)(2,1)S(1)}, u32[]{:S(2)}, u32[]{:S(2)}) async-start(bf16[64,2,16,128]{3,2,1,0:T(8,128)(2,1)} %shard_map.55), calls=%async_computation | async-start | bytes 1048576 | tf_op jit(solution)/shard_map/all_to_all | solution.py:185
  21.6 9.0 %collective-permute-start.2 = (bf16[16,16,128]{2,1,0:T(8,128)(2,1)S(1)}, bf16[16,16,128]{2,1,0:T(8,128)(2,1)S(1)}, u32[]{:S(2)}, u32[]{:S(2)}) collective-permute-start(bf16[16,16,128]{2,1,0:T(8,128)(2,1)S(1)} %get-tuple-element.10), channel_id=1, source_target_pairs={{0,384},{128,256},{256,128},{384,0},{1,385},{129,257},{257,129},{3... | collective-permute-start | bytes 196616 | tf_op jit(solution)/shard_map/ppermute | solution.py:195
  26.0 7.1 %collective-permute-start.1 = (bf16[16,16,128]{2,1,0:T(8,128)(2,1)S(1)}, bf16[16,16,128]{2,1,0:T(8,128)(2,1)S(1)}, u32[]{:S(2)}, u32[]{:S(2)}) collective-permute-start(bf16[16,16,128]{2,1,0:T(8,128)(2,1)S(1)} %get-tuple-element.11), channel_id=1, source_target_pairs={{0,256},{128,384},{256,0},{384,128},{1,257},{129,385},{257,1},{385... | collective-permute-start | bytes 196616 | tf_op jit(solution)/shard_map/ppermute | solution.py:195
  28.3 5.5 %collective-permute-start = (bf16[16,16,128]{2,1,0:T(8,128)(2,1)S(1)}, bf16[16,16,128]{2,1,0:T(8,128)(2,1)S(1)}, u32[]{:S(2)}, u32[]{:S(2)}) collective-permute-start(bf16[16,16,128]{2,1,0:T(8,128)(2,1)S(1)} %get-tuple-element.12), channel_id=1, source_target_pairs={{0,128},{128,0},{256,384},{384,256},{1,129},{129,1},{257,385},{385... | collective-permute-start | bytes 196616 | tf_op jit(solution)/shard_map/ppermute | solution.py:195
  50.7 21.9 %collective-permute-start.8 = (bf16[64,2,16,128]{3,2,1,0:T(8,128)(2,1)S(1)}, bf16[64,2,16,128]{3,2,1,0:T(8,128)(2,1)S(1)}, u32[]{:S(2)}, u32[]{:S(2)}) collective-permute-start(bf16[64,2,16,128]{3,2,1,0:T(8,128)(2,1)S(1)} %all-to-all-done.rest_0_), channel_id=1, source_target_pairs={{0,64},{64,32},{32,96},{96,0},{1,65},{65,33},{33,97},{97,1},{2,66}... | collective-permute-start | bytes 1572872 | tf_op jit(solution)/shard_map/ppermute | solution.py:202
  53.8 22.4 %collective-permute-start.6 = (bf16[64,2,16,128]{3,2,1,0:T(8,128)(2,1)S(1)}, bf16[64,2,16,128]{3,2,1,0:T(8,128)(2,1)S(1)}, u32[]{:S(2)}, u32[]{:S(2)}) collective-permute-start(bf16[64,2,16,128]{3,2,1,0:T(8,128)(2,1)S(1)} %all-to-all-done.rest_0_), channel_id=1, source_target_pairs={{0,32},{64,96},{32,0},{96,64},{1,33},{65,97},{33,1},{97,65},{2,34}... | collective-permute-start | bytes 1572872 | tf_op jit(solution)/shard_map/ppermute | solution.py:202
  58.2 24.1 %collective-permute-start.4 = (bf16[64,2,16,128]{3,2,1,0:T(8,128)(2,1)S(1)}, bf16[64,2,16,128]{3,2,1,0:T(8,128)(2,1)S(1)}, u32[]{:S(2)}, u32[]{:S(2)}) collective-permute-start(bf16[64,2,16,128]{3,2,1,0:T(8,128)(2,1)S(1)} %all-to-all-done.rest_0_), channel_id=1, source_target_pairs={{0,96},{64,0},{32,64},{96,32},{1,97},{65,1},{33,65},{97,33},{2,98}... | collective-permute-start | bytes 1572872 | tf_op jit(solution)/shard_map/ppermute | solution.py:202
  61.3 23.1 %all-to-all-start.1 = ((bf16[16,4,16,128]{3,2,1,0:T(8,128)(2,1)}), bf16[16,4,16,128]{3,2,1,0:T(8,128)(2,1)S(1)}, u32[]{:S(2)}, u32[]{:S(2)}) async-start(bf16[16,4,16,128]{3,2,1,0:T(8,128)(2,1)} %pad_maximum_fusion), calls=%async_computation.1 | async-start | bytes 524288 | tf_op jit(solution)/shard_map/all_to_all | solution.py:198
  68.0 16.3 %collective-permute-start.3 = (bf16[64,2,16,128]{3,2,1,0:T(8,128)(2,1)S(1)}, bf16[64,2,16,128]{3,2,1,0:T(8,128)(2,1)S(1)}, u32[]{:S(2)}, u32[]{:S(2)}) collective-permute-start(bf16[64,2,16,128]{3,2,1,0:T(8,128)(2,1)S(1)} %all-to-all-done.rest_0_), channel_id=1, source_target_pairs={{0,1},{1,0},{2,3},{3,2},{4,5},{5,4},{6,7},{7,6},{8,9},{9,8},{10,11... | collective-permute-start | bytes 1572872 | tf_op jit(solution)/shard_map/ppermute | solution.py:203
  72.7 11.7 %collective-permute-start.9 = (bf16[64,2,16,128]{3,2,1,0:T(8,128)(2,1)S(1)}, bf16[64,2,16,128]{3,2,1,0:T(8,128)(2,1)S(1)}, u32[]{:S(2)}, u32[]{:S(2)}) collective-permute-start(bf16[64,2,16,128]{3,2,1,0:T(8,128)(2,1)S(1)} %collective-permute-done.8.rest_6_), channel_id=1, source_target_pairs={{0,1},{1,0},{2,3},{3,2},{4,5},{5,4},{6,7},{7,6},{8,9},{9,8},{10,11... | collective-permute-start | bytes 1572872 | tf_op jit(solution)/shard_map/ppermute | solution.py:203
  76.2 8.2 %collective-permute-start.7 = (bf16[64,2,16,128]{3,2,1,0:T(8,128)(2,1)S(1)}, bf16[64,2,16,128]{3,2,1,0:T(8,128)(2,1)}, u32[]{:S(2)}, u32[]{:S(2)}) collective-permute-start(bf16[64,2,16,128]{3,2,1,0:T(8,128)(2,1)S(1)} %collective-permute-done.6.rest_4_), channel_id=1, source_target_pairs={{0,1},{1,0},{2,3},{3,2},{4,5},{5,4},{6,7},{7,6},{8,9},{9,8},{10,11... | collective-permute-start | bytes 1572872 | tf_op jit(solution)/shard_map/ppermute | solution.py:203
  82.3 3.9 %collective-permute-start.5 = (bf16[64,2,16,128]{3,2,1,0:T(8,128)(2,1)S(1)}, bf16[64,2,16,128]{3,2,1,0:T(8,128)(2,1)}, u32[]{:S(2)}, u32[]{:S(2)}) collective-permute-start(bf16[64,2,16,128]{3,2,1,0:T(8,128)(2,1)S(1)} %collective-permute-done.4.rest_2_), channel_id=1, source_target_pairs={{0,1},{1,0},{2,3},{3,2},{4,5},{5,4},{6,7},{7,6},{8,9},{9,8},{10,11... | collective-permute-start | bytes 1572872 | tf_op jit(solution)/shard_map/ppermute | solution.py:203
  84.2 2.0 %copy-start = (s32[8,8]{1,0:T(8,128)S(1)}, s32[8,8]{1,0:T(8,128)}, u32[]{:S(2)}) copy-start(s32[8,8]{1,0:T(8,128)} %mask.1) | copy-start | bytes 772
  84.2 2.0 %copy-start.1 = (s32[8]{0:T(128)S(1)}, s32[8]{0:T(128)}, u32[]{:S(2)}) copy-start(s32[8]{0:T(128)} %counts.1) | copy-start | bytes 100
